TPU v7x, 128 devices: a whole 4x4x4 slice. The times are simulated.
128 devices in a mesh: gx: 8 (over x, core), gy: 16 (over y, z).
Axes of the slice: x: 4, y: 4, z: 4, core: 2. Of those that a mesh axis runs over, the one named last changes fastest.
Arguments:
- flow_state: float32 [6, 256, 32768], P(None, 'gx', 'gy'), may hold values from -6 to 6
- drag_coefficient: float32 [256, 32768], P('gx', 'gy'), may hold values from 0.05 to 0.5
- wet_mask: int32 [256, 32768], P('gx', 'gy'), may hold values 0 or 1
- target_elem: int32 [256, 32768], P('gx', 'gy'), may hold values from 0 to 32767, as said below
- target_node: int32 [256, 32768], P('gx', 'gy'), may hold values from 0 to 24
- displacement: float32 [3, 5, 5, 5, 2, 16, 2048], P(None, None, None, None, None, 'gx', 'gy'), as said below
- previous: float32 [3, 5, 5, 5, 2, 16, 2048], P(None, None, None, None, None, 'gx', 'gy'), as said below
- density: float32 [2, 16, 2048], P(None, 'gx', 'gy'), may hold values from 1 to 3
- lame_first: float32 [2, 16, 2048], P(None, 'gx', 'gy'), may hold values from 1 to 4
- shear_modulus: float32 [2, 16, 2048], P(None, 'gx', 'gy'), may hold values from 0.5 to 2
Outputs:
- flow_final: float32 [6, 256, 32768], P(None, 'gx', 'gy')
- displacement_next: float32 [3, 5, 5, 5, 2, 16, 2048], P(None, None, None, None, None, 'gx', 'gy')
- displacement_last: float32 [3, 5, 5, 5, 2, 16, 2048], P(None, None, None, None, None, 'gx', 'gy')
Inputs may be any that keep to these rules, and one draw needn't show every extreme that they name: `target_elem`: each cell's element lies at most one element row and one element column outside the 2 x 128 block of elements that shares the cell's device; the value is element row times 2048 plus element column. `displacement`: a grid point shared by adjacent elements holds the same value in every copy. `previous`: a grid point shared by adjacent elements holds the same value in every copy.
All inputs are finite; a program needn't handle non-finite values. No bound on the sum of `wet_mask` on one device may be relied on, other than what follows from the above.
Results may differ from a plain program's by a relative error of at most 0.00021.
Values sent between devices are 32-bit elements; how exact they have to be, the bound alone decides.
A program may use at most 192 MiB of HBM per device.

v0:
```python
import jax
import jax.numpy as jnp
import numpy as np
from jax import lax
from jax.sharding import PartitionSpec as P

FLOW_STEPS = 4
SOLID_STEPS = 2


gll_points = np.array([-1.0, -np.sqrt(3.0 / 7.0), 0.0, np.sqrt(3.0 / 7.0), 1.0])
gll_weights = np.array([0.1, 49.0 / 90.0, 32.0 / 45.0, 49.0 / 90.0, 0.1])
flow_dt = 0.4
diffusion = 0.2
coupling = 0.5
upper_gravity = 0.8
density_ratio = 0.7
speed_floor = 0.0001
load_factor = 4.0
solid_dt = 0.04


def extended(block, sides, width):
    for axis, dim in sides:
        count = lax.axis_size(axis)
        forward = [(i, i + 1) for i in range(count - 1)]
        backward = [(target, source) for source, target in forward]
        low = lax.ppermute(
            lax.slice_in_dim(block, block.shape[dim] - width, None, axis=dim), axis, forward
        )
        high = lax.ppermute(lax.slice_in_dim(block, 0, width, axis=dim), axis, backward)
        block = jnp.concatenate([low, block, high], axis=dim)
    return block


def legendre_four(x):
    return (35.0 * x**4 - 30.0 * x**2 + 3.0) / 8.0


def derivative_table():
    result = np.zeros((5, 5))
    for i in range(5):
        for j in range(5):
            if i != j:
                result[i, j] = (
                    legendre_four(gll_points[i])
                    / legendre_four(gll_points[j])
                    / (gll_points[i] - gll_points[j])
                )
    result[0, 0] = -5.0
    result[4, 4] = 5.0
    return result


def pressures(fields, buoyancy):
    press_one = buoyancy * (fields[0] + fields[1])
    press_two = upper_gravity * (density_ratio * fields[0] + fields[1])
    return jnp.concatenate([fields, press_one[None], press_two[None]], axis=0)


def advance(center, padded, drag_coefficient):
    ahead_x = padded[:, 2:, 1:-1]
    behind_x = padded[:, :-2, 1:-1]
    ahead_y = padded[:, 1:-1, 2:]
    behind_y = padded[:, 1:-1, :-2]
    slope_x = 0.5 * (ahead_x - behind_x)
    slope_y = 0.5 * (ahead_y - behind_y)
    spread = ahead_x + behind_x + ahead_y + behind_y - 4.0 * center
    flow_speed = jnp.sqrt(center[2] * center[2] + center[3] * center[3] + speed_floor)
    dense_depth = center[0] - flow_dt * (slope_x[2] + slope_y[3]) + diffusion * spread[0]
    light_depth = center[1] - flow_dt * (slope_x[4] + slope_y[5]) + diffusion * spread[1]
    dense_xmom = (
        center[2]
        - flow_dt
        * (
            slope_x[6]
            + drag_coefficient * flow_speed * center[2]
            + coupling * (center[2] - center[4])
        )
        + diffusion * spread[2]
    )
    dense_ymom = (
        center[3]
        - flow_dt
        * (
            slope_y[6]
            + drag_coefficient * flow_speed * center[3]
            + coupling * (center[3] - center[5])
        )
        + diffusion * spread[3]
    )
    light_xmom = (
        center[4]
        - flow_dt * (slope_x[7] + coupling * (center[4] - center[2]))
        + diffusion * spread[4]
    )
    light_ymom = (
        center[5]
        - flow_dt * (slope_y[7] + coupling * (center[5] - center[3]))
        + diffusion * spread[5]
    )
    return jnp.stack([dense_depth, light_depth, dense_xmom, dense_ymom, light_xmom, light_ymom])


def basal_traction(fields, buoyancy, drag_coefficient):
    flow_speed = jnp.sqrt(fields[2] * fields[2] + fields[3] * fields[3] + speed_floor)
    press_one = buoyancy * (fields[0] + fields[1])
    rubbing = load_factor * drag_coefficient * flow_speed
    return jnp.stack([rubbing * fields[2], rubbing * fields[3], -load_factor * press_one]).reshape(
        3, -1
    )


def weights_cube():
    cube = (
        gll_weights.reshape(5, 1, 1) * gll_weights.reshape(1, 5, 1) * gll_weights.reshape(1, 1, 5)
    )
    return jnp.asarray(cube.reshape(5, 5, 5, 1, 1, 1), jnp.float32)


def internal_force(values, lame_first, shear_modulus):
    highest = lax.Precision.HIGHEST
    table = jnp.asarray(derivative_table(), jnp.float32)
    weights_3d = weights_cube()
    gradients = [
        jnp.einsum("pa,iabczxy->ipbczxy", table, values, precision=highest),
        jnp.einsum("pb,iabczxy->iapczxy", table, values, precision=highest),
        jnp.einsum("pc,iabczxy->iabpzxy", table, values, precision=highest),
    ]
    divergence = gradients[0][0] + gradients[1][1] + gradients[2][2]
    forces = []
    for i in range(3):
        weighted = []
        for j in range(3):
            stress = shear_modulus * (gradients[j][i] + gradients[i][j])
            if i == j:
                stress = stress + lame_first * divergence
            weighted.append(weights_3d * stress)
        pulled = jnp.einsum("pa,pbczxy->abczxy", table, weighted[0], precision=highest)
        pulled = pulled + jnp.einsum("pb,apczxy->abczxy", table, weighted[1], precision=highest)
        pulled = pulled + jnp.einsum("pc,abpzxy->abczxy", table, weighted[2], precision=highest)
        forces.append(-pulled)
    return jnp.stack(forces)


def assemble(values):
    boundary = jnp.stack([values[:, 0, :, :, :, 0, :], values[:, 4, :, :, :, -1, :]])
    summed = values[:, 4, :, :, :, :-1, :] + values[:, 0, :, :, :, 1:, :]
    values = values.at[:, 4, :, :, :, :-1, :].set(summed).at[:, 0, :, :, :, 1:, :].set(summed)
    beyond = extended(boundary, (("gx", 0),), 1)
    values = values.at[:, 0, :, :, :, 0, :].add(beyond[0]).at[:, 4, :, :, :, -1, :].add(beyond[3])
    boundary = jnp.stack([values[:, :, 0, :, :, :, 0], values[:, :, 4, :, :, :, -1]])
    summed = values[:, :, 4, :, :, :, :-1] + values[:, :, 0, :, :, :, 1:]
    values = values.at[:, :, 4, :, :, :, :-1].set(summed).at[:, :, 0, :, :, :, 1:].set(summed)
    beyond = extended(boundary, (("gy", 0),), 1)
    values = values.at[:, :, 0, :, :, :, 0].add(beyond[0]).at[:, :, 4, :, :, :, -1].add(beyond[3])
    summed = values[:, :, :, 4, :-1] + values[:, :, :, 0, 1:]
    values = values.at[:, :, :, 4, :-1].set(summed).at[:, :, :, 0, 1:].set(summed)
    return values


def per_device(
    flow_state,
    drag_coefficient,
    wet_mask,
    target_elem,
    target_node,
    displacement,
    previous,
    density,
    lame_first,
    shear_modulus,
):
    buoyancy = 1.0 - 0.6 * wet_mask.astype(jnp.float32)
    fields = flow_state
    for counter in range(FLOW_STEPS):
        stacked = pressures(fields, buoyancy)
        padded = extended(stacked, (("gx", 1), ("gy", 2)), 1)
        fields = advance(stacked, padded, drag_coefficient)
    traction = basal_traction(fields, buoyancy, drag_coefficient)
    block_rows = displacement.shape[5]
    block_cols = displacement.shape[6]
    devices_y = lax.axis_size("gy")
    surface_cols = block_cols * devices_y
    flat_target = target_elem.reshape(-1)
    face_node = target_node.reshape(-1)
    elem_row = flat_target // surface_cols
    elem_col = flat_target % surface_cols
    local_x = elem_row - block_rows * lax.axis_index("gx") + 1
    local_y = elem_col - block_cols * lax.axis_index("gy") + 1
    slot_index = (face_node * (block_rows + 2) + local_x) * (block_cols + 2) + local_y
    load_table = jnp.zeros((3, 25 * (block_rows + 2) * (block_cols + 2)), jnp.float32)
    load_table = load_table.at[:, slot_index].add(traction)
    load_table = load_table.reshape(3, 25, block_rows + 2, block_cols + 2)
    beyond = extended(load_table, (("gx", 2), ("gy", 3)), 1)
    own_loads = load_table[:, :, 1:-1, 1:-1]
    own_loads = own_loads.at[:, :, 0, :].add(beyond[:, :, 0, 2:-2])
    own_loads = own_loads.at[:, :, -1, :].add(beyond[:, :, -1, 2:-2])
    own_loads = own_loads.at[:, :, :, 0].add(beyond[:, :, 2:-2, 0])
    own_loads = own_loads.at[:, :, :, -1].add(beyond[:, :, 2:-2, -1])
    own_loads = own_loads.at[:, :, 0, 0].add(beyond[:, :, 0, 0])
    own_loads = own_loads.at[:, :, 0, -1].add(beyond[:, :, 0, -1])
    own_loads = own_loads.at[:, :, -1, 0].add(beyond[:, :, -1, 0])
    own_loads = own_loads.at[:, :, -1, -1].add(beyond[:, :, -1, -1])
    surface_load = own_loads.reshape(3, 5, 5, block_rows, block_cols)
    masses = assemble(density[None, None, None, None] * weights_cube()[None])
    current = displacement
    for counter in range(SOLID_STEPS):
        force = internal_force(current, lame_first, shear_modulus)
        force = force.at[:, :, :, 0, 0].add(surface_load)
        acceleration = assemble(force) / masses
        advanced = 2.0 * current - previous + solid_dt * solid_dt * acceleration
        previous = current
        current = advanced
    return (fields, current, previous)


def solution(mesh):
    return jax.shard_map(
        per_device,
        mesh=mesh,
        in_specs=(
            P(None, "gx", "gy"),
            P("gx", "gy"),
            P("gx", "gy"),
            P("gx", "gy"),
            P("gx", "gy"),
            P(None, None, None, None, None, "gx", "gy"),
            P(None, None, None, None, None, "gx", "gy"),
            P(None, "gx", "gy"),
            P(None, "gx", "gy"),
            P(None, "gx", "gy"),
        ),
        out_specs=(
            P(None, "gx", "gy"),
            P(None, None, None, None, None, "gx", "gy"),
            P(None, None, None, None, None, "gx", "gy"),
        ),
        check_vma=False,
    )
```

profile of v0, /device:TPU:1, one launch (start us, length us, event | category | flops | bytes accessed | tf_op | source)
XLA Modules:
  0.0 1229.5 jit_solution(10349484038556478071)
XLA Ops:
  64.8 17.5 %scatter.70 = f32[1,5,5,5,2,2,128]{3,5,6,4,2,1,0:T(2,128)} dynamic-update-slice(f32[1,5,5,5,2,2,128]{3,5,6,4,2,1,0:T(2,128)} %copy-done.1, f32[1,1,5,5,2,1,128]{3,5,6,4,2,1,0:T(1,128)S(1)} %get-tuple-element.552, s32[]{:T(128)} %constant.1027.clone.1, s32[]{:T(128)} %constant.1025.clone.1, s32[]{:T(128)} %constant.1027.clone.1, s32[]{:T(128)} %constant.1027.clone.1, s32[]{:T(128)} %constant.1027.clone.1, ...) | dynamic-update-slice | bytes 51204 | tf_op jit(solution)/shard_map/scatter | solution.py:149
  82.3 4.2 compare_select_fusion
  86.5 4.2 broadcast_select_fusion
  92.0 18.2 %scatter.71 = f32[1,5,5,5,2,2,128]{3,5,6,4,2,1,0:T(2,128)} dynamic-update-slice(f32[1,5,5,5,2,2,128]{3,5,6,4,2,1,0:T(2,128)} %scatter.70, f32[1,1,5,5,2,1,128]{3,5,6,4,2,1,0:T(1,128)} %broadcast_select_fusion, s32[]{:T(128)} %constant.1027.clone.1, s32[]{:T(128)S(1)} %bitcast.688, s32[]{:T(128)} %constant.1027.clone.1, s32[]{:T(128)} %constant.1027.clone.1, s32[]{:T(128)} %constant.1027.clone.1, ...) | dynamic-update-slice | bytes 51204 | tf_op jit(solution)/shard_map/scatter | solution.py:149
  114.1 17.6 %scatter-add.104 = f32[1,5,5,5,2,2,128]{3,5,6,4,2,1,0:T(2,128)} dynamic-update-slice(f32[1,5,5,5,2,2,128]{3,5,6,4,2,1,0:T(2,128)} %scatter.71, f32[1,1,5,5,2,1,128]{3,5,6,4,2,1,0:T(1,128)} %slice_add_fusion.3, s32[]{:T(128)} %constant.1027.clone.1, s32[]{:T(128)} %constant.1027.clone.1, s32[]{:T(128)} %constant.1027.clone.1, s32[]{:T(128)} %constant.1027.clone.1, s32[]{:T(128)} %constant.1027.clone.1, ...) | dynamic-update-slice | bytes 51204 | tf_op jit(solution)/shard_map/scatter-add | solution.py:151
  135.9 17.6 %scatter-add.105 = f32[1,5,5,5,2,2,128]{3,5,6,4,2,1,0:T(2,128)} dynamic-update-slice(f32[1,5,5,5,2,2,128]{3,5,6,4,2,1,0:T(2,128)} %scatter-add.104, f32[1,1,5,5,2,1,128]{3,5,6,4,2,1,0:T(1,128)} %slice_add_fusion.2, s32[]{:T(128)} %constant.1027.clone.1, s32[]{:T(128)} %constant.1025.clone.1, s32[]{:T(128)} %constant.1027.clone.1, s32[]{:T(128)} %constant.1027.clone.1, s32[]{:T(128)} %constant.1027.clone.1, ...) | dynamic-update-slice | bytes 51204 | tf_op jit(solution)/shard_map/scatter-add | solution.py:151
  153.4 3.4 slice_add_fusion.1
  159.0 4.6 collective-permute-start.3
  167.2 4.8 multiply_subtract_fusion.3
  172.0 4.7 subtract_multiply_fusion.6
  188.2 6.4 copy.800
  194.6 4.1 collective-permute-start.26
  201.3 4.2 collective-permute-start.7
  209.5 5.3 collective-permute-done.6
  224.6 3.4 collective-permute-start.9
  228.0 4.1 select_dynamic-update-slice_fusion
  232.2 6.2 collective-permute-start.11
  242.1 6.1 collective-permute-done.10
  264.3 5.9 collective-permute-start.15
  271.4 5.2 slice_add_fusion
  276.6 4.8 copy.602
  281.4 4.0 copy.603
  285.4 266.5 %scatter.76 = f32[5,5,5,2,2,128]{2,4,5,3,1,0:T(2,128)} dynamic-update-slice(f32[5,5,5,2,2,128]{2,4,5,3,1,0:T(2,128)} %bitcast.664, f32[5,5,1,1,2,128]{2,4,5,3,1,0:T(2,128)} %copy.603, s32[]{:T(128)} %constant.1027.clone.1, s32[]{:T(128)} %constant.1027.clone.1, s32[]{:T(128)} %constant.1025.clone.1, s32[]{:T(128)} %constant.1027.clone.1, s32[]{:T(128)} %constant.1027.clone.1, s32[]{:T(128)} %constant.1027.clone.1) | dynamic-update-slice | bytes 51204 | tf_op jit(solution)/shard_map/scatter | solution.py:158
  551.9 52.1 %scatter.79 = f32[5,5,5,2,2,128]{2,4,5,3,1,0:T(2,128)} dynamic-update-slice(f32[5,5,5,2,2,128]{2,4,5,3,1,0:T(2,128)} %scatter.76, f32[5,5,1,1,2,128]{2,4,5,3,1,0:T(2,128)} %copy.603, s32[]{:T(128)} %constant.1027.clone.1, s32[]{:T(128)} %constant.1027.clone.1, s32[]{:T(128)S(1)} %bitcast.690, s32[]{:T(128)} %bitcast.96, s32[]{:T(128)} %constant.1027.clone.1, s32[]{:T(128)} %constant.1027.clone.1) | dynamic-update-slice | bytes 51204 | tf_op jit(solution)/shard_map/scatter | solution.py:158
  604.0 10.5 copy.605
  614.5 3.5 subtract_multiply_fusion.1
  624.7 15.9 %copy.585 = f32[65536,3]{1,0:T(8,128)} copy(f32[65536,3]{0,1:T(4,128)S(1)} %maximum_bitcast_fusion) | data formatting | bytes 1572864 | tf_op jit(solution)/shard_map/stack | solution.py:109
  640.6 350.5 %scatter_custom_fusion = f32[3,13000]{0,1:T(8,128)} fusion(s32[65536]{0:T(1024)} %bitcast.683, f32[65536,3]{1,0:T(8,128)} %copy.585, f32[]{:T(128)} %constant.1024.clone.1), kind=kCustom, calls=%fused_computation.1 | custom fusion | flops 196608 | bytes 156512 | tf_op jit(solution)/shard_map/scatter-add | solution.py:193
  991.1 4.6 copy.586
  996.2 4.0 collective-permute-start.16
  1006.3 5.0 collective-permute-start.18
  1017.2 4.0 collective-permute-done.19
  1021.3 5.6 scatter-add.86
  1030.6 6.9 scatter-add.90
  1039.4 5.7 scatter-add.94
  1045.6 5.1 collective-permute-start.20
  1054.1 3.7 collective-permute-done.21
  1064.2 6.1 scatter.64
  1072.6 26.7 %scatter.65 = f32[3,5,5,5,2,2,128]{6,4,3,2,0,5,1:T(2,128)S(1)} dynamic-update-slice(f32[3,5,5,5,2,2,128]{6,4,3,2,0,5,1:T(2,128)S(1)} %scatter.64, f32[3,5,1,5,2,2,127]{6,4,3,2,0,5,1:T(2,128)} %dynamic-slice_select_fusion.1, s32[]{:T(128)} %constant.1027.clone.1, s32[]{:T(128)} %constant.1027.clone.1, s32[]{:T(128)S(1)} %bitcast.693, s32[]{:T(128)} %constant.1027.clone.1, s32[]{:T(128)} %constant.1027.clone.1, ...) | dynamic-update-slice | bytes 304804 | tf_op jit(solution)/shard_map/scatter | solution.py:154
  1106.6 13.2 %scatter-add.101 = f32[3,5,5,5,2,2,128]{6,4,3,2,0,5,1:T(2,128)S(1)} dynamic-update-slice(f32[3,5,5,5,2,2,128]{6,4,3,2,0,5,1:T(2,128)S(1)} %scatter-add.100, f32[3,5,1,5,2,2,1]{6,4,3,2,0,5,1:T(2,128)S(1)} %slice_add_fusion.22, s32[]{:T(128)} %constant.1027.clone.1, s32[]{:T(128)} %constant.1027.clone.1, s32[]{:T(128)} %constant.1025.clone.1, s32[]{:T(128)} %constant.1027.clone.1, ...) | dynamic-update-slice | bytes 2404 | tf_op jit(solution)/shard_map/scatter-add | solution.py:156
  1123.2 4.0 scatter.69
  1151.5 3.7 collective-permute-done.29
  1158.7 5.5 collective-permute-start.30
  1164.2 6.1 scatter.84
  1172.7 26.7 %scatter.85 = f32[3,5,5,5,2,2,128]{6,4,3,2,0,5,1:T(2,128)S(1)} dynamic-update-slice(f32[3,5,5,5,2,2,128]{6,4,3,2,0,5,1:T(2,128)S(1)} %scatter.84, f32[3,5,1,5,2,2,127]{6,4,3,2,0,5,1:T(2,128)} %dynamic-slice_select_fusion, s32[]{:T(128)} %constant.1027.clone.1, s32[]{:T(128)} %constant.1027.clone.1, s32[]{:T(128)S(1)} %bitcast.697, s32[]{:T(128)} %constant.1027.clone.1, s32[]{:T(128)} %constant.1027.clone.1, ...) | dynamic-update-slice | bytes 304804 | tf_op jit(solution)/shard_map/scatter | solution.py:154
  1202.6 3.5 scatter-add.138
  1206.8 13.2 %scatter-add.139 = f32[3,5,5,5,2,2,128]{6,4,3,2,0,5,1:T(2,128)S(1)} dynamic-update-slice(f32[3,5,5,5,2,2,128]{6,4,3,2,0,5,1:T(2,128)S(1)} %scatter-add.138, f32[3,5,1,5,2,2,1]{6,4,3,2,0,5,1:T(2,128)S(1)} %slice_add_fusion.19, s32[]{:T(128)} %constant.1027.clone.1, s32[]{:T(128)} %constant.1027.clone.1, s32[]{:T(128)} %constant.1025.clone.1, s32[]{:T(128)} %constant.1027.clone.1, ...) | dynamic-update-slice | bytes 2404 | tf_op jit(solution)/shard_map/scatter-add | solution.py:156
  1223.3 3.8 scatter.89
  (334 shorter events, 214.1 us)
Async XLA Ops:
  3.0 7.4 copy-start.50
  3.0 7.6 copy-start.47
  4.0 152.9 %collective-permute-start = (f32[8,1,2048]{2,1,0:T(1,128)}, f32[8,1,2048]{2,1,0:T(1,128)}, u32[]{:S(2)}, u32[]{:S(2)}) collective-permute-start(f32[8,1,2048]{2,1,0:T(1,128)} %get-tuple-element.583), channel_id=1, source_target_pairs={{16,0},{32,16},{48,32},{64,48},{80,64},{96,80},{112,96},{17,1},{33... | collective-permute-start | bytes 196616 | tf_op jit(solution)/shard_map/ppermute | solution.py:31
  7.3 149.5 %collective-permute-start.1 = (f32[8,1,2048]{2,1,0:T(1,128)}, f32[8,1,2048]{2,1,0:T(1,128)}, u32[]{:S(2)}, u32[]{:S(2)}) collective-permute-start(f32[8,1,2048]{2,1,0:T(1,128)} %get-tuple-element.582), channel_id=1, source_target_pairs={{0,16},{16,32},{32,48},{48,64},{64,80},{80,96},{96,112},{1,17},{17... | collective-permute-start | bytes 196616 | tf_op jit(solution)/shard_map/ppermute | solution.py:28
  16.6 11.6 copy-start.3
  16.6 11.6 copy-start.43
  21.2 89.1 %collective-permute-start.24 = (f32[1,1,5,5,2,128]{5,4,3,2,1,0:T(2,128)}, f32[1,1,5,5,2,128]{5,4,3,2,1,0:T(2,128)}, u32[]{:S(2)}, u32[]{:S(2)}) collective-permute-start(f32[1,1,5,5,2,128]{5,4,3,2,1,0:T(2,128)} %copy.598), channel_id=1, source_target_pairs={{0,16},{16,32},{32,48},{48,64},{64,80},{80,96},{96,112},{1,17},{17... | collective-permute-start | bytes 76808 | tf_op jit(solution)/shard_map/ppermute | solution.py:28
  25.5 106.2 %collective-permute-start.25 = (f32[1,1,5,5,2,128]{5,4,3,2,1,0:T(2,128)}, f32[1,1,5,5,2,128]{5,4,3,2,1,0:T(2,128)}, u32[]{:S(2)}, u32[]{:S(2)}) collective-permute-start(f32[1,1,5,5,2,128]{5,4,3,2,1,0:T(2,128)} %copy.600), channel_id=1, source_target_pairs={{16,0},{32,16},{48,32},{64,48},{80,64},{96,80},{112,96},{17,1},{33... | collective-permute-start | bytes 76808 | tf_op jit(solution)/shard_map/ppermute | solution.py:31
  40.8 6.9 copy-start.41
  157.7 7.7 collective-permute-start.2
  159.0 8.2 collective-permute-start.3
  165.0 13.4 %copy-start.13 = (f32[8,32,2048]{2,1,0:T(8,128)}, f32[8,32,2048]{2,1,0:T(8,128)S(1)}, u32[]{:S(2)}) copy-start(f32[8,32,2048]{2,1,0:T(8,128)S(1)} %subtract_multiply_fusion.7) | copy-start | bytes 6291460
  181.3 18.8 %collective-permute-start.4 = (f32[8,1,2048]{2,1,0:T(1,128)}, f32[8,1,2048]{2,1,0:T(1,128)S(1)}, u32[]{:S(2)}, u32[]{:S(2)}) collective-permute-start(f32[8,1,2048]{2,1,0:T(1,128)} %get-tuple-element.581), channel_id=1, source_target_pairs={{16,0},{32,16},{48,32},{64,48},{80,64},{96,80},{112,96},{17,1},{33... | collective-permute-start | bytes 196616 | tf_op jit(solution)/shard_map/ppermute | solution.py:31
  183.5 16.7 %collective-permute-start.5 = (f32[8,1,2048]{2,1,0:T(1,128)}, f32[8,1,2048]{2,1,0:T(1,128)S(1)}, u32[]{:S(2)}, u32[]{:S(2)}) collective-permute-start(f32[8,1,2048]{2,1,0:T(1,128)} %get-tuple-element.580), channel_id=1, source_target_pairs={{0,16},{16,32},{32,48},{48,64},{64,80},{80,96},{96,112},{1,17},{17... | collective-permute-start | bytes 196616 | tf_op jit(solution)/shard_map/ppermute | solution.py:28
  194.6 12.2 copy-start.15
  194.6 45.2 %collective-permute-start.26 = (f32[1,1,5,5,2,2]{3,5,4,2,1,0:T(2,128)}, f32[1,1,5,5,2,2]{3,5,4,2,1,0:T(2,128)S(1)}, u32[]{:S(2)}, u32[]{:S(2)}) collective-permute-start(f32[1,1,5,5,2,2]{3,5,4,2,1,0:T(2,128)} %get-tuple-element.549), channel_id=1, source_target_pairs={{0,1},{1,2},{2,3},{3,4},{4,5},{5,6},{6,7},{7,8},{8,9},{9,10},{10,1... | collective-permute-start | bytes 1208 | tf_op jit(solution)/shard_map/ppermute | solution.py:28
  198.7 16.1 %copy-start.5 = (f32[8,32,2048]{2,1,0:T(8,128)S(1)}, f32[8,32,2048]{2,1,0:T(8,128)}, u32[]{:S(2)}) copy-start(f32[8,32,2048]{2,1,0:T(8,128)} %copy-done.4) | copy-start | bytes 6291460
  198.7 62.9 %collective-permute-start.27 = (f32[1,1,5,5,2,2]{3,5,4,2,1,0:T(2,128)}, f32[1,1,5,5,2,2]{3,5,4,2,1,0:T(2,128)S(1)}, u32[]{:S(2)}, u32[]{:S(2)}) collective-permute-start(f32[1,1,5,5,2,2]{3,5,4,2,1,0:T(2,128)} %get-tuple-element.548), channel_id=1, source_target_pairs={{1,0},{2,1},{3,2},{4,3},{5,4},{6,5},{7,6},{8,7},{9,8},{10,9},{11,1... | collective-permute-start | bytes 1208 | tf_op jit(solution)/shard_map/ppermute | solution.py:31
  201.3 8.2 collective-permute-start.7
  205.5 9.3 collective-permute-start.6
  218.9 9.1 slice-start
  220.4 7.6 slice-start.1
  222.3 9.8 collective-permute-start.8
  224.6 7.5 collective-permute-start.9
  232.2 9.9 collective-permute-start.11
  238.5 9.8 collective-permute-start.10
  256.0 5.6 collective-permute-start.12
  258.3 4.6 collective-permute-start.13
  261.6 9.8 copy-start.2
  264.3 350.2 %collective-permute-start.15 = (f32[8,34,1]{2,1,0:T(8,128)}, f32[8,34,1]{2,1,0:T(8,128)}, u32[]{:S(2)}, u32[]{:S(2)}) collective-permute-start(f32[8,34,1]{2,1,0:T(8,128)} %get-tuple-element.564), channel_id=1, source_target_pairs={{0,1},{1,2},{2,3},{3,4},{4,5},{5,6},{6,7},{7,8},{8,9},{9,10},{10,1... | collective-permute-start | bytes 3272 | tf_op jit(solution)/shard_map/ppermute | solution.py:28
  270.1 344.4 %collective-permute-start.14 = (f32[8,34,1]{2,1,0:T(8,128)}, f32[8,34,1]{2,1,0:T(8,128)}, u32[]{:S(2)}, u32[]{:S(2)}) collective-permute-start(f32[8,34,1]{2,1,0:T(8,128)} %get-tuple-element.565), channel_id=1, source_target_pairs={{1,0},{2,1},{3,2},{4,3},{5,4},{6,5},{7,6},{8,7},{9,8},{10,9},{11,1... | collective-permute-start | bytes 3272 | tf_op jit(solution)/shard_map/ppermute | solution.py:31
  991.1 11.5 copy-start.29
  991.1 11.5 copy-start.32
  996.2 8.3 collective-permute-start.16
  1000.2 5.7 collective-permute-start.17
  1004.5 40.6 %copy-start.12 = (f32[3,5,5,5,2,2,128]{6,1,5,4,3,2,0:T(8,128)S(1)}, f32[3,5,5,5,2,2,128]{6,1,5,4,3,2,0:T(8,128)}, u32[]{:S(2)}) copy-start(f32[3,5,5,5,2,2,128]{6,1,5,4,3,2,0:T(8,128)} %pad_maximum_fusion.41) | copy-start | bytes 2304004
  1006.3 9.3 collective-permute-start.18
  1012.1 9.1 collective-permute-start.19
  1045.6 8.4 collective-permute-start.20
  1052.1 5.7 collective-permute-start.21
  1059.9 67.3 %copy-start.34 = (f32[5,5,5,2,2,128]{5,3,2,1,4,0:T(2,128)S(1)}, f32[5,5,5,2,2,128]{5,3,2,1,4,0:T(2,128)}, u32[]{:S(2)}) copy-start(f32[5,5,5,2,2,128]{5,3,2,1,4,0:T(2,128)} %copy.605) | copy-start | bytes 768004
  1059.9 67.4 %copy-start.39 = (f32[3,5,5,5,2,2,128]{6,5,4,3,2,1,0:T(2,128)S(1)}, f32[3,5,5,5,2,2,128]{6,5,4,3,2,1,0:T(2,128)}, u32[]{:S(2)}) copy-start(f32[3,5,5,5,2,2,128]{6,5,4,3,2,1,0:T(2,128)} %param.101) | copy-start | bytes 2304004
  1061.3 40.7 %collective-permute-start.22 = (f32[1,3,5,5,2,2]{3,5,4,2,1,0:T(2,128)S(1)}, f32[1,3,5,5,2,2]{3,5,4,2,1,0:T(2,128)S(1)}, u32[]{:S(2)}, u32[]{:S(2)}) collective-permute-start(f32[1,3,5,5,2,2]{3,5,4,2,1,0:T(2,128)S(1)} %bitcast.702), channel_id=1, source_target_pairs={{0,1},{1,2},{2,3},{3,4},{4,5},{5,6},{6,7},{7,8},{8,9},{9,10},{10,1... | collective-permute-start | bytes 3608 | tf_op jit(solution)/shard_map/ppermute | solution.py:28
  1100.7 5.2 collective-permute-start.23
  1144.1 7.3 collective-permute-start.28
  1149.5 5.7 collective-permute-start.29
  1158.7 43.3 %collective-permute-start.30 = (f32[1,3,5,5,2,2]{3,5,4,2,1,0:T(2,128)S(1)}, f32[1,3,5,5,2,2]{3,5,4,2,1,0:T(2,128)S(1)}, u32[]{:S(2)}, u32[]{:S(2)}) collective-permute-start(f32[1,3,5,5,2,2]{3,5,4,2,1,0:T(2,128)S(1)} %bitcast.700), channel_id=1, source_target_pairs={{0,1},{1,2},{2,3},{3,4},{4,5},{5,6},{6,7},{7,8},{8,9},{9,10},{10,1... | collective-permute-start | bytes 3608 | tf_op jit(solution)/shard_map/ppermute | solution.py:28
  1200.7 5.4 collective-permute-start.31
  (37 other events, 103.3 us)
where the time goes:
time: 1250 us; the launch traced here: 1230 us
  local copies, waits for them, and re-layouts  613 us (49%)
  other arithmetic  456 us (36%)
  starting transfers between devices  95 us (8%)
  waiting for transfers between devices  33.4 us (3%)
  matrix products  29.2 us (2%)
    scatter-add x1, other arithmetic, per_device(): load_table = load_table.at[:, slot_index].add(traction)  350 us
    scatter x7, local copies, waits for them, and re-layouts, assemble(): values.at[:, :, :, 4, :-1].set(summed).at[:, :, :, 0, 1:].set(summed)  343 us
    scatter x5, local copies, waits for them, and re-layouts, assemble(): values.at[:, :, 4, :, :, :, :-1].set(summed).at[:, :, 0, :, :, :, 1:]  67.2 us
    ppermute x16, starting transfers between devices, extended(): lax.ppermute(lax.slice_in_dim(block, block.shape[dim] - width, None, axis...  65.7 us
    scatter x3, local copies, waits for them, and re-layouts, assemble(): values.at[:, 4, :, :, :, :-1, :].set(summed).at[:, 0, :, :, :, 1:, :]  35.8 us
    scatter-add x2, local copies, waits for them, and re-layouts, assemble(): values.at[:, 0, :, :, :, 0, :].add(beyond[0]).at[:, 4, :, :, :, -1, :]  35.1 us
    scatter-add x4, local copies, waits for them, and re-layouts, assemble(): values.at[:, :, 0, :, :, :, 0].add(beyond[0]).at[:, :, 4, :, :, :, -1]  33.2 us
    ppermute x16, starting transfers between devices, extended(): lax.ppermute(lax.slice_in_dim(block, 0, width, axis=dim), axis, backward)  29.4 us
  transfers between devices with their start and end apart: 32, of which 12 were waited for; matrix products, arithmetic and copies ran while one was open for 49% of the time, Pallas kernels for 0%

commit v1 on v0

--- a/solution.py
+++ b/solution.py
@@ -2,6 +2,8 @@
 import jax.numpy as jnp
 import numpy as np
 from jax import lax
+from jax.experimental import pallas as pl
+from jax.experimental.pallas import tpu as pltpu
 from jax.sharding import PartitionSpec as P
 
 FLOW_STEPS = 4
@@ -52,63 +54,242 @@
     return result
 
 
-def pressures(fields, buoyancy):
-    press_one = buoyancy * (fields[0] + fields[1])
-    press_two = upper_gravity * (density_ratio * fields[0] + fields[1])
-    return jnp.concatenate([fields, press_one[None], press_two[None]], axis=0)
-
-
-def advance(center, padded, drag_coefficient):
-    ahead_x = padded[:, 2:, 1:-1]
-    behind_x = padded[:, :-2, 1:-1]
-    ahead_y = padded[:, 1:-1, 2:]
-    behind_y = padded[:, 1:-1, :-2]
-    slope_x = 0.5 * (ahead_x - behind_x)
-    slope_y = 0.5 * (ahead_y - behind_y)
-    spread = ahead_x + behind_x + ahead_y + behind_y - 4.0 * center
-    flow_speed = jnp.sqrt(center[2] * center[2] + center[3] * center[3] + speed_floor)
-    dense_depth = center[0] - flow_dt * (slope_x[2] + slope_y[3]) + diffusion * spread[0]
-    light_depth = center[1] - flow_dt * (slope_x[4] + slope_y[5]) + diffusion * spread[1]
-    dense_xmom = (
-        center[2]
-        - flow_dt
-        * (
-            slope_x[6]
-            + drag_coefficient * flow_speed * center[2]
-            + coupling * (center[2] - center[4])
+def flow_body(
+    drag_ref, wet_ref, elem_ref, node_ref, flow_any,
+    xlo_ref, xhi_ref, ylo_ref, yhi_ref, corner_ref,
+    out_any, table_ref,
+    ext, drag, buoy, scale, tract, row_slot, col_slot, sems,
+):
+    rows, cols = drag_ref.shape
+    wide = cols + 128
+    tall = rows + 8
+    at_x, at_y = lax.axis_index("gx"), lax.axis_index("gy")
+    last_x, last_y = lax.axis_size("gx") - 1, lax.axis_size("gy") - 1
+    own_in = pltpu.make_async_copy(flow_any, ext.at[0, :, 0:rows, 0:cols], sems.at[0])
+    own_in.start()
+
+    def wetness(x):
+        return 1.0 - 0.6 * x
+
+    sub = lax.broadcasted_iota(jnp.int32, (8, 128), 0)
+    lane = lax.broadcasted_iota(jnp.int32, (8, 128), 1)
+    up_half = sub < 4
+    left_half = lane < 64
+
+    def zero_rows(tile):
+        tile = jnp.where(up_half & (at_x == last_x), 0.0, tile)
+        return jnp.where(jnp.logical_not(up_half) & (at_x == 0), 0.0, tile)
+
+    def zero_cols(tile):
+        tile = jnp.where(left_half & (at_y == last_y), 0.0, tile)
+        return jnp.where(jnp.logical_not(left_half) & (at_y == 0), 0.0, tile)
+
+    def place(k, r, c, tile):
+        if k < 6:
+            ext[0, k, r, c] = tile
+        elif k == 6:
+            drag[r, c] = tile
+        else:
+            buoy[r, c] = wetness(tile)
+
+    tail = pl.ds(cols, 128)
+    foot = pl.ds(rows, 8)
+    ones = jnp.full((8, 128), 0.2, jnp.float32)
+    row_scale = zero_rows(ones)
+    col_scale = zero_cols(ones)
+
+    def halo_rows(t, carry):
+        at = pl.ds(pl.multiple_of(t * 128, 128), 128)
+        for k in range(8):
+            tile = jnp.where(up_half, xhi_ref[k, :, at], xlo_ref[k, :, at])
+            place(k, foot, at, zero_rows(tile))
+        for r in range(0, rows, 8):
+            scale[r : r + 8, at] = ones
+        scale[foot, at] = row_scale
+        return carry
+
+    lax.fori_loop(0, cols // 128, halo_rows, 0)
+    for k in range(8):
+        for r in range(0, rows, 8):
+            tile = jnp.where(left_half, yhi_ref[k, r : r + 8, :], ylo_ref[k, r : r + 8, :])
+            place(k, pl.ds(r, 8), tail, zero_cols(tile))
+        tile = jnp.where(
+            up_half,
+            jnp.where(left_half, corner_ref[3, k], corner_ref[2, k]),
+            jnp.where(left_half, corner_ref[1, k], corner_ref[0, k]),
         )
-        + diffusion * spread[2]
-    )
-    dense_ymom = (
-        center[3]
-        - flow_dt
-        * (
-            slope_y[6]
-            + drag_coefficient * flow_speed * center[3]
-            + coupling * (center[3] - center[5])
+        place(k, foot, tail, zero_cols(zero_rows(tile)))
+    for r in range(0, rows, 8):
+        scale[r : r + 8, tail] = col_scale
+    scale[foot, tail] = zero_cols(row_scale)
+
+    def own_cells(t, carry):
+        at = pl.ds(pl.multiple_of(t * 128, 128), 128)
+        drag[0:rows, at] = drag_ref[:, at]
+        buoy[0:rows, at] = wetness(wet_ref[:, at].astype(jnp.float32))
+        e = elem_ref[:, at]
+        n = node_ref[:, at]
+        surface_cols = 128 * (last_y + 1)
+        er = e // surface_cols
+        lx = er - 2 * at_x + 1
+        ly = (e - er * surface_cols) - 128 * at_y + 1
+        inside = (ly >= 1) & (ly <= 128)
+        a = jnp.where(inside, 2 * n + (lx & 1), 50)
+        b = jnp.where(
+            inside,
+            (lx >> 1) * 128 + ly - 1,
+            jnp.where(ly == 0, 0, 128) + 4 * n + lx,
         )
-        + diffusion * spread[3]
-    )
-    light_xmom = (
-        center[4]
-        - flow_dt * (slope_x[7] + coupling * (center[4] - center[2]))
-        + diffusion * spread[4]
-    )
-    light_ymom = (
-        center[5]
-        - flow_dt * (slope_y[7] + coupling * (center[5] - center[3]))
-        + diffusion * spread[5]
-    )
-    return jnp.stack([dense_depth, light_depth, dense_xmom, dense_ymom, light_xmom, light_ymom])
-
-
-def basal_traction(fields, buoyancy, drag_coefficient):
-    flow_speed = jnp.sqrt(fields[2] * fields[2] + fields[3] * fields[3] + speed_floor)
-    press_one = buoyancy * (fields[0] + fields[1])
-    rubbing = load_factor * drag_coefficient * flow_speed
-    return jnp.stack([rubbing * fields[2], rubbing * fields[3], -load_factor * press_one]).reshape(
-        3, -1
-    )
+        row_slot[:, at] = a.astype(jnp.float32)
+        col_slot[:, at] = b.astype(jnp.float32)
+        return carry
+
+    lax.fori_loop(0, cols // 128, own_cells, 0)
+    own_in.wait()
+
+    lanes = lax.broadcasted_iota(jnp.int32, (tall, 128), 1)
+    first_lane = lanes == 0
+    last_lane = lanes == 127
+    tiles = wide // 128
+
+    def press(f0, f1, b):
+        return b * (f0 + f1), upper_gravity * density_ratio * f0 + upper_gravity * f1
+
+    def step(s, carry):
+        now = s % 2
+        later = 1 - now
+
+        def tile_step(t, carry):
+            at = pl.ds(pl.multiple_of(t * 128, 128), 128)
+            t_hi = jnp.where(t == tiles - 1, 0, t + 1)
+            t_lo = jnp.where(t == 0, tiles - 1, t - 1)
+            at_hi = pl.ds(pl.multiple_of(t_hi * 128, 128), 128)
+            at_lo = pl.ds(pl.multiple_of(t_lo * 128, 128), 128)
+            f = [ext[now, k, :, at] for k in range(6)]
+            b = buoy[:, at]
+            one, two = press(f[0], f[1], b)
+            sums = [None] * 6
+
+            def add(k, value):
+                sums[k] = value if sums[k] is None else sums[k] + value
+
+            for ahead in (True, False):
+                by = tall - 1 if ahead else 1
+                def rolled(x):
+                    return pltpu.roll(x, by, 0)
+                sg = -1.0 if ahead else 1.0
+                def mix(x, y):
+                    return x - y if ahead else x + y
+                add(0, rolled(mix(f[0], f[2])))
+                add(1, rolled(mix(f[1], f[4])))
+                add(2, rolled(mix(f[2], one)))
+                add(3, rolled(f[3]))
+                add(4, rolled(mix(f[4], two)))
+                add(5, rolled(f[5]))
+            for ahead in (True, False):
+                by = 127 if ahead else 1
+                edge = first_lane if ahead else last_lane
+                other = at_hi if ahead else at_lo
+                g = [jnp.where(edge, ext[now, k, :, other], f[k]) for k in range(6)]
+                gb = jnp.where(edge, buoy[:, other], b)
+                g_one, g_two = press(g[0], g[1], gb)
+                def rolled(x):
+                    return pltpu.roll(x, by, 1)
+                def mix(x, y):
+                    return x - y if ahead else x + y
+                add(0, rolled(mix(g[0], g[3])))
+                add(1, rolled(mix(g[1], g[5])))
+                add(2, rolled(g[2]))
+                add(3, rolled(mix(g[3], g_one)))
+                add(4, rolled(g[4]))
+                add(5, rolled(mix(g[5], g_two)))
+            speed = jnp.sqrt(f[2] * f[2] + f[3] * f[3] + speed_floor)
+            rub = 2.0 * drag[:, at] * speed
+            k = scale[:, at]
+            ext[later, 0, :, at] = k * (f[0] + sums[0])
+            ext[later, 1, :, at] = k * (f[1] + sums[1])
+            ext[later, 2, :, at] = k * (sums[2] + f[4] - rub * f[2])
+            ext[later, 3, :, at] = k * (sums[3] + f[5] - rub * f[3])
+            ext[later, 4, :, at] = k * (sums[4] + f[2])
+            ext[later, 5, :, at] = k * (sums[5] + f[3])
+            return carry
+
+        return lax.fori_loop(0, tiles, tile_step, carry)
+
+    lax.fori_loop(0, FLOW_STEPS, step, 0)
+    own_out = pltpu.make_async_copy(ext.at[0, :, 0:rows, 0:cols], out_any, sems.at[1])
+    own_out.start()
+
+    def pull(t, carry):
+        at = pl.ds(pl.multiple_of(t * 128, 128), 128)
+        f = [ext[0, k, 0:rows, at] for k in range(4)]
+        rub = load_factor * drag[0:rows, at] * jnp.sqrt(f[2] * f[2] + f[3] * f[3] + speed_floor)
+        tract[0, :, at] = rub * f[2]
+        tract[1, :, at] = rub * f[3]
+        tract[2, :, at] = -load_factor * (buoy[0:rows, at] * (f[0] + f[1]))
+        return carry
+
+    lax.fori_loop(0, cols // 128, pull, 0)
+
+    table_ref[...] = jnp.zeros_like(table_ref)
+    count = lax.broadcasted_iota(jnp.int32, (16, cols), 0).astype(jnp.float32).astype(jnp.bfloat16)
+
+    def spread(r, carry):
+        line = pl.ds(r, 1)
+
+        def wide16(x):
+            return jnp.broadcast_to(x, (16, cols)).astype(jnp.bfloat16)
+
+        parts = []
+        for k in range(3):
+            value = tract[k, line, :]
+            high = value.astype(jnp.bfloat16).astype(jnp.float32)
+            parts.append(wide16(value))
+            parts.append(wide16(value - high))
+        a = wide16(row_slot[line, :])
+        b = wide16(col_slot[line, :])
+        zero = jnp.zeros((16, cols), jnp.bfloat16)
+        one = jnp.ones((16, cols), jnp.bfloat16)
+        hits = [a == count + jnp.bfloat16(16 * m) for m in range(4)]
+        left = jnp.concatenate([jnp.where(h, p, zero) for p in parts for h in hits], axis=0)
+        right = jnp.concatenate(
+            [jnp.where(b == count + jnp.bfloat16(16 * m), one, zero) for m in range(16)], axis=0
+        )
+        got = lax.dot_general(
+            left, right, (((1,), (1,)), ((), ())), preferred_element_type=jnp.float32
+        )
+        table_ref[...] += got
+        return carry
+
+    lax.fori_loop(0, rows, spread, 0)
+    own_out.wait()
+
+
+def flow_call(flow, drag, wet, elem, node, xlo, xhi, ylo, yhi, corner):
+    rows, cols = drag.shape
+    tall, wide = rows + 8, cols + 128
+    vmem = pl.BlockSpec(memory_space=pltpu.VMEM)
+    hbm = pl.BlockSpec(memory_space=pl.ANY)
+    return pl.pallas_call(
+        flow_body,
+        out_shape=(
+            jax.ShapeDtypeStruct((6, rows, cols), jnp.float32),
+            jax.ShapeDtypeStruct((384, 256), jnp.float32),
+        ),
+        in_specs=[vmem] * 4 + [hbm] + [vmem] * 5,
+        out_specs=(hbm, vmem),
+        scratch_shapes=[
+            pltpu.VMEM((2, 6, tall, wide), jnp.float32),
+            pltpu.VMEM((tall, wide), jnp.float32),
+            pltpu.VMEM((tall, wide), jnp.float32),
+            pltpu.VMEM((tall, wide), jnp.float32),
+            pltpu.VMEM((3, rows, cols), jnp.float32),
+            pltpu.VMEM((rows, cols), jnp.float32),
+            pltpu.VMEM((rows, cols), jnp.float32),
+            pltpu.SemaphoreType.DMA((2,)),
+        ],
+        compiler_params=pltpu.CompilerParams(vmem_limit_bytes=48 * 2**20),
+    )(drag, wet, elem, node, flow, xlo, xhi, ylo, yhi, corner)
 
 
 def weights_cube():
@@ -171,27 +352,30 @@
     lame_first,
     shear_modulus,
 ):
-    buoyancy = 1.0 - 0.6 * wet_mask.astype(jnp.float32)
-    fields = flow_state
-    for counter in range(FLOW_STEPS):
-        stacked = pressures(fields, buoyancy)
-        padded = extended(stacked, (("gx", 1), ("gy", 2)), 1)
-        fields = advance(stacked, padded, drag_coefficient)
-    traction = basal_traction(fields, buoyancy, drag_coefficient)
+    stacked = jnp.concatenate(
+        [flow_state, drag_coefficient[None], wet_mask.astype(jnp.float32)[None]], axis=0
+    )
+    ring_x, ring_y = lax.axis_size("gx"), lax.axis_size("gy")
+
+    def moved(x, axis, count, by):
+        return lax.ppermute(x, axis, [(i, (i + by) % count) for i in range(count)])
+
+    x_lo = moved(stacked[:, -8:, :], "gx", ring_x, 1)
+    x_hi = moved(stacked[:, :8, :], "gx", ring_x, -1)
+    y_lo = moved(stacked[:, :, -128:], "gy", ring_y, 1)
+    y_hi = moved(stacked[:, :, :128], "gy", ring_y, -1)
+    corner_lo = moved(jnp.stack([x_lo[:, :, -128:], x_hi[:, :, -128:]]), "gy", ring_y, 1)
+    corner_hi = moved(jnp.stack([x_lo[:, :, :128], x_hi[:, :, :128]]), "gy", ring_y, -1)
+    corner = jnp.stack([corner_lo[0], corner_hi[0], corner_lo[1], corner_hi[1]])
+    fields, slots = flow_call(
+        flow_state, drag_coefficient, wet_mask, target_elem, target_node,
+        x_lo, x_hi, y_lo, y_hi, corner,
+    )
     block_rows = displacement.shape[5]
-    block_cols = displacement.shape[6]
-    devices_y = lax.axis_size("gy")
-    surface_cols = block_cols * devices_y
-    flat_target = target_elem.reshape(-1)
-    face_node = target_node.reshape(-1)
-    elem_row = flat_target // surface_cols
-    elem_col = flat_target % surface_cols
-    local_x = elem_row - block_rows * lax.axis_index("gx") + 1
-    local_y = elem_col - block_cols * lax.axis_index("gy") + 1
-    slot_index = (face_node * (block_rows + 2) + local_x) * (block_cols + 2) + local_y
-    load_table = jnp.zeros((3, 25 * (block_rows + 2) * (block_cols + 2)), jnp.float32)
-    load_table = load_table.at[:, slot_index].add(traction)
-    load_table = load_table.reshape(3, 25, block_rows + 2, block_cols + 2)
+    slots = slots.reshape(3, 2, 64, 256).sum(axis=1)
+    middle = slots[:, :50].reshape(3, 25, 2, 2, 128).transpose(0, 1, 3, 2, 4).reshape(3, 25, 4, 128)
+    sides = slots[:, 50].reshape(3, 2, 128)[:, :, :100].reshape(3, 2, 25, 4)
+    load_table = jnp.concatenate([sides[:, 0, :, :, None], middle, sides[:, 1, :, :, None]], axis=3)
     beyond = extended(load_table, (("gx", 2), ("gy", 3)), 1)
     own_loads = load_table[:, :, 1:-1, 1:-1]
     own_loads = own_loads.at[:, :, 0, :].add(beyond[:, :, 0, 2:-2])
@@ -202,7 +386,7 @@
     own_loads = own_loads.at[:, :, 0, -1].add(beyond[:, :, 0, -1])
     own_loads = own_loads.at[:, :, -1, 0].add(beyond[:, :, -1, 0])
     own_loads = own_loads.at[:, :, -1, -1].add(beyond[:, :, -1, -1])
-    surface_load = own_loads.reshape(3, 5, 5, block_rows, block_cols)
+    surface_load = own_loads.reshape(3, 5, 5, block_rows, displacement.shape[6])
     masses = assemble(density[None, None, None, None] * weights_cube()[None])
     current = displacement
     for counter in range(SOLID_STEPS):

time: 1250 us -> 787 us (0.63)
  other arithmetic: 456 us -> 59.7 us
  starting transfers between devices: 95 us -> 56.7 us
  Pallas kernels: 0 us -> 30.7 us
  local copies, waits for them, and re-layouts: 613 us -> 583 us
  waiting for transfers between devices: 33.4 us -> 18.8 us
    scatter-add x1 -> x0, other arithmetic: 350 us -> none  [per_device(): load_table = load_table.at[:, slot_index].add(traction)]
    ppermute x16 -> x8, starting transfers between devices: 65.7 us -> 30.8 us  [extended(): lax.ppermute(lax.slice_in_dim(block, block.shape[dim] - width, None, axis...]
    pallas_call x0 -> x1, Pallas kernels: none -> 30.7 us  [flow_call(): pl.pallas_call(flow_body, out_shape=(jax.ShapeDtypeStruct((6, rows, cols)...]
    mul x9 -> x0, other arithmetic: 21.9 us -> none  [the longest x4 10.8 us: advance(): slope_y = 0.5 * (ahead_y - behind_y)]
    ppermute x16 -> x8, starting transfers between devices: 29.4 us -> 12.9 us  [extended(): lax.ppermute(lax.slice_in_dim(block, 0, width, axis=dim), axis, backward)]
    another operation x11 -> x15, local copies, waits for them, and re-layouts: 22.4 us -> 6.59 us  [the longest x1 15.9 us: basal_traction(): jnp.stack([rubbing * fields[2], rubbing * fields[3], -load_factor * press...]
    ppermute x0 -> x6, starting transfers between devices: none -> 12.9 us  [moved(): return lax.ppermute(x, axis, [(i, (i + by) % count) for i in range(count)])]
  transfers between devices with their start and end apart: 32 -> 22, of which waited for: 12 -> 6; matrix products, arithmetic and copies ran while one was open for 49% -> 72% of each run, Pallas kernels for 0% -> 0%
where the time goes in v1:
time: 787 us; the launch traced here: 773 us
  local copies, waits for them, and re-layouts  583 us (74%)
  other arithmetic  59.7 us (8%)
  starting transfers between devices  56.7 us (7%)
  Pallas kernels  30.7 us (4%)
  matrix products  22.4 us (3%)
  waiting for transfers between devices  18.8 us (2%)
    scatter x7, local copies, waits for them, and re-layouts, assemble(): values.at[:, :, :, 4, :-1].set(summed).at[:, :, :, 0, 1:].set(summed)  345 us
    scatter x5, local copies, waits for them, and re-layouts, assemble(): values.at[:, :, 4, :, :, :, :-1].set(summed).at[:, :, 0, :, :, :, 1:]  67.7 us
    scatter x3, local copies, waits for them, and re-layouts, assemble(): values.at[:, 4, :, :, :, :-1, :].set(summed).at[:, 0, :, :, :, 1:, :]  36 us
    scatter-add x2, local copies, waits for them, and re-layouts, assemble(): values.at[:, 0, :, :, :, 0, :].add(beyond[0]).at[:, 4, :, :, :, -1, :]  35.1 us
    scatter-add x4, local copies, waits for them, and re-layouts, assemble(): values.at[:, :, 0, :, :, :, 0].add(beyond[0]).at[:, :, 4, :, :, :, -1]  33.2 us
    ppermute x8, starting transfers between devices, extended(): lax.ppermute(lax.slice_in_dim(block, block.shape[dim] - width, None, axis...  30.8 us
    pallas_call x1, Pallas kernels, flow_call(): pl.pallas_call(flow_body, out_shape=(jax.ShapeDtypeStruct((6, rows, cols)...  30.7 us
    unnamed x65, local copies, waits for them, and re-layouts  18 us
  transfers between devices with their start and end apart: 22, of which 6 were waited for; matrix products, arithmetic and copies ran while one was open for 72% of the time, Pallas kernels for 0%

profile of v1, /device:TPU:1, one launch (start us, length us, event | category | flops | bytes accessed | tf_op | source)
XLA Modules:
  0.0 773.2 jit_solution(5272152411148475731)
XLA Ops:
  1.4 4.0 broadcast_multiply_fusion
  5.5 2.7 copy-done.9
  8.2 2.6 fusion.98
  11.6 4.5 collective-permute-start.14
  26.5 2.4 fusion.5
  44.0 17.8 %scatter.70 = f32[1,5,5,5,2,2,128]{3,5,6,4,2,1,0:T(2,128)} dynamic-update-slice(f32[1,5,5,5,2,2,128]{3,5,6,4,2,1,0:T(2,128)} %copy-done.9, f32[1,1,5,5,2,1,128]{3,5,6,4,2,1,0:T(1,128)} %get-tuple-element.516, s32[]{:T(128)} %constant.969.clone.1, s32[]{:T(128)} %constant.975.clone.1, s32[]{:T(128)} %constant.969.clone.1, s32[]{:T(128)} %constant.969.clone.1, s32[]{:T(128)} %constant.969.clone.1, ...) | dynamic-update-slice | bytes 51204 | tf_op jit(solution)/shard_map/scatter | solution.py:330
  61.8 2.5 pad_maximum_fusion.1
  64.3 4.3 broadcast_select_fusion
  69.3 18.2 %scatter.71 = f32[1,5,5,5,2,2,128]{3,5,6,4,2,1,0:T(2,128)} dynamic-update-slice(f32[1,5,5,5,2,2,128]{3,5,6,4,2,1,0:T(2,128)} %scatter.70, f32[1,1,5,5,2,1,128]{3,5,6,4,2,1,0:T(1,128)} %broadcast_select_fusion, s32[]{:T(128)} %constant.969.clone.1, s32[]{:T(128)S(1)} %bitcast.287, s32[]{:T(128)} %constant.969.clone.1, s32[]{:T(128)} %constant.969.clone.1, s32[]{:T(128)} %constant.969.clone.1, ...) | dynamic-update-slice | bytes 51204 | tf_op jit(solution)/shard_map/scatter | solution.py:330
  88.1 4.6 collective-permute-start.3
  94.5 3.0 slice_add_fusion.3
  97.6 17.6 %scatter-add.95 = f32[1,5,5,5,2,2,128]{3,5,6,4,2,1,0:T(2,128)} dynamic-update-slice(f32[1,5,5,5,2,2,128]{3,5,6,4,2,1,0:T(2,128)} %scatter.71, f32[1,1,5,5,2,1,128]{3,5,6,4,2,1,0:T(1,128)} %slice_add_fusion.3, s32[]{:T(128)} %constant.969.clone.1, s32[]{:T(128)} %constant.969.clone.1, s32[]{:T(128)} %constant.969.clone.1, s32[]{:T(128)} %constant.969.clone.1, s32[]{:T(128)} %constant.969.clone.1, ...) | dynamic-update-slice | bytes 51204 | tf_op jit(solution)/shard_map/scatter-add | solution.py:332
  117.0 3.4 slice_add_fusion.2
  120.3 17.6 %scatter-add.96 = f32[1,5,5,5,2,2,128]{3,5,6,4,2,1,0:T(2,128)} dynamic-update-slice(f32[1,5,5,5,2,2,128]{3,5,6,4,2,1,0:T(2,128)} %scatter-add.95, f32[1,1,5,5,2,1,128]{3,5,6,4,2,1,0:T(1,128)} %slice_add_fusion.2, s32[]{:T(128)} %constant.969.clone.1, s32[]{:T(128)} %constant.975.clone.1, s32[]{:T(128)} %constant.969.clone.1, s32[]{:T(128)} %constant.969.clone.1, s32[]{:T(128)} %constant.969.clone.1, ...) | dynamic-update-slice | bytes 51204 | tf_op jit(solution)/shard_map/scatter-add | solution.py:332
  137.9 6.4 copy.781
  144.3 2.4 slice_add_fusion.1
  150.2 5.3 select_dynamic-update-slice_fusion
  161.8 4.5 collective-permute-start.5
  171.1 30.7 %shard_map.166 = (f32[6,32,2048]{2,1,0:T(8,128)}, f32[384,256]{1,0:T(8,128)S(1)}) custom-call(f32[32,2048]{1,0:T(8,128)S(1)} %copy-done.1, s32[32,2048]{1,0:T(8,128)S(1)} %copy-done.2, s32[32,2048]{1,0:T(8,128)S(1)} %copy-done.3, s32[32,2048]{1,0:T(8,128)S(1)} %copy-done.4, f32[6,32,2048]{2,1,0:T(8,128)S(1)} %copy-done, ...), custom_call_target="tpu_custom_call" | custom-call | tf_op jit(solution)/shard_map/pallas_call | solution.py:273
  204.6 6.7 collective-permute-start.6
  213.2 6.4 slice_add_fusion
  222.6 267.4 %scatter.76 = f32[5,5,5,2,2,128]{2,4,5,3,1,0:T(2,128)} dynamic-update-slice(f32[5,5,5,2,2,128]{2,4,5,3,1,0:T(2,128)} %bitcast.265, f32[5,5,1,1,2,128]{2,4,5,3,1,0:T(2,128)S(1)} %copy.611, s32[]{:T(128)} %constant.969.clone.1, s32[]{:T(128)} %constant.969.clone.1, s32[]{:T(128)} %constant.975.clone.1, s32[]{:T(128)} %constant.969.clone.1, s32[]{:T(128)} %constant.969.clone.1, s32[]{:T(128)} %constant.969.clone.1) | dynamic-update-slice | bytes 51204 | tf_op jit(solution)/shard_map/scatter | solution.py:339
  490.0 53.0 %scatter.79 = f32[5,5,5,2,2,128]{2,4,5,3,1,0:T(2,128)} dynamic-update-slice(f32[5,5,5,2,2,128]{2,4,5,3,1,0:T(2,128)} %scatter.76, f32[5,5,1,1,2,128]{2,4,5,3,1,0:T(2,128)S(1)} %copy.611, s32[]{:T(128)} %constant.969.clone.1, s32[]{:T(128)} %constant.969.clone.1, s32[]{:T(128)S(1)} %bitcast.289, s32[]{:T(128)} %bitcast.47, s32[]{:T(128)} %constant.969.clone.1, s32[]{:T(128)} %constant.969.clone.1) | dynamic-update-slice | bytes 51204 | tf_op jit(solution)/shard_map/scatter | solution.py:339
  543.1 9.9 %copy.613 = f32[5,5,5,2,2,128]{5,3,2,1,4,0:T(2,128)S(1)} copy(f32[5,5,5,2,2,128]{2,4,5,3,1,0:T(2,128)} %scatter.79) | data formatting | bytes 512000 | tf_op jit(solution)/shard_map/scatter | solution.py:339
  554.5 2.4 collective-permute-start.8
  563.3 6.0 collective-permute-done.9
  569.5 5.6 scatter-add.79
  577.9 7.1 scatter-add.81
  585.8 5.7 scatter-add.85
  592.1 5.0 collective-permute-start.10
  600.5 3.7 collective-permute-done.11
  605.5 3.8 collective-permute-start.12
  609.3 6.3 scatter.64
  617.2 26.8 %scatter.65 = f32[3,5,5,5,2,2,128]{6,4,3,2,0,5,1:T(2,128)S(1)} dynamic-update-slice(f32[3,5,5,5,2,2,128]{6,4,3,2,0,5,1:T(2,128)S(1)} %scatter.64, f32[3,5,1,5,2,2,127]{6,4,3,2,0,5,1:T(2,128)S(1)} %dynamic-slice_select_fusion.1, s32[]{:T(128)} %constant.969.clone.1, s32[]{:T(128)} %constant.969.clone.1, s32[]{:T(128)S(1)} %bitcast.292, s32[]{:T(128)} %constant.969.clone.1, s32[]{:T(128)} %constant.969.clone.1, ...) | dynamic-update-slice | bytes 304804 | tf_op jit(solution)/shard_map/scatter | solution.py:335
  646.5 3.3 scatter-add.91
  650.5 13.2 %scatter-add.94 = f32[3,5,5,5,2,2,128]{6,4,3,2,0,5,1:T(2,128)S(1)} dynamic-update-slice(f32[3,5,5,5,2,2,128]{6,4,3,2,0,5,1:T(2,128)S(1)} %scatter-add.91, f32[3,5,1,5,2,2,1]{6,4,3,2,0,5,1:T(2,128)S(1)} %slice_add_fusion.14, s32[]{:T(128)} %constant.969.clone.1, s32[]{:T(128)} %constant.969.clone.1, s32[]{:T(128)} %constant.975.clone.1, s32[]{:T(128)} %constant.969.clone.1, s32[]{:T(128)} %constant.969.clone.1, ...) | dynamic-update-slice | bytes 2404 | tf_op jit(solution)/shard_map/scatter-add | solution.py:337
  663.9 3.2 scatter.66
  667.0 4.0 scatter.69
  685.8 3.2 scatter-add.101
  689.3 2.9 collective-permute-start.18
  696.9 3.7 collective-permute-done.19
  703.4 4.1 collective-permute-start.20
  707.6 6.3 scatter.84
  715.5 26.8 %scatter.85 = f32[3,5,5,5,2,2,128]{6,4,3,2,0,5,1:T(2,128)S(1)} dynamic-update-slice(f32[3,5,5,5,2,2,128]{6,4,3,2,0,5,1:T(2,128)S(1)} %scatter.84, f32[3,5,1,5,2,2,127]{6,4,3,2,0,5,1:T(2,128)S(1)} %dynamic-slice_select_fusion, s32[]{:T(128)} %constant.969.clone.1, s32[]{:T(128)} %constant.969.clone.1, s32[]{:T(128)S(1)} %bitcast.296, s32[]{:T(128)} %constant.969.clone.1, s32[]{:T(128)} %constant.969.clone.1, ...) | dynamic-update-slice | bytes 304804 | tf_op jit(solution)/shard_map/scatter | solution.py:335
  746.3 3.5 scatter-add.106
  750.5 13.2 %scatter-add.109 = f32[3,5,5,5,2,2,128]{6,4,3,2,0,5,1:T(2,128)S(1)} dynamic-update-slice(f32[3,5,5,5,2,2,128]{6,4,3,2,0,5,1:T(2,128)S(1)} %scatter-add.106, f32[3,5,1,5,2,2,1]{6,4,3,2,0,5,1:T(2,128)S(1)} %slice_add_fusion.11, s32[]{:T(128)} %constant.969.clone.1, s32[]{:T(128)} %constant.969.clone.1, s32[]{:T(128)} %constant.975.clone.1, s32[]{:T(128)} %constant.969.clone.1, s32[]{:T(128)} %constant.969.clone.1, ...) | dynamic-update-slice | bytes 2404 | tf_op jit(solution)/shard_map/scatter-add | solution.py:337
  763.9 3.2 scatter.86
  767.1 3.8 scatter.89
  (222 shorter events, 106.5 us)
Async XLA Ops:
  5.5 2.7 copy-start.9
  8.2 10.7 %copy-start.2 = (s32[32,2048]{1,0:T(8,128)S(1)}, s32[32,2048]{1,0:T(8,128)}, u32[]{:S(2)}) copy-start(s32[32,2048]{1,0:T(8,128)} %wet_ref.1) | copy-start | bytes 786436
  10.8 8.1 %copy-start = (f32[6,32,2048]{2,1,0:T(8,128)S(1)}, f32[6,32,2048]{2,1,0:T(8,128)}, u32[]{:S(2)}) copy-start(f32[6,32,2048]{2,1,0:T(8,128)} %flow_any.1) | copy-start | bytes 4718596
  10.8 8.2 %copy-start.1 = (f32[32,2048]{1,0:T(8,128)S(1)}, f32[32,2048]{1,0:T(8,128)}, u32[]{:S(2)}) copy-start(f32[32,2048]{1,0:T(8,128)} %drag_ref.1) | copy-start | bytes 786436
  11.6 75.9 %collective-permute-start.14 = (f32[1,1,5,5,2,128]{5,4,3,2,1,0:T(2,128)}, f32[1,1,5,5,2,128]{5,4,3,2,1,0:T(2,128)S(1)}, u32[]{:S(2)}, u32[]{:S(2)}) collective-permute-start(f32[1,1,5,5,2,128]{5,4,3,2,1,0:T(2,128)} %copy.606), channel_id=1, source_target_pairs={{0,16},{16,32},{32,48},{48,64},{64,80},{80,96},{96,112},{1,17},{17... | collective-permute-start | bytes 76808 | tf_op jit(solution)/shard_map/ppermute | solution.py:30
  16.9 98.2 %collective-permute-start.15 = (f32[1,1,5,5,2,128]{5,4,3,2,1,0:T(2,128)}, f32[1,1,5,5,2,128]{5,4,3,2,1,0:T(2,128)}, u32[]{:S(2)}, u32[]{:S(2)}) collective-permute-start(f32[1,1,5,5,2,128]{5,4,3,2,1,0:T(2,128)} %copy.608), channel_id=1, source_target_pairs={{16,0},{32,16},{48,32},{64,48},{80,64},{96,80},{112,96},{17,1},{33... | collective-permute-start | bytes 76808 | tf_op jit(solution)/shard_map/ppermute | solution.py:33
  20.2 6.3 copy-start.21
  20.2 141.2 %collective-permute-start = (f32[8,8,2048]{2,1,0:T(8,128)}, f32[8,8,2048]{2,1,0:T(8,128)S(1)}, u32[]{:S(2)}, u32[]{:S(2)}) collective-permute-start(f32[8,8,2048]{2,1,0:T(8,128)} %get-tuple-element.526), channel_id=1, source_target_pairs={{0,16},{16,32},{32,48},{48,64},{64,80},{80,96},{96,112},{112,0},{1... | collective-permute-start | bytes 1572872 | tf_op jit(solution)/shard_map/ppermute | solution.py:361
  21.9 139.4 %collective-permute-start.1 = (f32[8,8,2048]{2,1,0:T(8,128)}, f32[8,8,2048]{2,1,0:T(8,128)S(1)}, u32[]{:S(2)}, u32[]{:S(2)}) collective-permute-start(f32[8,8,2048]{2,1,0:T(8,128)} %get-tuple-element.525), channel_id=1, source_target_pairs={{0,112},{16,0},{32,16},{48,32},{64,48},{80,64},{96,80},{112,96},{1... | collective-permute-start | bytes 1572872 | tf_op jit(solution)/shard_map/ppermute | solution.py:361
  22.6 145.3 %collective-permute-start.2 = (f32[8,32,128]{2,1,0:T(8,128)}, f32[8,32,128]{2,1,0:T(8,128)S(1)}, u32[]{:S(2)}, u32[]{:S(2)}) collective-permute-start(f32[8,32,128]{2,1,0:T(8,128)} %get-tuple-element.524), channel_id=1, source_target_pairs={{0,1},{1,2},{2,3},{3,4},{4,5},{5,6},{6,7},{7,8},{8,9},{9,10},{10,1... | collective-permute-start | bytes 393224 | tf_op jit(solution)/shard_map/ppermute | solution.py:361
  26.5 2.4 copy-start.10
  31.7 0.7 copy-start.19
  31.7 0.7 copy-start.22
  31.7 0.7 copy-start.24
  32.4 0.7 copy-start.18
  35.7 1.4 copy-start.28
  35.7 2.1 copy-start.27
  35.7 2.7 copy-start.26
  61.8 2.5 copy-start.12
  88.1 80.5 %collective-permute-start.3 = (f32[8,32,128]{2,1,0:T(8,128)S(1)}, f32[8,32,128]{2,1,0:T(8,128)S(1)}, u32[]{:S(2)}, u32[]{:S(2)}) collective-permute-start(f32[8,32,128]{2,1,0:T(8,128)S(1)} %get-tuple-element.523), channel_id=1, source_target_pairs={{0,15},{1,0},{2,1},{3,2},{4,3},{5,4},{6,5},{7,6},{8,7},{9,8},{10,9... | collective-permute-start | bytes 393224 | tf_op jit(solution)/shard_map/ppermute | solution.py:361
  147.4 8.1 %collective-permute-start.16 = (f32[1,1,5,5,2,2]{3,5,4,2,1,0:T(2,128)S(1)}, f32[1,1,5,5,2,2]{3,5,4,2,1,0:T(2,128)S(1)}, u32[]{:S(2)}, u32[]{:S(2)}) collective-permute-start(f32[1,1,5,5,2,2]{3,5,4,2,1,0:T(2,128)S(1)} %get-tuple-element.513), channel_id=1, source_target_pairs={{0,1},{1,2},{2,3},{3,4},{4,5},{5,6},{6,7},{7,8},{8,9},{9,10},{10,1... | collective-permute-start | bytes 1208 | tf_op jit(solution)/shard_map/ppermute | solution.py:30
  155.5 13.8 %copy-start.3 = (s32[32,2048]{1,0:T(8,128)S(1)}, s32[32,2048]{1,0:T(8,128)}, u32[]{:S(2)}) copy-start(s32[32,2048]{1,0:T(8,128)} %elem_ref.1) | copy-start | bytes 786436
  155.5 13.8 %copy-start.4 = (s32[32,2048]{1,0:T(8,128)S(1)}, s32[32,2048]{1,0:T(8,128)}, u32[]{:S(2)}) copy-start(s32[32,2048]{1,0:T(8,128)} %node_ref.1) | copy-start | bytes 786436
  155.5 4.5 collective-permute-start.17
  161.4 6.5 collective-permute-start.4
  161.8 6.2 collective-permute-start.5
  169.3 0.9 copy-start.6
  170.2 0.9 copy-start.8
  202.8 8.5 %copy-start.14 = (f32[3,25,4,1]{3,2,1,0:T(4,128)}, f32[3,25,4,1]{3,2,1,0:T(4,128)S(1)}, u32[]{:S(2)}) copy-start(f32[3,25,4,1]{3,2,1,0:T(4,128)S(1)} %copy.593) | copy-start | bytes 3604
  203.3 7.9 %copy-start.16 = (f32[3,25,4,1]{3,2,1,0:T(4,128)}, f32[3,25,4,1]{3,2,1,0:T(4,128)S(1)}, u32[]{:S(2)}) copy-start(f32[3,25,4,1]{3,2,1,0:T(4,128)S(1)} %copy.594) | copy-start | bytes 3604
  204.6 348.4 %collective-permute-start.6 = (f32[3,25,1,130]{3,2,1,0:T(1,128)}, f32[3,25,1,130]{3,2,1,0:T(1,128)}, u32[]{:S(2)}, u32[]{:S(2)}) collective-permute-start(f32[3,25,1,130]{3,2,1,0:T(1,128)} %get-tuple-element.543), channel_id=1, source_target_pairs={{0,16},{16,32},{32,48},{48,64},{64,80},{80,96},{96,112},{1,17},{17... | collective-permute-start | bytes 117008 | tf_op jit(solution)/shard_map/ppermute | solution.py:30
  211.3 341.7 %collective-permute-start.7 = (f32[3,25,1,130]{3,2,1,0:T(1,128)}, f32[3,25,1,130]{3,2,1,0:T(1,128)}, u32[]{:S(2)}, u32[]{:S(2)}) collective-permute-start(f32[3,25,1,130]{3,2,1,0:T(1,128)} %get-tuple-element.542), channel_id=1, source_target_pairs={{16,0},{32,16},{48,32},{64,48},{80,64},{96,80},{112,96},{17,1},{33... | collective-permute-start | bytes 117008 | tf_op jit(solution)/shard_map/ppermute | solution.py:33
  543.1 10.0 %copy-start.15 = (f32[3,25,4,1]{3,2,1,0:T(4,128)S(1)}, f32[3,25,4,1]{3,2,1,0:T(4,128)}, u32[]{:S(2)}) copy-start(f32[3,25,4,1]{3,2,1,0:T(4,128)} %copy-done.14) | copy-start | bytes 3604
  543.1 10.0 %copy-start.17 = (f32[3,25,4,1]{3,2,1,0:T(4,128)S(1)}, f32[3,25,4,1]{3,2,1,0:T(4,128)}, u32[]{:S(2)}) copy-start(f32[3,25,4,1]{3,2,1,0:T(4,128)} %copy-done.16) | copy-start | bytes 3604
  554.4 37.2 %copy-start.13 = (f32[3,5,5,5,2,2,128]{6,1,5,4,3,2,0:T(8,128)S(1)}, f32[3,5,5,5,2,2,128]{6,1,5,4,3,2,0:T(8,128)}, u32[]{:S(2)}) copy-start(f32[3,5,5,5,2,2,128]{6,1,5,4,3,2,0:T(8,128)} %pad_maximum_fusion.1) | copy-start | bytes 2304004
  554.5 8.2 %collective-permute-start.8 = (f32[3,25,6,1]{3,2,1,0:T(8,128)S(1)}, f32[3,25,6,1]{3,2,1,0:T(8,128)S(1)}, u32[]{:S(2)}, u32[]{:S(2)}) collective-permute-start(f32[3,25,6,1]{3,2,1,0:T(8,128)S(1)} %get-tuple-element.537), channel_id=1, source_target_pairs={{0,1},{1,2},{2,3},{3,4},{4,5},{5,6},{6,7},{7,8},{8,9},{9,10},{10,1... | collective-permute-start | bytes 5408 | tf_op jit(solution)/shard_map/ppermute | solution.py:30
  559.5 9.9 %collective-permute-start.9 = (f32[3,25,6,1]{3,2,1,0:T(8,128)S(1)}, f32[3,25,6,1]{3,2,1,0:T(8,128)S(1)}, u32[]{:S(2)}, u32[]{:S(2)}) collective-permute-start(f32[3,25,6,1]{3,2,1,0:T(8,128)S(1)} %get-tuple-element.536), channel_id=1, source_target_pairs={{1,0},{2,1},{3,2},{4,3},{5,4},{6,5},{7,6},{8,7},{9,8},{10,9},{11,1... | collective-permute-start | bytes 5408 | tf_op jit(solution)/shard_map/ppermute | solution.py:33
  592.1 8.4 %collective-permute-start.10 = (f32[1,3,5,5,2,128]{5,4,3,2,1,0:T(2,128)S(1)}, f32[1,3,5,5,2,128]{5,4,3,2,1,0:T(2,128)S(1)}, u32[]{:S(2)}, u32[]{:S(2)}) collective-permute-start(f32[1,3,5,5,2,128]{5,4,3,2,1,0:T(2,128)S(1)} %get-tuple-element.534), channel_id=1, source_target_pairs={{0,16},{16,32},{32,48},{48,64},{64,80},{80,96},{96,112},{1,17},{17... | collective-permute-start | bytes 230408 | tf_op jit(solution)/shard_map/ppermute | solution.py:30
  598.5 5.7 collective-permute-start.11
  605.5 40.4 %collective-permute-start.12 = (f32[1,3,5,5,2,2]{3,5,4,2,1,0:T(2,128)S(1)}, f32[1,3,5,5,2,2]{3,5,4,2,1,0:T(2,128)S(1)}, u32[]{:S(2)}, u32[]{:S(2)}) collective-permute-start(f32[1,3,5,5,2,2]{3,5,4,2,1,0:T(2,128)S(1)} %bitcast.300), channel_id=1, source_target_pairs={{0,1},{1,2},{2,3},{3,4},{4,5},{5,6},{6,7},{7,8},{8,9},{9,10},{10,1... | collective-permute-start | bytes 3608 | tf_op jit(solution)/shard_map/ppermute | solution.py:30
  644.1 27.0 %copy-start.11 = (f32[3,5,5,5,2,2,128]{6,5,4,3,2,1,0:T(2,128)S(1)}, f32[3,5,5,5,2,2,128]{6,5,4,3,2,1,0:T(2,128)}, u32[]{:S(2)}) copy-start(f32[3,5,5,5,2,2,128]{6,5,4,3,2,1,0:T(2,128)} %param.100) | copy-start | bytes 2304004
  644.6 5.2 collective-permute-start.13
  677.3 0.7 copy-start.20
  677.3 0.7 copy-start.25
  689.3 7.5 collective-permute-start.18
  694.9 5.7 collective-permute-start.19
  703.4 41.6 %collective-permute-start.20 = (f32[1,3,5,5,2,2]{3,5,4,2,1,0:T(2,128)S(1)}, f32[1,3,5,5,2,2]{3,5,4,2,1,0:T(2,128)}, u32[]{:S(2)}, u32[]{:S(2)}) collective-permute-start(f32[1,3,5,5,2,2]{3,5,4,2,1,0:T(2,128)S(1)} %bitcast.299), channel_id=1, source_target_pairs={{0,1},{1,2},{2,3},{3,4},{4,5},{5,6},{6,7},{7,8},{8,9},{9,10},{10,1... | collective-permute-start | bytes 3608 | tf_op jit(solution)/shard_map/ppermute | solution.py:30
  743.7 6.1 collective-permute-start.21
  (3 other events, 1.9 us)

commit v2 on v1

--- a/solution.py
+++ b/solution.py
@@ -20,19 +20,6 @@
 speed_floor = 0.0001
 load_factor = 4.0
 solid_dt = 0.04
-
-
-def extended(block, sides, width):
-    for axis, dim in sides:
-        count = lax.axis_size(axis)
-        forward = [(i, i + 1) for i in range(count - 1)]
-        backward = [(target, source) for source, target in forward]
-        low = lax.ppermute(
-            lax.slice_in_dim(block, block.shape[dim] - width, None, axis=dim), axis, forward
-        )
-        high = lax.ppermute(lax.slice_in_dim(block, 0, width, axis=dim), axis, backward)
-        block = jnp.concatenate([low, block, high], axis=dim)
-    return block
 
 
 def legendre_four(x):
@@ -56,10 +43,11 @@
 
 def flow_body(
     drag_ref, wet_ref, elem_ref, node_ref, flow_any,
-    xlo_ref, xhi_ref, ylo_ref, yhi_ref, corner_ref,
-    out_any, table_ref,
-    ext, drag, buoy, scale, tract, row_slot, col_slot, sems,
+    *refs,
 ):
+    got = (refs[0:5], refs[5:10], refs[10:15])
+    out_any, own_ref, beyond_ref, sides_ref = refs[15:19]
+    ext, drag, buoy, scale, tract, row_slot, col_slot, table_ref, sems = refs[19:]
     rows, cols = drag_ref.shape
     wide = cols + 128
     tall = rows + 8
@@ -84,6 +72,12 @@
         tile = jnp.where(left_half & (at_y == last_y), 0.0, tile)
         return jnp.where(jnp.logical_not(left_half) & (at_y == 0), 0.0, tile)
 
+    def received(k, n, *at):
+        if k < 6:
+            return got[0][n][(k, *at)]
+        tile = got[k - 5][n][at]
+        return tile if k == 6 else tile.astype(jnp.float32)
+
     def place(k, r, c, tile):
         if k < 6:
             ext[0, k, r, c] = tile
@@ -101,8 +95,7 @@
     def halo_rows(t, carry):
         at = pl.ds(pl.multiple_of(t * 128, 128), 128)
         for k in range(8):
-            tile = jnp.where(up_half, xhi_ref[k, :, at], xlo_ref[k, :, at])
-            place(k, foot, at, zero_rows(tile))
+            place(k, foot, at, zero_rows(received(k, 0, slice(None), at)))
         for r in range(0, rows, 8):
             scale[r : r + 8, at] = ones
         scale[foot, at] = row_scale
@@ -111,13 +104,11 @@
     lax.fori_loop(0, cols // 128, halo_rows, 0)
     for k in range(8):
         for r in range(0, rows, 8):
-            tile = jnp.where(left_half, yhi_ref[k, r : r + 8, :], ylo_ref[k, r : r + 8, :])
+            at = (slice(r, r + 8), slice(None))
+            tile = jnp.where(left_half, received(k, 2, *at), received(k, 1, *at))
             place(k, pl.ds(r, 8), tail, zero_cols(tile))
-        tile = jnp.where(
-            up_half,
-            jnp.where(left_half, corner_ref[3, k], corner_ref[2, k]),
-            jnp.where(left_half, corner_ref[1, k], corner_ref[0, k]),
-        )
+        at = (slice(None), slice(None))
+        tile = jnp.where(left_half, received(k, 4, *at), received(k, 3, *at))
         place(k, foot, tail, zero_cols(zero_rows(tile)))
     for r in range(0, rows, 8):
         scale[r : r + 8, tail] = col_scale
@@ -134,11 +125,14 @@
         lx = er - 2 * at_x + 1
         ly = (e - er * surface_cols) - 128 * at_y + 1
         inside = (ly >= 1) & (ly <= 128)
-        a = jnp.where(inside, 2 * n + (lx & 1), 50)
+        own_row = (lx == 1) | (lx == 2)
+        half = jnp.where(own_row, 0, 1)
+        line = 2 * n + jnp.where(lx >= 2, 1, 0)
+        a = jnp.where(inside, line, 50)
         b = jnp.where(
             inside,
-            (lx >> 1) * 128 + ly - 1,
-            jnp.where(ly == 0, 0, 128) + 4 * n + lx,
+            half * 128 + ly - 1,
+            jnp.where(ly == 0, 0, 128) + 64 * half + line,
         )
         row_slot[:, at] = a.astype(jnp.float32)
         col_slot[:, at] = b.astype(jnp.float32)
@@ -262,22 +256,21 @@
         return carry
 
     lax.fori_loop(0, rows, spread, 0)
+    table = [table_ref[128 * k : 128 * k + 64] + table_ref[128 * k + 64 : 128 * k + 128] for k in range(3)]
+    load_parts(table, own_ref, beyond_ref, sides_ref)
     own_out.wait()
 
 
-def flow_call(flow, drag, wet, elem, node, xlo, xhi, ylo, yhi, corner):
+def flow_call(flow, drag, wet, elem, node, halos):
     rows, cols = drag.shape
     tall, wide = rows + 8, cols + 128
     vmem = pl.BlockSpec(memory_space=pltpu.VMEM)
     hbm = pl.BlockSpec(memory_space=pl.ANY)
     return pl.pallas_call(
         flow_body,
-        out_shape=(
-            jax.ShapeDtypeStruct((6, rows, cols), jnp.float32),
-            jax.ShapeDtypeStruct((384, 256), jnp.float32),
-        ),
-        in_specs=[vmem] * 4 + [hbm] + [vmem] * 5,
-        out_specs=(hbm, vmem),
+        out_shape=(shape(6, rows, cols), shape(3, 56, 128), shape(3, 56, 128), shape(8, 128)),
+        in_specs=[vmem] * 4 + [hbm] + [vmem] * 15,
+        out_specs=(hbm, vmem, vmem, vmem),
         scratch_shapes=[
             pltpu.VMEM((2, 6, tall, wide), jnp.float32),
             pltpu.VMEM((tall, wide), jnp.float32),
@@ -286,58 +279,465 @@
             pltpu.VMEM((3, rows, cols), jnp.float32),
             pltpu.VMEM((rows, cols), jnp.float32),
             pltpu.VMEM((rows, cols), jnp.float32),
+            pltpu.VMEM((384, 256), jnp.float32),
             pltpu.SemaphoreType.DMA((2,)),
         ],
         compiler_params=pltpu.CompilerParams(vmem_limit_bytes=48 * 2**20),
-    )(drag, wet, elem, node, flow, xlo, xhi, ylo, yhi, corner)
-
-
-def weights_cube():
-    cube = (
-        gll_weights.reshape(5, 1, 1) * gll_weights.reshape(1, 5, 1) * gll_weights.reshape(1, 1, 5)
+    )(drag, wet, elem, node, flow, *halos)
+
+
+def line(matrix, s):
+    even = [s[0] + s[4], s[1] + s[3]]
+    odd = [s[0] - s[4], s[1] - s[3]]
+    out = [None] * 5
+    for a in range(2):
+        half_sum = [0.5 * (matrix[a, p] - matrix[a, 4 - p]) for p in range(2)]
+        half_diff = [0.5 * (matrix[a, p] + matrix[a, 4 - p]) for p in range(2)]
+        x = float(half_sum[0]) * odd[0] + float(half_sum[1]) * odd[1]
+        y = float(half_diff[0]) * even[0] + float(half_diff[1]) * even[1] + float(matrix[a, 2]) * s[2]
+        out[a] = x + y
+        out[4 - a] = x - y
+    out[2] = float(matrix[2, 0]) * odd[0] + float(matrix[2, 1]) * odd[1]
+    return out
+
+
+def lane_row():
+    lane = lax.broadcasted_iota(jnp.int32, (4, 128), 1)
+    row = lax.broadcasted_iota(jnp.int32, (4, 128), 0)
+    return lane, row
+
+
+def internal_local(u_ref, lame_ref, shear_ref, stress, force):
+    table = derivative_table()
+
+    def slope_x(m, carry):
+        for i in range(3):
+            lines = line(table, [u_ref[i * 125 + a * 25 + m] for a in range(5)])
+            for a in range(5):
+                stress[i * 125 + a * 25 + m] = lines[a]
+        return carry
+
+    lax.fori_loop(0, 25, slope_x, 0)
+
+    def plane(a, carry):
+        weight = jnp.where(
+            (a == 0) | (a == 4),
+            np.float32(gll_weights[0]),
+            jnp.where(a == 2, np.float32(gll_weights[2]), np.float32(gll_weights[1])),
+        )
+        lame = lame_ref[...] * -weight
+        shear = shear_ref[...] * -weight
+
+        def at(i, b, c):
+            return i * 125 + a * 25 + b * 5 + c
+
+        slope_y, slope_z = [], []
+        for i in range(3):
+            u = [[u_ref[at(i, b, c)] for c in range(5)] for b in range(5)]
+            along_y = [line(table, [u[b][c] for b in range(5)]) for c in range(5)]
+            slope_y.append([[along_y[c][b] for c in range(5)] for b in range(5)])
+            slope_z.append([line(table, u[b]) for b in range(5)])
+        pull_y = [[[None] * 5 for b in range(5)] for i in range(3)]
+        pull_z = [[[None] * 5 for b in range(5)] for i in range(3)]
+        for b in range(5):
+            for c in range(5):
+                w = np.float32(gll_weights[b] * gll_weights[c])
+                g = [[stress[at(i, b, c)], slope_y[i][b][c], slope_z[i][b][c]] for i in range(3)]
+                mu = shear * w
+                twice = mu + mu
+                spread = (lame * w) * (g[0][0] + g[1][1] + g[2][2])
+                s00 = spread + twice * g[0][0]
+                s11 = spread + twice * g[1][1]
+                s22 = spread + twice * g[2][2]
+                s01 = mu * (g[0][1] + g[1][0])
+                s02 = mu * (g[0][2] + g[2][0])
+                s12 = mu * (g[1][2] + g[2][1])
+                stress[at(0, b, c)] = s00
+                stress[at(1, b, c)] = s01
+                stress[at(2, b, c)] = s02
+                for i, (s_y, s_z) in enumerate(((s01, s02), (s11, s12), (s12, s22))):
+                    pull_y[i][b][c] = s_y
+                    pull_z[i][b][c] = s_z
+        for i in range(3):
+            along_y = [line(table.T, [pull_y[i][b][c] for b in range(5)]) for c in range(5)]
+            for b in range(5):
+                along_z = line(table.T, pull_z[i][b])
+                for c in range(5):
+                    force[at(i, b, c)] = along_y[c][b] + along_z[c]
+        return carry
+
+    lax.fori_loop(0, 5, plane, 0)
+    lane, row = lane_row()
+    low_x = row % 2 == 0
+    low_z = row < 2
+
+    def close_x(m, carry):
+        for i in range(3):
+            pulled = line(table.T, [stress[i * 125 + a * 25 + m] for a in range(5)])
+            f = [force[i * 125 + a * 25 + m] + pulled[a] for a in range(5)]
+            near = f[0] + jnp.where(low_x, 0.0, pltpu.roll(f[4], 1, 0))
+            far = f[4] + jnp.where(low_x, pltpu.roll(f[0], 3, 0), 0.0)
+            for a, value in enumerate((near, f[1], f[2], f[3], far)):
+                force[i * 125 + a * 25 + m] = value
+        return carry
+
+    lax.fori_loop(0, 25, close_x, 0)
+
+    def close_yz(ia, carry):
+        base = ia * 25
+        f = [[force[base + b * 5 + c] for c in range(5)] for b in range(5)]
+        for c in range(5):
+            near, far = f[0][c], f[4][c]
+            f[0][c] = near + jnp.where(lane == 0, 0.0, pltpu.roll(far, 1, 1))
+            f[4][c] = far + jnp.where(lane == 127, 0.0, pltpu.roll(near, 127, 1))
+        for b in range(5):
+            near, far = f[b][0], f[b][4]
+            f[b][0] = near + jnp.where(low_z, 0.0, pltpu.roll(far, 2, 0))
+            f[b][4] = far + jnp.where(low_z, pltpu.roll(near, 2, 0), 0.0)
+        for b in range(5):
+            for c in range(5):
+                if b in (0, 4) or c in (0, 4):
+                    force[base + b * 5 + c] = f[b][c]
+        return carry
+
+    lax.fori_loop(0, 15, close_yz, 0)
+
+
+def pack_faces(force, face_x, face_y):
+    lane, row = lane_row()
+    low_x = row % 2 == 0
+
+    def pack_x(m, carry):
+        for i in range(3):
+            face_x[i * 25 + m] = jnp.where(low_x, force[i * 125 + m], force[i * 125 + 100 + m])
+        return carry
+
+    lax.fori_loop(0, 25, pack_x, 0)
+    ends = [jnp.zeros((4, 128), jnp.float32)] * 2
+    for a in range(5):
+        for i in range(3):
+            for c in range(5):
+                q = a * 15 + i * 5 + c
+                n = i * 125 + a * 25 + c
+                ends[0] = jnp.where(lane == q, pltpu.roll(force[n], q, 1), ends[0])
+                ends[1] = jnp.where(lane == q, pltpu.roll(force[n + 20], q + 1, 1), ends[1])
+    face_y[0] = ends[0]
+    face_y[1] = ends[1]
+
+
+def open_edges():
+    at_x, at_y = lax.axis_index("gx"), lax.axis_index("gy")
+    has = {-1: at_x > 0, 1: at_x < lax.axis_size("gx") - 1}
+    has_y = {-1: at_y > 0, 1: at_y < lax.axis_size("gy") - 1}
+    return has, has_y
+
+
+def add_faces(force, got_x, got_y):
+    has_x, has_y = open_edges()
+    lane, row = lane_row()
+    low_x = row % 2 == 0
+
+    def add_x(m, carry):
+        for i in range(3):
+            low = jnp.where(low_x & has_x[-1], pltpu.roll(got_x[0][i * 25 + m], 3, 0), 0.0)
+            high = jnp.where(low_x | jnp.logical_not(has_x[1]), 0.0, pltpu.roll(got_x[1][i * 25 + m], 1, 0))
+            force[i * 125 + m] += low
+            force[i * 125 + 100 + m] += high
+        return carry
+
+    lax.fori_loop(0, 25, add_x, 0)
+    first, final = lane < 15, (lane >= 60) & (lane < 75)
+    columns = []
+    for side, end in ((-1, 1), (1, 0)):
+        straight = got_y[0, side][end]
+        low = pltpu.roll(pltpu.roll(got_y[-1, side][end], 68, 1), 3, 0)
+        high = pltpu.roll(pltpu.roll(got_y[1, side][end], 60, 1), 1, 0)
+        total = straight + jnp.where(first & low_x & has_x[-1], low, 0.0)
+        total = total + jnp.where(final & jnp.logical_not(low_x) & has_x[1], high, 0.0)
+        columns.append(jnp.where(has_y[side], total, 0.0))
+    for a in range(5):
+        for i in range(3):
+            for c in range(5):
+                q = a * 15 + i * 5 + c
+                n = i * 125 + a * 25 + c
+                force[n] += jnp.where(lane == 0, pltpu.roll(columns[0], (128 - q) % 128, 1), 0.0)
+                force[n + 20] += jnp.where(lane == 127, pltpu.roll(columns[1], 127 - q, 1), 0.0)
+
+
+def inverse_masses(density_ref, around, inverse):
+    has_x, has_y = open_edges()
+    lane, row = lane_row()
+    low_x = row % 2 == 0
+    low_z = row < 2
+
+    def beside(mine, left, right):
+        left = jnp.where(has_y[-1], left, 0.0)
+        right = jnp.where(has_y[1], right, 0.0)
+        before = jnp.where(lane == 0, pltpu.roll(left, 1, 1), pltpu.roll(mine, 1, 1))
+        after = jnp.where(lane == 127, pltpu.roll(right, 127, 1), pltpu.roll(mine, 127, 1))
+        return mine + before, mine, mine + after
+
+    mine = beside(density_ref[...], around[0, -1][...], around[0, 1][...])
+    low = beside(around[-1, 0][...], around[-1, -1][...], around[-1, 1][...])
+    high = beside(around[1, 0][...], around[1, -1][...], around[1, 1][...])
+    for b in range(3):
+        lo = jnp.where(has_x[-1], low[b], 0.0)
+        hi = jnp.where(has_x[1], high[b], 0.0)
+        before = mine[b] + jnp.where(low_x, pltpu.roll(lo, 3, 0), pltpu.roll(mine[b], 1, 0))
+        after = mine[b] + jnp.where(low_x, pltpu.roll(mine[b], 3, 0), pltpu.roll(hi, 1, 0))
+        for a, value in enumerate((before, mine[b], after)):
+            top = value + jnp.where(low_z, 0.0, pltpu.roll(value, 2, 0))
+            bottom = value + jnp.where(low_z, pltpu.roll(value, 2, 0), 0.0)
+            for c, total in enumerate((top, value, bottom)):
+                inverse[a * 9 + b * 3 + c] = (solid_dt * solid_dt) / total
+
+
+def kind(node):
+    return 0 if node == 0 else 2 if node == 4 else 1
+
+
+def advance_solid(force, load, inverse, now_ref, before_ref, out_ref):
+    def component(i, carry):
+        for a in range(5):
+            for b in range(5):
+                for c in range(5):
+                    n = a * 25 + b * 5 + c
+                    f = force[i * 125 + n]
+                    if c == 0:
+                        f = f + load[i * 25 + a * 5 + b]
+                    w = np.float32(1.0 / (gll_weights[a] * gll_weights[b] * gll_weights[c]))
+                    step = (inverse[kind(a) * 9 + kind(b) * 3 + kind(c)] * w) * f
+                    at = i * 125 + n
+                    out_ref[at] = (now_ref[at] + now_ref[at] - before_ref[at]) + step
+        return carry
+
+    lax.fori_loop(0, 3, component, 0)
+
+
+def load_grid():
+    row = lax.broadcasted_iota(jnp.int32, (56, 128), 0)
+    lane = lax.broadcasted_iota(jnp.int32, (56, 128), 1)
+    return row, lane
+
+
+def rows_up(x, by):
+    return jnp.concatenate([x[by:], jnp.zeros((by, 128), jnp.float32)], axis=0)
+
+
+def rows_down(x, by):
+    return jnp.concatenate([jnp.zeros((by, 128), jnp.float32), x[:-by]], axis=0)
+
+
+def masks_x():
+    row, lane = load_grid()
+    even = row % 2 == 0
+    odd = row % 2 == 1
+    return (row < 10) & even, (row < 10) & odd, (row >= 40) & (row < 50) & even, (row >= 40) & (row < 50) & odd
+
+
+def masks_y():
+    row, lane = load_grid()
+    place = row % 10
+    return (place < 2) & (row < 50), (place >= 8) & (row < 50), lane == 0, lane == 127
+
+
+def join_x(x):
+    near_even, near_odd, far_even, far_odd = masks_x()
+    return (
+        x
+        + jnp.where(near_odd, pltpu.roll(rows_up(x, 40), 1, 0), 0.0)
+        + jnp.where(far_even, pltpu.roll(rows_down(x, 40), 55, 0), 0.0)
     )
-    return jnp.asarray(cube.reshape(5, 5, 5, 1, 1, 1), jnp.float32)
-
-
-def internal_force(values, lame_first, shear_modulus):
-    highest = lax.Precision.HIGHEST
-    table = jnp.asarray(derivative_table(), jnp.float32)
-    weights_3d = weights_cube()
-    gradients = [
-        jnp.einsum("pa,iabczxy->ipbczxy", table, values, precision=highest),
-        jnp.einsum("pb,iabczxy->iapczxy", table, values, precision=highest),
-        jnp.einsum("pc,iabczxy->iabpzxy", table, values, precision=highest),
-    ]
-    divergence = gradients[0][0] + gradients[1][1] + gradients[2][2]
-    forces = []
-    for i in range(3):
-        weighted = []
-        for j in range(3):
-            stress = shear_modulus * (gradients[j][i] + gradients[i][j])
-            if i == j:
-                stress = stress + lame_first * divergence
-            weighted.append(weights_3d * stress)
-        pulled = jnp.einsum("pa,pbczxy->abczxy", table, weighted[0], precision=highest)
-        pulled = pulled + jnp.einsum("pb,apczxy->abczxy", table, weighted[1], precision=highest)
-        pulled = pulled + jnp.einsum("pc,abpzxy->abczxy", table, weighted[2], precision=highest)
-        forces.append(-pulled)
-    return jnp.stack(forces)
-
-
-def assemble(values):
-    boundary = jnp.stack([values[:, 0, :, :, :, 0, :], values[:, 4, :, :, :, -1, :]])
-    summed = values[:, 4, :, :, :, :-1, :] + values[:, 0, :, :, :, 1:, :]
-    values = values.at[:, 4, :, :, :, :-1, :].set(summed).at[:, 0, :, :, :, 1:, :].set(summed)
-    beyond = extended(boundary, (("gx", 0),), 1)
-    values = values.at[:, 0, :, :, :, 0, :].add(beyond[0]).at[:, 4, :, :, :, -1, :].add(beyond[3])
-    boundary = jnp.stack([values[:, :, 0, :, :, :, 0], values[:, :, 4, :, :, :, -1]])
-    summed = values[:, :, 4, :, :, :, :-1] + values[:, :, 0, :, :, :, 1:]
-    values = values.at[:, :, 4, :, :, :, :-1].set(summed).at[:, :, 0, :, :, :, 1:].set(summed)
-    beyond = extended(boundary, (("gy", 0),), 1)
-    values = values.at[:, :, 0, :, :, :, 0].add(beyond[0]).at[:, :, 4, :, :, :, -1].add(beyond[3])
-    summed = values[:, :, :, 4, :-1] + values[:, :, :, 0, 1:]
-    values = values.at[:, :, :, 4, :-1].set(summed).at[:, :, :, 0, 1:].set(summed)
-    return values
+
+
+def join_x_wide(own, halo):
+    near_even, near_odd, far_even, far_odd = masks_x()
+    own_new = join_x(own)
+    own_new = own_new + jnp.where(near_even, rows_up(halo, 40), 0.0)
+    own_new = own_new + jnp.where(far_odd, rows_down(halo, 40), 0.0)
+    halo_new = halo + jnp.where(far_even, rows_down(own, 40), 0.0)
+    halo_new = halo_new + jnp.where(near_odd, rows_up(own, 40), 0.0)
+    return own_new, halo_new
+
+
+def join_y(x, sides):
+    near, far, first, final = masks_y()
+    before, after = pltpu.roll(x, 1, 1), pltpu.roll(x, 127, 1)
+    fill_before = 0.0 if sides is None else pltpu.roll(sides, 1, 1)
+    fill_after = 0.0 if sides is None else pltpu.roll(sides, 127, 1)
+    out = x + jnp.where(near, rows_up(jnp.where(first, fill_before, before), 8), 0.0)
+    out = out + jnp.where(far, rows_down(jnp.where(final, fill_after, after), 8), 0.0)
+    if sides is None:
+        return out
+    new = sides + jnp.where(far & final, rows_down(after, 8), 0.0)
+    new = new + jnp.where(near & first, rows_up(before, 8), 0.0)
+    return out, new
+
+
+def columns_from(tile):
+    row, lane = load_grid()
+    turned = jnp.concatenate([tile, jnp.zeros((120, 128), jnp.float32)], axis=0).T
+    out = []
+    for k in range(3):
+        halves = []
+        for h in range(2):
+            part = turned[64 * h : 64 * h + 56]
+            left = pltpu.roll(part, 127 - 2 * k, 1)
+            right = pltpu.roll(part, (128 - 2 * k - 1) % 128, 1)
+            value = jnp.where(lane == 127, left, jnp.where(lane == 0, right, 0.0))
+            halves.append(jnp.where(row < 50, value, 0.0))
+        out.append(halves)
+    return out
+
+
+def columns_to(columns):
+    lane = lax.broadcasted_iota(jnp.int32, (128, 128), 1)
+    total = jnp.zeros((128, 128), jnp.float32)
+    for k in range(3):
+        pad = jnp.zeros((8, 128), jnp.float32)
+        x = jnp.concatenate([columns[k][0], pad, columns[k][1], pad], axis=0)
+        total = jnp.where(lane == 2 * k, pltpu.roll(x, 2 * k + 1, 1), total)
+        total = jnp.where(lane == 2 * k + 1, pltpu.roll(x, 2 * k + 1, 1), total)
+    return total.T[:8]
+
+
+def load_parts(table, own_ref, beyond_ref, sides_ref):
+    row, lane = load_grid()
+    line_of = lax.broadcasted_iota(jnp.int32, (8, 128), 0)
+    raw = jnp.zeros((8, 128), jnp.float32)
+    for k in range(3):
+        for side in range(2):
+            last = jnp.broadcast_to(table[k][50:51, 128 * side : 128 * side + 128], (8, 128))
+            raw = jnp.where(line_of == 2 * k + side, last, raw)
+    columns = columns_from(raw)
+    new_columns = []
+    for k in range(3):
+        own = jnp.where(row < 50, table[k][:56, :128], 0.0)
+        halo = jnp.where(row < 50, table[k][:56, 128:], 0.0)
+        own, halo = join_x_wide(own, halo)
+        sides = join_x_wide(columns[k][0], columns[k][1])
+        own, side_own = join_y(own, sides[0])
+        halo, side_halo = join_y(halo, sides[1])
+        own_ref[k] = own
+        beyond_ref[k] = halo
+        new_columns.append((side_own, side_halo))
+    sides_ref[...] = columns_to(new_columns)
+
+
+def load_total(own_ref, got_x, got_y, load):
+    has_x, has_y = open_edges()
+    row, lane = load_grid()
+    even = row % 2 == 0
+    tile_lane = lax.broadcasted_iota(jnp.int32, (8, 128), 1)
+    tile_row = lax.broadcasted_iota(jnp.int32, (8, 128), 0)
+    ends = []
+    for side in (-1, 1):
+        low = jnp.where(has_x[-1], pltpu.roll(got_y[-1, side][...], 127, 1), 0.0)
+        high = jnp.where(has_x[1], pltpu.roll(got_y[1, side][...], 1, 1), 0.0)
+        tile = jnp.where(tile_lane < 64, got_y[0, side][...], jnp.where(tile_lane % 2 == 0, low, high))
+        ends.append(jnp.where(has_y[side], tile, 0.0))
+    columns = columns_from(jnp.where(tile_row % 2 == 0, ends[1], ends[0]))
+    for k in range(3):
+        low = jnp.where(has_x[-1], pltpu.roll(got_x[0][k], 55, 0), 0.0)
+        high = jnp.where(has_x[1], pltpu.roll(got_x[1][k], 1, 0), 0.0)
+        rows = jnp.where(even, low, high) + join_y(columns[k][1], None)
+        total = own_ref[k] + join_x(jnp.where(row < 50, rows, 0.0)) + join_y(columns[k][0], None)
+        for n in range(25):
+            load[k * 25 + n] = jnp.concatenate(
+                [total[2 * n : 2 * n + 2], jnp.zeros((2, 128), jnp.float32)], axis=0
+            )
+
+
+AROUND = [(-1, 0), (1, 0), (0, -1), (0, 1), (-1, -1), (-1, 1), (1, -1), (1, 1)]
+ASIDE = AROUND[2:]
+
+
+def swap(collective_id, operands, outs, messages):
+    count = len(messages)
+
+    def body(*refs):
+        ins, out_refs = refs[: len(operands)], refs[len(operands) : len(operands) + len(outs)]
+        sent, come = refs[len(operands) + len(outs) :]
+        at_x, at_y = lax.axis_index("gx"), lax.axis_index("gy")
+        size_x, size_y = lax.axis_size("gx"), lax.axis_size("gy")
+
+        def device(move):
+            return ((at_x + move[0] + size_x) % size_x, (at_y + move[1] + size_y) % size_y)
+
+        barrier = pltpu.get_barrier_semaphore()
+        for move in AROUND:
+            pl.semaphore_signal(barrier, inc=1, device_id=device(move), device_id_type=pl.DeviceIdType.MESH)
+        pl.semaphore_wait(barrier, len(AROUND))
+        copies = []
+        for n, (source, source_index, target, target_index, move) in enumerate(messages):
+            copies.append(
+                pltpu.make_async_remote_copy(
+                    src_ref=ins[source].at[source_index] if source_index is not None else ins[source],
+                    dst_ref=out_refs[target].at[target_index] if target_index is not None else out_refs[target],
+                    send_sem=sent.at[n],
+                    recv_sem=come.at[n],
+                    device_id=device(move),
+                    device_id_type=pl.DeviceIdType.MESH,
+                )
+            )
+            copies[-1].start()
+        for copy in copies:
+            copy.wait()
+
+    return pl.pallas_call(
+        body,
+        out_shape=tuple(outs),
+        in_specs=[pl.BlockSpec(memory_space=pl.ANY)] * len(operands),
+        out_specs=tuple([pl.BlockSpec(memory_space=pl.ANY)] * len(outs)),
+        scratch_shapes=[pltpu.SemaphoreType.DMA((count,)), pltpu.SemaphoreType.DMA((count,))],
+        compiler_params=pltpu.CompilerParams(collective_id=collective_id, has_side_effects=True),
+    )(*operands)
+
+
+def shape(*dims, kind=jnp.float32):
+    return jax.ShapeDtypeStruct(dims, kind)
+
+
+def local(body, operands, outs, scratch):
+    vmem = pl.BlockSpec(memory_space=pltpu.VMEM)
+    return pl.pallas_call(
+        body,
+        out_shape=tuple(outs),
+        in_specs=[vmem] * len(operands),
+        out_specs=tuple([vmem] * len(outs)),
+        scratch_shapes=[pltpu.VMEM(dims, jnp.float32) for dims in scratch],
+        compiler_params=pltpu.CompilerParams(vmem_limit_bytes=48 * 2**20),
+    )(*operands)
+
+
+def first_body(u_ref, lame_ref, shear_ref, density_ref, *refs):
+    around = {move: refs[n] for n, move in enumerate(AROUND)}
+    force, face_x, face_y, inverse, stress = refs[8:]
+    inverse_masses(density_ref, around, inverse)
+    internal_local(u_ref, lame_ref, shear_ref, stress, force)
+    pack_faces(force, face_x, face_y)
+
+
+def middle_body(force0, u_ref, before_ref, lame_ref, shear_ref, inverse, own_ref, *refs):
+    face_got_x, load_got_x = refs[0:2], refs[2:4]
+    face_got_y = {move: refs[4 + n] for n, move in enumerate(ASIDE)}
+    load_got_y = {move: refs[10 + n] for n, move in enumerate(ASIDE)}
+    u_next, force, face_x, face_y, load, stress = refs[16:]
+    load_total(own_ref, load_got_x, load_got_y, load)
+    force[...] = force0[...]
+    add_faces(force, face_got_x, face_got_y)
+    advance_solid(force, load, inverse, u_ref, before_ref, u_next)
+    internal_local(u_next, lame_ref, shear_ref, stress, force)
+    pack_faces(force, face_x, face_y)
+
+
+def last_body(force1, u_ref, before_ref, inverse, load, *refs):
+    face_got_x = refs[0:2]
+    face_got_y = {move: refs[2 + n] for n, move in enumerate(ASIDE)}
+    u_next, force = refs[8:]
+    force[...] = force1[...]
+    add_faces(force, face_got_x, face_got_y)
+    advance_solid(force, load, inverse, u_ref, before_ref, u_next)
 
 
 def per_device(
@@ -352,51 +752,78 @@
     lame_first,
     shear_modulus,
 ):
-    stacked = jnp.concatenate(
-        [flow_state, drag_coefficient[None], wet_mask.astype(jnp.float32)[None]], axis=0
+    rows, cols = drag_coefficient.shape
+    u = displacement.reshape(375, 4, 128)
+    before = previous.reshape(375, 4, 128)
+    density, lame, shear = (x.reshape(4, 128) for x in (density, lame_first, shear_modulus))
+    edge_rows = {-1: pl.ds(0, 4), 1: pl.ds(rows - 4, 4)}
+    edge_cols = {-1: pl.ds(0, 128), 1: pl.ds(cols - 128, 128)}
+    place_rows = {-1: pl.ds(0, 4), 1: pl.ds(4, 4)}
+    outs, messages = [], []
+    for source, lead in ((0, (6,)), (1, ()), (2, ())):
+        kind_of = jnp.int32 if source == 2 else jnp.float32
+        every = (slice(None),) * len(lead)
+        base = len(outs)
+        outs += [shape(*lead, 8, cols, kind=kind_of)]
+        outs += [shape(*lead, rows, 128, kind=kind_of)] * 2
+        outs += [shape(*lead, 8, 128, kind=kind_of)] * 2
+        for dx, dy in AROUND:
+            row_in = edge_rows.get(dx, pl.ds(0, rows))
+            row_out = place_rows.get(dx, pl.ds(0, rows))
+            col_in = edge_cols.get(dy, pl.ds(0, cols))
+            where = 0 if dy == 0 else (1 if dx == 0 else 3) + (0 if dy == 1 else 1)
+            messages.append(
+                (source, every + (row_in, col_in), base + where,
+                 every + (row_out, pl.ds(0, cols if dy == 0 else 128)), (dx, dy))
+            )
+    base = len(outs)
+    outs += [shape(4, 128)] * 8
+    for n, (dx, dy) in enumerate(AROUND):
+        messages.append((3, None, base + AROUND.index((-dx, -dy)), None, (dx, dy)))
+    got = swap(1, [flow_state, drag_coefficient, wet_mask, density], outs, messages)
+
+    full = (375, 4, 128)
+    force, face_x, face_y, inverse = local(
+        first_body,
+        [u, lame, shear, density, *got[15:]],
+        [shape(*full), shape(75, 4, 128), shape(2, 4, 128), shape(27, 4, 128)],
+        [full],
     )
-    ring_x, ring_y = lax.axis_size("gx"), lax.axis_size("gy")
-
-    def moved(x, axis, count, by):
-        return lax.ppermute(x, axis, [(i, (i + by) % count) for i in range(count)])
-
-    x_lo = moved(stacked[:, -8:, :], "gx", ring_x, 1)
-    x_hi = moved(stacked[:, :8, :], "gx", ring_x, -1)
-    y_lo = moved(stacked[:, :, -128:], "gy", ring_y, 1)
-    y_hi = moved(stacked[:, :, :128], "gy", ring_y, -1)
-    corner_lo = moved(jnp.stack([x_lo[:, :, -128:], x_hi[:, :, -128:]]), "gy", ring_y, 1)
-    corner_hi = moved(jnp.stack([x_lo[:, :, :128], x_hi[:, :, :128]]), "gy", ring_y, -1)
-    corner = jnp.stack([corner_lo[0], corner_hi[0], corner_lo[1], corner_hi[1]])
-    fields, slots = flow_call(
-        flow_state, drag_coefficient, wet_mask, target_elem, target_node,
-        x_lo, x_hi, y_lo, y_hi, corner,
+    fields, own, beyond, sides = flow_call(
+        flow_state, drag_coefficient, wet_mask, target_elem, target_node, got[:15]
     )
-    block_rows = displacement.shape[5]
-    slots = slots.reshape(3, 2, 64, 256).sum(axis=1)
-    middle = slots[:, :50].reshape(3, 25, 2, 2, 128).transpose(0, 1, 3, 2, 4).reshape(3, 25, 4, 128)
-    sides = slots[:, 50].reshape(3, 2, 128)[:, :, :100].reshape(3, 2, 25, 4)
-    load_table = jnp.concatenate([sides[:, 0, :, :, None], middle, sides[:, 1, :, :, None]], axis=3)
-    beyond = extended(load_table, (("gx", 2), ("gy", 3)), 1)
-    own_loads = load_table[:, :, 1:-1, 1:-1]
-    own_loads = own_loads.at[:, :, 0, :].add(beyond[:, :, 0, 2:-2])
-    own_loads = own_loads.at[:, :, -1, :].add(beyond[:, :, -1, 2:-2])
-    own_loads = own_loads.at[:, :, :, 0].add(beyond[:, :, 2:-2, 0])
-    own_loads = own_loads.at[:, :, :, -1].add(beyond[:, :, 2:-2, -1])
-    own_loads = own_loads.at[:, :, 0, 0].add(beyond[:, :, 0, 0])
-    own_loads = own_loads.at[:, :, 0, -1].add(beyond[:, :, 0, -1])
-    own_loads = own_loads.at[:, :, -1, 0].add(beyond[:, :, -1, 0])
-    own_loads = own_loads.at[:, :, -1, -1].add(beyond[:, :, -1, -1])
-    surface_load = own_loads.reshape(3, 5, 5, block_rows, displacement.shape[6])
-    masses = assemble(density[None, None, None, None] * weights_cube()[None])
-    current = displacement
-    for counter in range(SOLID_STEPS):
-        force = internal_force(current, lame_first, shear_modulus)
-        force = force.at[:, :, :, 0, 0].add(surface_load)
-        acceleration = assemble(force) / masses
-        advanced = 2.0 * current - previous + solid_dt * solid_dt * acceleration
-        previous = current
-        current = advanced
-    return (fields, current, previous)
+    faces = [shape(75, 4, 128)] * 2
+    face_messages = [(0, None, 1, None, (-1, 0)), (0, None, 0, None, (1, 0))]
+    sent_loads = [(2, None, 3, None, (-1, 0)), (2, None, 2, None, (1, 0))]
+    side_messages = [
+        (1, None, 4 + ASIDE.index((-dx, -dy)), None, (dx, dy)) for dx, dy in ASIDE
+    ] + [(3, None, 10 + ASIDE.index((-dx, -dy)), None, (dx, dy)) for dx, dy in ASIDE]
+    got = swap(
+        2,
+        [face_x, face_y, beyond, sides],
+        faces + [shape(3, 56, 128)] * 2 + [shape(2, 4, 128)] * 6 + [shape(8, 128)] * 6,
+        face_messages + sent_loads + side_messages,
+    )
+    u_one, force, face_x, face_y, load = local(
+        middle_body,
+        [force, u, before, lame, shear, inverse, own, *got],
+        [shape(*full), shape(*full), shape(75, 4, 128), shape(2, 4, 128), shape(75, 4, 128)],
+        [full],
+    )
+    got = swap(
+        3,
+        [face_x, face_y],
+        faces + [shape(2, 4, 128)] * 6,
+        face_messages
+        + [(1, None, 2 + ASIDE.index((-dx, -dy)), None, (dx, dy)) for dx, dy in ASIDE],
+    )
+    (u_two,) = local(
+        last_body,
+        [force, u_one, u, inverse, load, *got],
+        [shape(*full)],
+        [full],
+    )
+    return (fields, u_two.reshape(displacement.shape), u_one.reshape(displacement.shape))
 
 
 def solution(mesh):

time: 787 us -> 119 us (0.15); the launches traced: 773 us -> 116 us
  local copies, waits for them, and re-layouts: 583 us -> 35.2 us
  other arithmetic: 59.7 us -> 0 us
  starting transfers between devices: 56.7 us -> 0 us
  Pallas kernels: 30.7 us -> 80 us
  matrix products: 22.4 us -> 0 us
  waiting for transfers between devices: 18.8 us -> 0 us
    scatter x15 -> x0, local copies, waits for them, and re-layouts: 448 us -> none  [the longest x7 345 us: assemble(): values.at[:, :, :, 4, :-1].set(summed).at[:, :, :, 0, 1:].set(summed)]
    scatter-add x16 -> x0, local copies, waits for them, and re-layouts: 92.5 us -> none  [the longest x2 35.1 us: assemble(): values.at[:, 0, :, :, :, 0, :].add(beyond[0]).at[:, 4, :, :, :, -1, :]]
    ppermute x22 -> x0, starting transfers between devices: 56.7 us -> none  [the longest x8 30.8 us: extended(): lax.ppermute(lax.slice_in_dim(block, block.shape[dim] - width, None, axis...]
    pallas_call x1 -> x7, Pallas kernels: 30.7 us -> 80 us  [the longest x3 36.2 us: swap(): pl.pallas_call(body, out_shape=tuple(outs), in_specs=[pl.BlockSpec(memory...]
    dot_general x24 -> x0, matrix products: 22.4 us -> none  [the longest x6 6.69 us: internal_force(): jnp.einsum('pa,pbczxy->abczxy', table, weighted[0], precision=highest)]
    add x23 -> x0, other arithmetic: 22.2 us -> none  [the longest x3 6.61 us: assemble(): summed = values[:, :, :, 4, :-1] + values[:, :, :, 0, 1:]]
    ppermute x22 -> x0, waiting for transfers between devices: 18.8 us -> none  [the longest x8 15.2 us: extended(): lax.ppermute(lax.slice_in_dim(block, 0, width, axis=dim), axis, backward)]
    unnamed x65 -> x128, local copies, waits for them, and re-layouts: 18 us -> 35.2 us
  transfers between devices with their start and end apart: 22 -> 0, of which waited for: 6 -> 0; matrix products, arithmetic and copies ran while one was open for 72% -> 0% of each run, Pallas kernels for 0% -> 0%
where the time goes in v2:
time: 119 us; the launch traced here: 116 us
  Pallas kernels  80 us (67%)
  local copies, waits for them, and re-layouts  35.2 us (30%)
    pallas_call x3, Pallas kernels, swap(): pl.pallas_call(body, out_shape=tuple(outs), in_specs=[pl.BlockSpec(memory...  36.2 us
    unnamed x128, local copies, waits for them, and re-layouts  35.2 us
    pallas_call x1, Pallas kernels, flow_call(): pl.pallas_call(flow_body, out_shape=(shape(6, rows, cols), shape(3, 56, 1...  31.3 us
    pallas_call x3, Pallas kernels, local(): pl.pallas_call(body, out_shape=tuple(outs), in_specs=[vmem] * len(operand...  12.5 us

profile of v2, /device:TPU:1, one launch (start us, length us, event | category | flops | bytes accessed | tf_op | source)
XLA Modules:
  0.0 116.2 jit_solution(4303499350157813888)
XLA Ops:
  0.7 14.9 %shard_map.121 = (f32[6,8,2048]{2,1,0:T(8,128)}, f32[6,32,128]{2,1,0:T(8,128)}, f32[6,32,128]{2,1,0:T(8,128)}, f32[6,8,128]{2,1,0:T(8,128)}, f32[6,8,128]{2,1,0:...) custom-call(f32[6,32,2048]{2,1,0:T(8,128)} %flow_any.1, ...), custom_call_target="tpu_custom_call" | custom-call | tf_op jit(solution)/shard_map/pallas_call | solution.py:687
  15.6 1.0 copy-done.6
  16.6 0.9 copy-done.7
  17.5 0.9 copy-done.8
  18.5 0.9 copy-done.15
  19.4 0.9 copy-done.16
  20.2 0.8 copy-done.20
  21.1 0.8 copy-done.21
  21.9 0.7 copy-done.22
  22.7 0.7 copy-done.23
  23.4 0.7 copy-done.24
  24.1 0.7 copy-done.25
  24.8 0.7 copy-done.26
  25.6 0.7 copy-done.27
  26.3 0.7 copy-done.33
  26.9 0.7 copy-done.34
  27.6 0.7 copy-done.35
  28.3 0.7 copy-done.36
  29.1 31.3 %shard_map.122 = (f32[6,32,2048]{2,1,0:T(8,128)}, f32[3,56,128]{2,1,0:T(8,128)S(1)}, f32[3,56,128]{2,1,0:T(8,128)S(1)}, f32[8,128]{1,0:T(8,128)S(1)}) custom-call(f32[32,2048]{1,0:T(8,128)S(1)} %copy-done.2, s32[32,2048]{1,0:T(8,128)S(1)} %copy-done.3, s32[32,2048]{1,0:T(8,128)S(1)} %copy-done.7, s32[32,2048]{1,0:T(8,128)S(1)} %copy-done.8, ...), custom_call_target="tpu_custom_call" | custom-call | tf_op jit(solution)/shard_map/pallas_call | solution.py:269
  61.1 4.3 %shard_map.123 = (f32[375,4,128]{2,1,0:T(4,128)S(1)}, f32[75,4,128]{2,1,0:T(4,128)S(1)}, f32[2,4,128]{2,1,0:T(4,128)S(1)}, f32[27,4,128]{2,1,0:T(4,128)S(1)}) custom-call(f32[375,4,128]{2,1,0:T(4,128)S(1)} %bitcast.7, f32[4,128]{1,0:T(4,128)S(1)} %bitcast.14, f32[4,128]{1,0:T(4,128)S(1)} %bitcast.16, f32[4,128]{1,0:T(4,128)S(1)} %bitcast.13, ...), custom_call_target="tpu_custom_call" | custom-call | tf_op jit(solution)/shard_map/pallas_call | solution.py:703
  66.6 10.6 %shard_map.124 = (f32[75,4,128]{2,1,0:T(4,128)}, f32[75,4,128]{2,1,0:T(4,128)}, f32[3,56,128]{2,1,0:T(8,128)}, f32[3,56,128]{2,1,0:T(8,128)}, f32[2,4,128]{2,1,0...) custom-call(f32[75,4,128]{2,1,0:T(4,128)} %copy-done.12, ...), custom_call_target="tpu_custom_call" | custom-call | tf_op jit(solution)/shard_map/pallas_call | solution.py:687
  77.2 0.9 copy-done.13
  78.2 0.9 copy-done.14
  79.1 0.9 copy-done.17
  80.0 0.9 copy-done.18
  80.8 0.7 copy-done.37
  81.5 0.7 copy-done.38
  82.2 0.7 copy-done.39
  82.9 0.7 copy-done.40
  83.5 0.7 copy-done.41
  84.9 0.7 copy-done.43
  85.6 0.7 copy-done.44
  86.3 0.7 copy-done.45
  86.9 0.7 copy-done.46
  87.6 0.7 copy-done.47
  88.3 0.7 copy-done.48
  89.0 6.3 %shard_map.125 = (f32[375,4,128]{2,1,0:T(4,128)}, f32[375,4,128]{2,1,0:T(4,128)S(1)}, f32[75,4,128]{2,1,0:T(4,128)S(1)}, f32[2,4,128]{2,1,0:T(4,128)S(1)}, f32[75,4,128]{2,1,0:T(4,128)S(1)}) custom-call(f32[375,4,128]{2,1,0:T(4,128)S(1)} %get-tuple-element.87.force0, f32[375,4,128]{2,1,0:T(4,128)S(1)} %bitcast.8, f32[375,4,128]{2,1,0:T(4,128)S(1)} %bitcast.11, ...), custom_call_target="tpu_custom_call" | custom-call | tf_op jit(solution)/shard_map/pallas_call | solution.py:703
  96.6 10.7 %shard_map.126 = (f32[75,4,128]{2,1,0:T(4,128)}, f32[75,4,128]{2,1,0:T(4,128)}, f32[2,4,128]{2,1,0:T(4,128)}, f32[2,4,128]{2,1,0:T(4,128)}, f32[2,4,128]{2,1,0:T...) custom-call(f32[75,4,128]{2,1,0:T(4,128)} %copy-done.11, f32[2,4,128]{2,1,0:T(4,128)} %copy-done.55), custom_call_target="tpu_custom_call" | custom-call | tf_op jit(solution)/shard_map/pallas_call | solution.py:687
  107.3 1.1 copy-done.4
  108.4 0.9 copy-done.9
  109.3 0.9 copy-done.10
  110.3 0.7 copy-done.49
  110.9 0.7 copy-done.50
  111.6 0.7 copy-done.51
  112.3 0.7 copy-done.52
  113.0 0.7 copy-done.53
  113.6 0.7 copy-done.54
  114.3 1.9 %shard_map.127 = f32[375,4,128]{2,1,0:T(4,128)} custom-call(f32[375,4,128]{2,1,0:T(4,128)S(1)} %get-tuple-element.110.force1, f32[375,4,128]{2,1,0:T(4,128)S(1)} %copy-done.4, f32[375,4,128]{2,1,0:T(4,128)S(1)} %bitcast.9, f32[27,4,128]{2,1,0:T(4,128)S(1)} %get-tuple-element.88.inverse, f32[75,4,128]{2,1,0:T(4,128)S(1)} %get-tuple-element.112.load, ...), custom_call_target="tpu_custom_call" | custom-call | tf_op jit(solution)/shard_map/pallas_call | solution.py:703
  (87 shorter events, 3.9 us)
Async XLA Ops:
  0.6 14.9 %copy-start.3 = (s32[32,2048]{1,0:T(8,128)S(1)}, s32[32,2048]{1,0:T(8,128)}, u32[]{:S(2)}) copy-start(s32[32,2048]{1,0:T(8,128)} %wet_ref.1) | copy-start | bytes 786436
  0.6 14.9 %copy-start.2 = (f32[32,2048]{1,0:T(8,128)S(1)}, f32[32,2048]{1,0:T(8,128)}, u32[]{:S(2)}) copy-start(f32[32,2048]{1,0:T(8,128)} %drag_ref.1) | copy-start | bytes 786436
  0.7 14.9 %copy-start.1 = (f32[6,32,2048]{2,1,0:T(8,128)S(1)}, f32[6,32,2048]{2,1,0:T(8,128)}, u32[]{:S(2)}) copy-start(f32[6,32,2048]{2,1,0:T(8,128)} %flow_any.1) | copy-start | bytes 4718596
  15.6 1.0 copy-start.6
  16.6 0.9 copy-start.7
  17.5 0.9 copy-start.8
  18.5 0.9 copy-start.15
  19.4 0.9 copy-start.16
  20.2 0.8 copy-start.20
  21.1 0.8 copy-start.21
  21.9 0.7 copy-start.22
  22.7 0.7 copy-start.23
  23.4 0.7 copy-start.24
  24.1 0.7 copy-start.25
  24.8 0.7 copy-start.26
  25.6 0.7 copy-start.27
  28.3 0.7 copy-start.36
  29.0 32.0 %copy-start = (f32[3,5,5,5,2,2,128]{6,5,4,3,2,1,0:T(2,128)S(1)}, f32[3,5,5,5,2,2,128]{6,5,4,3,2,1,0:T(2,128)}, u32[]{:S(2)}) copy-start(f32[3,5,5,5,2,2,128]{6,5,4,3,2,1,0:T(2,128)} %param.15) | copy-start | bytes 2304004
  29.0 32.0 %copy-start.28 = (f32[2,2,128]{2,1,0:T(2,128)S(1)}, f32[2,2,128]{2,1,0:T(2,128)}, u32[]{:S(2)}) copy-start(f32[2,2,128]{2,1,0:T(2,128)} %param.17) | copy-start | bytes 6148
  29.0 32.0 %copy-start.29 = (f32[2,2,128]{2,1,0:T(2,128)S(1)}, f32[2,2,128]{2,1,0:T(2,128)}, u32[]{:S(2)}) copy-start(f32[2,2,128]{2,1,0:T(2,128)} %param.18) | copy-start | bytes 6148
  29.0 32.0 %copy-start.30 = (f32[2,2,128]{2,1,0:T(2,128)S(1)}, f32[2,2,128]{2,1,0:T(2,128)}, u32[]{:S(2)}) copy-start(f32[2,2,128]{2,1,0:T(2,128)} %param.19) | copy-start | bytes 6148
  29.0 32.0 %copy-start.56 = (f32[4,128]{1,0:T(4,128)S(1)}, f32[4,128]{1,0:T(4,128)}, u32[]{:S(2)}) copy-start(f32[4,128]{1,0:T(4,128)} %get-tuple-element.79.refs_0_) | copy-start | bytes 6148
  29.0 32.0 %copy-start.57 = (f32[4,128]{1,0:T(4,128)S(1)}, f32[4,128]{1,0:T(4,128)}, u32[]{:S(2)}) copy-start(f32[4,128]{1,0:T(4,128)} %get-tuple-element.80.refs_1_) | copy-start | bytes 6148
  29.0 32.0 %copy-start.58 = (f32[4,128]{1,0:T(4,128)S(1)}, f32[4,128]{1,0:T(4,128)}, u32[]{:S(2)}) copy-start(f32[4,128]{1,0:T(4,128)} %get-tuple-element.81.refs_2_) | copy-start | bytes 6148
  29.0 32.0 %copy-start.59 = (f32[4,128]{1,0:T(4,128)S(1)}, f32[4,128]{1,0:T(4,128)}, u32[]{:S(2)}) copy-start(f32[4,128]{1,0:T(4,128)} %get-tuple-element.82.refs_3_) | copy-start | bytes 6148
  29.0 32.0 %copy-start.60 = (f32[4,128]{1,0:T(4,128)S(1)}, f32[4,128]{1,0:T(4,128)}, u32[]{:S(2)}) copy-start(f32[4,128]{1,0:T(4,128)} %get-tuple-element.83.refs_4_) | copy-start | bytes 6148
  29.0 32.0 %copy-start.61 = (f32[4,128]{1,0:T(4,128)S(1)}, f32[4,128]{1,0:T(4,128)}, u32[]{:S(2)}) copy-start(f32[4,128]{1,0:T(4,128)} %get-tuple-element.84.refs_5_) | copy-start | bytes 6148
  29.0 32.0 %copy-start.62 = (f32[4,128]{1,0:T(4,128)S(1)}, f32[4,128]{1,0:T(4,128)}, u32[]{:S(2)}) copy-start(f32[4,128]{1,0:T(4,128)} %get-tuple-element.85.refs_6_) | copy-start | bytes 6148
  29.0 32.0 %copy-start.63 = (f32[4,128]{1,0:T(4,128)S(1)}, f32[4,128]{1,0:T(4,128)}, u32[]{:S(2)}) copy-start(f32[4,128]{1,0:T(4,128)} %get-tuple-element.86.refs_7_) | copy-start | bytes 6148
  61.0 4.4 %copy-start.19 = (f32[3,56,128]{2,1,0:T(8,128)}, f32[3,56,128]{2,1,0:T(8,128)S(1)}, u32[]{:S(2)}) copy-start(f32[3,56,128]{2,1,0:T(8,128)S(1)} %get-tuple-element.92.refs_2_) | copy-start | bytes 258052
  61.0 16.2 %copy-start.5 = (f32[3,5,5,5,2,2,128]{6,5,4,3,2,1,0:T(2,128)S(1)}, f32[3,5,5,5,2,2,128]{6,5,4,3,2,1,0:T(2,128)}, u32[]{:S(2)}) copy-start(f32[3,5,5,5,2,2,128]{6,5,4,3,2,1,0:T(2,128)} %param.16) | copy-start | bytes 2304004
  77.2 0.9 copy-start.13
  78.2 0.9 copy-start.14
  79.1 0.9 copy-start.17
  80.0 0.9 copy-start.18
  80.8 0.7 copy-start.37
  81.5 0.7 copy-start.38
  82.2 0.7 copy-start.39
  83.5 0.7 copy-start.41
  84.9 0.7 copy-start.43
  85.6 0.7 copy-start.44
  86.3 0.7 copy-start.45
  87.6 0.7 copy-start.47
  107.3 1.1 copy-start.4
  108.4 0.9 copy-start.9
  109.3 0.9 copy-start.10
  112.3 0.7 copy-start.52
  113.0 0.7 copy-start.53
  (16 other events, 10.5 us)

commit v3 on v2

--- a/solution.py
+++ b/solution.py
@@ -41,20 +41,15 @@
     return result
 
 
-def flow_body(
-    drag_ref, wet_ref, elem_ref, node_ref, flow_any,
-    *refs,
+def surface(
+    drag_ref, wet_ref, elem_ref, node_ref, got, own_ref, beyond_ref, sides_ref,
+    ext, drag, buoy, scale, tract, row_slot, col_slot, table_ref, store_fields,
 ):
-    got = (refs[0:5], refs[5:10], refs[10:15])
-    out_any, own_ref, beyond_ref, sides_ref = refs[15:19]
-    ext, drag, buoy, scale, tract, row_slot, col_slot, table_ref, sems = refs[19:]
     rows, cols = drag_ref.shape
     wide = cols + 128
     tall = rows + 8
     at_x, at_y = lax.axis_index("gx"), lax.axis_index("gy")
     last_x, last_y = lax.axis_size("gx") - 1, lax.axis_size("gy") - 1
-    own_in = pltpu.make_async_copy(flow_any, ext.at[0, :, 0:rows, 0:cols], sems.at[0])
-    own_in.start()
 
     def wetness(x):
         return 1.0 - 0.6 * x
@@ -139,7 +134,6 @@
         return carry
 
     lax.fori_loop(0, cols // 128, own_cells, 0)
-    own_in.wait()
 
     lanes = lax.broadcasted_iota(jnp.int32, (tall, 128), 1)
     first_lane = lanes == 0
@@ -211,8 +205,7 @@
         return lax.fori_loop(0, tiles, tile_step, carry)
 
     lax.fori_loop(0, FLOW_STEPS, step, 0)
-    own_out = pltpu.make_async_copy(ext.at[0, :, 0:rows, 0:cols], out_any, sems.at[1])
-    own_out.start()
+    store_fields.start()
 
     def pull(t, carry):
         at = pl.ds(pl.multiple_of(t * 128, 128), 128)
@@ -258,32 +251,6 @@
     lax.fori_loop(0, rows, spread, 0)
     table = [table_ref[128 * k : 128 * k + 64] + table_ref[128 * k + 64 : 128 * k + 128] for k in range(3)]
     load_parts(table, own_ref, beyond_ref, sides_ref)
-    own_out.wait()
-
-
-def flow_call(flow, drag, wet, elem, node, halos):
-    rows, cols = drag.shape
-    tall, wide = rows + 8, cols + 128
-    vmem = pl.BlockSpec(memory_space=pltpu.VMEM)
-    hbm = pl.BlockSpec(memory_space=pl.ANY)
-    return pl.pallas_call(
-        flow_body,
-        out_shape=(shape(6, rows, cols), shape(3, 56, 128), shape(3, 56, 128), shape(8, 128)),
-        in_specs=[vmem] * 4 + [hbm] + [vmem] * 15,
-        out_specs=(hbm, vmem, vmem, vmem),
-        scratch_shapes=[
-            pltpu.VMEM((2, 6, tall, wide), jnp.float32),
-            pltpu.VMEM((tall, wide), jnp.float32),
-            pltpu.VMEM((tall, wide), jnp.float32),
-            pltpu.VMEM((tall, wide), jnp.float32),
-            pltpu.VMEM((3, rows, cols), jnp.float32),
-            pltpu.VMEM((rows, cols), jnp.float32),
-            pltpu.VMEM((rows, cols), jnp.float32),
-            pltpu.VMEM((384, 256), jnp.float32),
-            pltpu.SemaphoreType.DMA((2,)),
-        ],
-        compiler_params=pltpu.CompilerParams(vmem_limit_bytes=48 * 2**20),
-    )(drag, wet, elem, node, flow, *halos)
 
 
 def line(matrix, s):
@@ -652,92 +619,140 @@
 ASIDE = AROUND[2:]
 
 
-def swap(collective_id, operands, outs, messages):
-    count = len(messages)
-
-    def body(*refs):
-        ins, out_refs = refs[: len(operands)], refs[len(operands) : len(operands) + len(outs)]
-        sent, come = refs[len(operands) + len(outs) :]
-        at_x, at_y = lax.axis_index("gx"), lax.axis_index("gy")
-        size_x, size_y = lax.axis_size("gx"), lax.axis_size("gy")
-
-        def device(move):
-            return ((at_x + move[0] + size_x) % size_x, (at_y + move[1] + size_y) % size_y)
-
-        barrier = pltpu.get_barrier_semaphore()
-        for move in AROUND:
-            pl.semaphore_signal(barrier, inc=1, device_id=device(move), device_id_type=pl.DeviceIdType.MESH)
-        pl.semaphore_wait(barrier, len(AROUND))
-        copies = []
-        for n, (source, source_index, target, target_index, move) in enumerate(messages):
-            copies.append(
-                pltpu.make_async_remote_copy(
-                    src_ref=ins[source].at[source_index] if source_index is not None else ins[source],
-                    dst_ref=out_refs[target].at[target_index] if target_index is not None else out_refs[target],
-                    send_sem=sent.at[n],
-                    recv_sem=come.at[n],
-                    device_id=device(move),
-                    device_id_type=pl.DeviceIdType.MESH,
-                )
-            )
-            copies[-1].start()
-        for copy in copies:
-            copy.wait()
-
-    return pl.pallas_call(
-        body,
-        out_shape=tuple(outs),
-        in_specs=[pl.BlockSpec(memory_space=pl.ANY)] * len(operands),
-        out_specs=tuple([pl.BlockSpec(memory_space=pl.ANY)] * len(outs)),
-        scratch_shapes=[pltpu.SemaphoreType.DMA((count,)), pltpu.SemaphoreType.DMA((count,))],
-        compiler_params=pltpu.CompilerParams(collective_id=collective_id, has_side_effects=True),
-    )(*operands)
-
-
 def shape(*dims, kind=jnp.float32):
     return jax.ShapeDtypeStruct(dims, kind)
 
 
-def local(body, operands, outs, scratch):
-    vmem = pl.BlockSpec(memory_space=pltpu.VMEM)
-    return pl.pallas_call(
-        body,
-        out_shape=tuple(outs),
-        in_specs=[vmem] * len(operands),
-        out_specs=tuple([vmem] * len(outs)),
-        scratch_shapes=[pltpu.VMEM(dims, jnp.float32) for dims in scratch],
-        compiler_params=pltpu.CompilerParams(vmem_limit_bytes=48 * 2**20),
-    )(*operands)
-
-
-def first_body(u_ref, lame_ref, shear_ref, density_ref, *refs):
-    around = {move: refs[n] for n, move in enumerate(AROUND)}
-    force, face_x, face_y, inverse, stress = refs[8:]
-    inverse_masses(density_ref, around, inverse)
-    internal_local(u_ref, lame_ref, shear_ref, stress, force)
-    pack_faces(force, face_x, face_y)
-
-
-def middle_body(force0, u_ref, before_ref, lame_ref, shear_ref, inverse, own_ref, *refs):
-    face_got_x, load_got_x = refs[0:2], refs[2:4]
-    face_got_y = {move: refs[4 + n] for n, move in enumerate(ASIDE)}
-    load_got_y = {move: refs[10 + n] for n, move in enumerate(ASIDE)}
-    u_next, force, face_x, face_y, load, stress = refs[16:]
-    load_total(own_ref, load_got_x, load_got_y, load)
-    force[...] = force0[...]
-    add_faces(force, face_got_x, face_got_y)
-    advance_solid(force, load, inverse, u_ref, before_ref, u_next)
-    internal_local(u_next, lame_ref, shear_ref, stress, force)
-    pack_faces(force, face_x, face_y)
-
-
-def last_body(force1, u_ref, before_ref, inverse, load, *refs):
-    face_got_x = refs[0:2]
-    face_got_y = {move: refs[2 + n] for n, move in enumerate(ASIDE)}
-    u_next, force = refs[8:]
-    force[...] = force1[...]
-    add_faces(force, face_got_x, face_got_y)
-    advance_solid(force, load, inverse, u_ref, before_ref, u_next)
+def halo_plan(rows, cols):
+    edge_rows = {-1: pl.ds(0, 4), 1: pl.ds(rows - 4, 4)}
+    edge_cols = {-1: pl.ds(0, 128), 1: pl.ds(cols - 128, 128)}
+    place_rows = {-1: pl.ds(0, 4), 1: pl.ds(4, 4)}
+    messages = []
+    for source in range(3):
+        every = (slice(None),) if source == 0 else ()
+        for dx, dy in AROUND:
+            row_in = edge_rows.get(dx, pl.ds(0, rows))
+            row_out = place_rows.get(dx, pl.ds(0, rows))
+            col_in = edge_cols.get(dy, pl.ds(0, cols))
+            where = 0 if dy == 0 else (1 if dx == 0 else 3) + (0 if dy == 1 else 1)
+            messages.append(
+                (source, every + (row_in, col_in), 5 * source + where,
+                 every + (row_out, pl.ds(0, cols if dy == 0 else 128)), (dx, dy))
+            )
+    return messages
+
+
+def whole_body(*refs):
+    (flow_in, drag_in, wet_in, elem_in, node_in, u_in, before_in, density_in, lame_in, shear_in) = refs[:10]
+    fields_out, next_out, last_out = refs[10:13]
+    (ext, drag, buoy, scale, tract, row_slot, col_slot, table) = refs[13:21]
+    halos = refs[21:36]
+    (drag_own, wet_own, elem_own, node_own) = refs[36:40]
+    (u_zero, before, u_one, u_two, force, stress, load, inverse) = refs[40:48]
+    (density, lame, shear, around) = refs[48:52]
+    (face_x, face_y, got_face_x, got_face_y) = refs[52:56]
+    (own, beyond, sides, got_beyond, got_sides) = refs[56:61]
+    local_sem, sent, come = refs[61:]
+    rows, cols = drag_own.shape
+    at_x, at_y = lax.axis_index("gx"), lax.axis_index("gy")
+    size_x, size_y = lax.axis_size("gx"), lax.axis_size("gy")
+
+    def device(move):
+        return ((at_x + move[0] + size_x) % size_x, (at_y + move[1] + size_y) % size_y)
+
+    def opposite(move):
+        return -move[0], -move[1]
+
+    barrier = pltpu.get_barrier_semaphore()
+    for move in AROUND:
+        pl.semaphore_signal(barrier, inc=1, device_id=device(move), device_id_type=pl.DeviceIdType.MESH)
+    reads = [
+        pltpu.make_async_copy(source, target, local_sem.at[n])
+        for n, (source, target) in enumerate(
+            (
+                (u_in, u_zero), (lame_in, lame), (shear_in, shear), (density_in, density),
+                (flow_in, ext.at[0, :, 0:rows, 0:cols]), (drag_in, drag_own), (wet_in, wet_own),
+                (elem_in, elem_own), (node_in, node_own), (before_in, before),
+            )
+        )
+    ]
+    for copy in reads:
+        copy.start()
+    store_fields = pltpu.make_async_copy(ext.at[0, :, 0:rows, 0:cols], fields_out, local_sem.at[10])
+    store_last = pltpu.make_async_copy(u_one, last_out, local_sem.at[11])
+    store_next = pltpu.make_async_copy(u_two, next_out, local_sem.at[12])
+    pl.semaphore_wait(barrier, len(AROUND))
+    number = [0]
+
+    def send(source, target, move):
+        n = number[0]
+        number[0] += 1
+        copy = pltpu.make_async_remote_copy(
+            src_ref=source, dst_ref=target, send_sem=sent.at[n], recv_sem=come.at[n],
+            device_id=device(move), device_id_type=pl.DeviceIdType.MESH,
+        )
+        copy.start()
+        return copy
+
+    operands = (flow_in, drag_in, wet_in)
+    first = [
+        send(operands[source].at[source_at], halos[target].at[target_at], move)
+        for source, source_at, target, target_at, move in halo_plan(rows, cols)
+    ]
+    first += [send(density_in, around.at[AROUND.index(opposite(move))], move) for move in AROUND]
+
+    def send_faces(step):
+        copies = [send(face_x.at[step], got_face_x.at[step, 1], (-1, 0))]
+        copies += [send(face_x.at[step], got_face_x.at[step, 0], (1, 0))]
+        for move in ASIDE:
+            copies.append(send(face_y.at[step], got_face_y.at[step, ASIDE.index(opposite(move))], move))
+        return copies
+
+    def faces_of(step):
+        return (
+            [got_face_x.at[step, n] for n in range(2)],
+            {move: got_face_y.at[step, n] for n, move in enumerate(ASIDE)},
+        )
+
+    for copy in reads[:3]:
+        copy.wait()
+    internal_local(u_zero, lame, shear, stress, force)
+    pack_faces(force, face_x.at[0], face_y.at[0])
+    faces = send_faces(0)
+    for copy in reads[3:] + first:
+        copy.wait()
+    inverse_masses(density, {move: around.at[n] for n, move in enumerate(AROUND)}, inverse)
+    surface(
+        drag_own, wet_own, elem_own, node_own, (halos[0:5], halos[5:10], halos[10:15]),
+        own, beyond, sides, ext, drag, buoy, scale, tract, row_slot, col_slot, table, store_fields,
+    )
+    loads = [send(beyond, got_beyond.at[1], (-1, 0)), send(beyond, got_beyond.at[0], (1, 0))]
+    for move in ASIDE:
+        loads.append(send(sides, got_sides.at[ASIDE.index(opposite(move))], move))
+    for copy in faces:
+        copy.wait()
+    add_faces(force, *faces_of(0))
+    for copy in loads:
+        copy.wait()
+    load_total(
+        own,
+        [got_beyond.at[n] for n in range(2)],
+        {move: got_sides.at[n] for n, move in enumerate(ASIDE)},
+        load,
+    )
+    advance_solid(force, load, inverse, u_zero, before, u_one)
+    store_last.start()
+    internal_local(u_one, lame, shear, stress, force)
+    pack_faces(force, face_x.at[1], face_y.at[1])
+    faces = send_faces(1)
+    for copy in faces:
+        copy.wait()
+    add_faces(force, *faces_of(1))
+    advance_solid(force, load, inverse, u_one, u_zero, u_two)
+    store_next.start()
+    store_fields.wait()
+    store_last.wait()
+    store_next.wait()
 
 
 def per_device(
@@ -753,77 +768,47 @@
     shear_modulus,
 ):
     rows, cols = drag_coefficient.shape
-    u = displacement.reshape(375, 4, 128)
-    before = previous.reshape(375, 4, 128)
-    density, lame, shear = (x.reshape(4, 128) for x in (density, lame_first, shear_modulus))
-    edge_rows = {-1: pl.ds(0, 4), 1: pl.ds(rows - 4, 4)}
-    edge_cols = {-1: pl.ds(0, 128), 1: pl.ds(cols - 128, 128)}
-    place_rows = {-1: pl.ds(0, 4), 1: pl.ds(4, 4)}
-    outs, messages = [], []
-    for source, lead in ((0, (6,)), (1, ()), (2, ())):
-        kind_of = jnp.int32 if source == 2 else jnp.float32
-        every = (slice(None),) * len(lead)
-        base = len(outs)
-        outs += [shape(*lead, 8, cols, kind=kind_of)]
-        outs += [shape(*lead, rows, 128, kind=kind_of)] * 2
-        outs += [shape(*lead, 8, 128, kind=kind_of)] * 2
-        for dx, dy in AROUND:
-            row_in = edge_rows.get(dx, pl.ds(0, rows))
-            row_out = place_rows.get(dx, pl.ds(0, rows))
-            col_in = edge_cols.get(dy, pl.ds(0, cols))
-            where = 0 if dy == 0 else (1 if dx == 0 else 3) + (0 if dy == 1 else 1)
-            messages.append(
-                (source, every + (row_in, col_in), base + where,
-                 every + (row_out, pl.ds(0, cols if dy == 0 else 128)), (dx, dy))
-            )
-    base = len(outs)
-    outs += [shape(4, 128)] * 8
-    for n, (dx, dy) in enumerate(AROUND):
-        messages.append((3, None, base + AROUND.index((-dx, -dy)), None, (dx, dy)))
-    got = swap(1, [flow_state, drag_coefficient, wet_mask, density], outs, messages)
-
-    full = (375, 4, 128)
-    force, face_x, face_y, inverse = local(
-        first_body,
-        [u, lame, shear, density, *got[15:]],
-        [shape(*full), shape(75, 4, 128), shape(2, 4, 128), shape(27, 4, 128)],
-        [full],
+    tall, wide = rows + 8, cols + 128
+    grid = displacement.shape
+    nodes = (375, 4, 128)
+    halo_shapes = []
+    for lead, kind_of in (((6,), jnp.float32), ((), jnp.float32), ((), jnp.int32)):
+        for dims in ((8, cols), (rows, 128), (rows, 128), (8, 128), (8, 128)):
+            halo_shapes.append(pltpu.VMEM((*lead, *dims), kind_of))
+
+    def floats(*dims):
+        return pltpu.VMEM(dims, jnp.float32)
+
+    def integers(*dims):
+        return pltpu.VMEM(dims, jnp.int32)
+
+    scratch = [
+        floats(2, 6, tall, wide), floats(tall, wide), floats(tall, wide), floats(tall, wide),
+        floats(3, rows, cols), floats(rows, cols), floats(rows, cols), floats(384, 256),
+        *halo_shapes,
+        floats(rows, cols), integers(rows, cols), integers(rows, cols), integers(rows, cols),
+        *[floats(*nodes)] * 6, floats(75, 4, 128), floats(27, 4, 128),
+        floats(4, 128), floats(4, 128), floats(4, 128), floats(8, 4, 128),
+        floats(2, 75, 4, 128), floats(2, 2, 4, 128), floats(2, 2, 75, 4, 128), floats(2, 6, 2, 4, 128),
+        floats(3, 56, 128), floats(3, 56, 128), floats(8, 128), floats(2, 3, 56, 128), floats(6, 8, 128),
+        pltpu.SemaphoreType.DMA((13,)), pltpu.SemaphoreType.DMA((56,)), pltpu.SemaphoreType.DMA((56,)),
+    ]
+    anywhere = pl.BlockSpec(memory_space=pl.ANY)
+    fields, u_two, u_one = pl.pallas_call(
+        whole_body,
+        out_shape=(shape(6, rows, cols), shape(*nodes), shape(*nodes)),
+        in_specs=[anywhere] * 10,
+        out_specs=(anywhere,) * 3,
+        scratch_shapes=scratch,
+        compiler_params=pltpu.CompilerParams(
+            collective_id=1, has_side_effects=True, vmem_limit_bytes=56 * 2**20
+        ),
+    )(
+        flow_state, drag_coefficient, wet_mask, target_elem, target_node,
+        displacement.reshape(nodes), previous.reshape(nodes),
+        *(x.reshape(4, 128) for x in (density, lame_first, shear_modulus)),
     )
-    fields, own, beyond, sides = flow_call(
-        flow_state, drag_coefficient, wet_mask, target_elem, target_node, got[:15]
-    )
-    faces = [shape(75, 4, 128)] * 2
-    face_messages = [(0, None, 1, None, (-1, 0)), (0, None, 0, None, (1, 0))]
-    sent_loads = [(2, None, 3, None, (-1, 0)), (2, None, 2, None, (1, 0))]
-    side_messages = [
-        (1, None, 4 + ASIDE.index((-dx, -dy)), None, (dx, dy)) for dx, dy in ASIDE
-    ] + [(3, None, 10 + ASIDE.index((-dx, -dy)), None, (dx, dy)) for dx, dy in ASIDE]
-    got = swap(
-        2,
-        [face_x, face_y, beyond, sides],
-        faces + [shape(3, 56, 128)] * 2 + [shape(2, 4, 128)] * 6 + [shape(8, 128)] * 6,
-        face_messages + sent_loads + side_messages,
-    )
-    u_one, force, face_x, face_y, load = local(
-        middle_body,
-        [force, u, before, lame, shear, inverse, own, *got],
-        [shape(*full), shape(*full), shape(75, 4, 128), shape(2, 4, 128), shape(75, 4, 128)],
-        [full],
-    )
-    got = swap(
-        3,
-        [face_x, face_y],
-        faces + [shape(2, 4, 128)] * 6,
-        face_messages
-        + [(1, None, 2 + ASIDE.index((-dx, -dy)), None, (dx, dy)) for dx, dy in ASIDE],
-    )
-    (u_two,) = local(
-        last_body,
-        [force, u_one, u, inverse, load, *got],
-        [shape(*full)],
-        [full],
-    )
-    return (fields, u_two.reshape(displacement.shape), u_one.reshape(displacement.shape))
+    return (fields, u_two.reshape(grid), u_one.reshape(grid))
 
 
 def solution(mesh):

time: 119 us -> 71.2 us (0.60); the launches traced: 116 us -> 70.6 us
  local copies, waits for them, and re-layouts: 35.2 us -> 4.57 us
  Pallas kernels: 80 us -> 65.4 us
    unnamed x128 -> x7, local copies, waits for them, and re-layouts: 35.2 us -> 4.57 us
    pallas_call x7 -> x1, Pallas kernels: 80 us -> 65.4 us  [per_device(): pl.pallas_call(whole_body, out_shape=(shape(6, rows, cols), shape(*nodes)...]
where the time goes in v3:
time: 71.2 us; the launch traced here: 70.6 us
  Pallas kernels  65.4 us (92%)
  local copies, waits for them, and re-layouts  4.57 us (6%)
    pallas_call x1, Pallas kernels, per_device(): pl.pallas_call(whole_body, out_shape=(shape(6, rows, cols), shape(*nodes)...  65.4 us
    unnamed x7, local copies, waits for them, and re-layouts  4.57 us

profile of v3, /device:TPU:1, one launch (start us, length us, event | category | flops | bytes accessed | tf_op | source)
XLA Modules:
  0.0 70.6 jit_solution(74540872262047377)
XLA Ops:
  0.6 65.4 %shard_map.121 = (f32[6,32,2048]{2,1,0:T(8,128)}, f32[375,4,128]{2,1,0:T(4,128)}, f32[375,4,128]{2,1,0:T(4,128)}) custom-call(f32[6,32,2048]{2,1,0:T(8,128)} %refs_0_.1, f32[32,2048]{1,0:T(8,128)} %refs_1_.1, s32[32,2048]{1,0:T(8,128)} %refs_2_.1, s32[32,2048]{1,0:T(8,128)} %refs_3_.1, s32[32,2048]{1,0:T(8,128)} %refs_4_.1, f32[375,4,128]{2,1,0:T(4,128)} %bitcast.9, ...), custom_call_target="tpu_custom_call" | custom-call | tf_op jit(solution)/shard_map/pallas_call | solution.py:797
  66.0 0.0 copy-start.1
  66.0 0.0 copy-start
  66.0 2.8 %copy.16 = f32[6,32,2048]{2,1,0:T(8,128)} copy(f32[6,32,2048]{2,1,0:T(8,128)} %get-tuple-element.12) | data formatting | bytes 3145728
  68.8 0.0 copy-done.1
  68.8 0.9 %copy.17 = f32[3,5,5,5,2,2,128]{6,5,4,3,2,1,0:T(2,128)} copy(f32[3,5,5,5,2,2,128]{6,5,4,3,2,1,0:T(2,128)S(1)} %bitcast.8) | data formatting | bytes 1536000
  69.7 0.0 copy-done
  69.7 0.9 %copy.18 = f32[3,5,5,5,2,2,128]{6,5,4,3,2,1,0:T(2,128)} copy(f32[3,5,5,5,2,2,128]{6,5,4,3,2,1,0:T(2,128)S(1)} %bitcast.7) | data formatting | bytes 1536000
Async XLA Ops:
  66.0 2.8 %copy-start.1 = (f32[375,4,128]{2,1,0:T(4,128)S(1)}, f32[375,4,128]{2,1,0:T(4,128)}, u32[]{:S(2)}) copy-start(f32[375,4,128]{2,1,0:T(4,128)} %get-tuple-element.7) | copy-start | bytes 2304004
  66.0 3.7 %copy-start = (f32[375,4,128]{2,1,0:T(4,128)S(1)}, f32[375,4,128]{2,1,0:T(4,128)}, u32[]{:S(2)}) copy-start(f32[375,4,128]{2,1,0:T(4,128)} %get-tuple-element.8) | copy-start | bytes 2304004

commit v4 on v3

--- a/solution.py
+++ b/solution.py
@@ -8,6 +8,8 @@
 
 FLOW_STEPS = 4
 SOLID_STEPS = 2
+SLOT_ROWS = 51
+GROUP = 8
 
 
 gll_points = np.array([-1.0, -np.sqrt(3.0 / 7.0), 0.0, np.sqrt(3.0 / 7.0), 1.0])
@@ -143,8 +145,7 @@
     def press(f0, f1, b):
         return b * (f0 + f1), upper_gravity * density_ratio * f0 + upper_gravity * f1
 
-    def step(s, carry):
-        now = s % 2
+    def step(now, carry):
         later = 1 - now
 
         def tile_step(t, carry):
@@ -202,9 +203,9 @@
             ext[later, 5, :, at] = k * (sums[5] + f[3])
             return carry
 
-        return lax.fori_loop(0, tiles, tile_step, carry)
-
-    lax.fori_loop(0, FLOW_STEPS, step, 0)
+        return lax.fori_loop(0, tiles, tile_step, carry, unroll=True)
+
+    lax.fori_loop(0, FLOW_STEPS // 2, lambda _, carry: step(1, step(0, carry)), 0)
     store_fields.start()
 
     def pull(t, carry):
@@ -219,37 +220,60 @@
     lax.fori_loop(0, cols // 128, pull, 0)
 
     table_ref[...] = jnp.zeros_like(table_ref)
-    count = lax.broadcasted_iota(jnp.int32, (16, cols), 0).astype(jnp.float32).astype(jnp.bfloat16)
-
-    def spread(r, carry):
-        line = pl.ds(r, 1)
-
-        def wide16(x):
-            return jnp.broadcast_to(x, (16, cols)).astype(jnp.bfloat16)
-
-        parts = []
-        for k in range(3):
-            value = tract[k, line, :]
-            high = value.astype(jnp.bfloat16).astype(jnp.float32)
-            parts.append(wide16(value))
-            parts.append(wide16(value - high))
-        a = wide16(row_slot[line, :])
-        b = wide16(col_slot[line, :])
-        zero = jnp.zeros((16, cols), jnp.bfloat16)
-        one = jnp.ones((16, cols), jnp.bfloat16)
-        hits = [a == count + jnp.bfloat16(16 * m) for m in range(4)]
-        left = jnp.concatenate([jnp.where(h, p, zero) for p in parts for h in hits], axis=0)
-        right = jnp.concatenate(
-            [jnp.where(b == count + jnp.bfloat16(16 * m), one, zero) for m in range(16)], axis=0
+    narrow = jnp.bfloat16
+    row16 = lax.broadcasted_iota(jnp.int32, (16, cols), 0)
+    count = row16.astype(jnp.float32).astype(narrow)
+
+    def spread(group, carry):
+        lefts, rights = [], []
+        for n in range(GROUP):
+            line = pl.ds(group * GROUP + n, 1)
+
+            def wide16(x):
+                return jnp.broadcast_to(x, (16, cols)).astype(narrow)
+
+            parts = []
+            for k in range(3):
+                value = tract[k, line, :]
+                high = value.astype(narrow).astype(jnp.float32)
+                parts.append(wide16(value))
+                parts.append(wide16(value - high))
+            a = wide16(row_slot[line, :])
+            b = wide16(col_slot[line, :])
+            zero = jnp.zeros((16, cols), narrow)
+            one = jnp.ones((16, cols), narrow)
+            pieces = []
+            for top in range(0, table_ref.shape[0], 16):
+                part, last = top // SLOT_ROWS, min((top + 15) // SLOT_ROWS, 5)
+                skip = top - SLOT_ROWS * part
+                if part == last:
+                    pieces.append(jnp.where(a == count + narrow(skip), parts[part], zero))
+                else:
+                    split = SLOT_ROWS * last - top
+                    target = row16 + jnp.where(row16 < split, skip, -split)
+                    mixed = jnp.where(count < narrow(split), parts[part], parts[last])
+                    pieces.append(jnp.where(a == target.astype(jnp.float32).astype(narrow), mixed, zero))
+            lefts.append(jnp.concatenate(pieces, axis=0))
+            rights.append(
+                jnp.concatenate([jnp.where(b == count + narrow(16 * m), one, zero) for m in range(16)], axis=0)
+            )
+        table_ref[...] += lax.dot_general(
+            jnp.concatenate(lefts, axis=1),
+            jnp.concatenate(rights, axis=1),
+            (((1,), (1,)), ((), ())),
+            preferred_element_type=jnp.float32,
         )
-        got = lax.dot_general(
-            left, right, (((1,), (1,)), ((), ())), preferred_element_type=jnp.float32
-        )
-        table_ref[...] += got
-        return carry
-
-    lax.fori_loop(0, rows, spread, 0)
-    table = [table_ref[128 * k : 128 * k + 64] + table_ref[128 * k + 64 : 128 * k + 128] for k in range(3)]
+        return carry
+
+    lax.fori_loop(0, rows // GROUP, spread, 0)
+
+    def part_rows(n):
+        return table_ref[SLOT_ROWS * n : SLOT_ROWS * n + SLOT_ROWS]
+
+    pad = jnp.zeros((64 - SLOT_ROWS, 256), jnp.float32)
+    table = [
+        jnp.concatenate([part_rows(2 * k) + part_rows(2 * k + 1), pad], axis=0) for k in range(3)
+    ]
     load_parts(table, own_ref, beyond_ref, sides_ref)
 
 
@@ -755,6 +779,15 @@
     store_next.wait()
 
 
+def store_body(*refs):
+    sems = refs[6]
+    copies = [pltpu.make_async_copy(refs[n], refs[3 + n], sems.at[n]) for n in range(3)]
+    for copy in copies:
+        copy.start()
+    for copy in copies:
+        copy.wait()
+
+
 def per_device(
     flow_state,
     drag_coefficient,
@@ -784,7 +817,7 @@
 
     scratch = [
         floats(2, 6, tall, wide), floats(tall, wide), floats(tall, wide), floats(tall, wide),
-        floats(3, rows, cols), floats(rows, cols), floats(rows, cols), floats(384, 256),
+        floats(3, rows, cols), floats(rows, cols), floats(rows, cols), floats(320, 256),
         *halo_shapes,
         floats(rows, cols), integers(rows, cols), integers(rows, cols), integers(rows, cols),
         *[floats(*nodes)] * 6, floats(75, 4, 128), floats(27, 4, 128),
@@ -794,7 +827,7 @@
         pltpu.SemaphoreType.DMA((13,)), pltpu.SemaphoreType.DMA((56,)), pltpu.SemaphoreType.DMA((56,)),
     ]
     anywhere = pl.BlockSpec(memory_space=pl.ANY)
-    fields, u_two, u_one = pl.pallas_call(
+    results = pl.pallas_call(
         whole_body,
         out_shape=(shape(6, rows, cols), shape(*nodes), shape(*nodes)),
         in_specs=[anywhere] * 10,
@@ -808,6 +841,13 @@
         displacement.reshape(nodes), previous.reshape(nodes),
         *(x.reshape(4, 128) for x in (density, lame_first, shear_modulus)),
     )
+    fields, u_two, u_one = pl.pallas_call(
+        store_body,
+        out_shape=tuple(shape(*x.shape) for x in results),
+        in_specs=[anywhere] * 3,
+        out_specs=(anywhere,) * 3,
+        scratch_shapes=[pltpu.SemaphoreType.DMA((3,))],
+    )(*results)
     return (fields, u_two.reshape(grid), u_one.reshape(grid))
 
 

time: 71.2 us -> 150 us (2.11)
  Pallas kernels: 65.4 us -> 149 us
  local copies, waits for them, and re-layouts: 4.57 us -> 0 us
    pallas_call x0 -> x1, Pallas kernels: none -> 95.3 us  [per_device(): pl.pallas_call(store_body, out_shape=tuple((shape(*x.shape) for x in resu...]
    pallas_call x1, Pallas kernels: 65.4 us -> 53.8 us  [per_device(): pl.pallas_call(whole_body, out_shape=(shape(6, rows, cols), shape(*nodes)...]
    unnamed x7 -> x0, local copies, waits for them, and re-layouts: 4.57 us -> none
where the time goes in v4:
time: 150 us
  Pallas kernels  149 us (99%)
    pallas_call x1, Pallas kernels, per_device(): pl.pallas_call(store_body, out_shape=tuple((shape(*x.shape) for x in resu...  95.3 us
    pallas_call x1, Pallas kernels, per_device(): pl.pallas_call(whole_body, out_shape=(shape(6, rows, cols), shape(*nodes)...  53.8 us

profile of v4, /device:TPU:1, one launch (start us, length us, event | category | flops | bytes accessed | tf_op | source)
XLA Modules:
  0.0 149.8 jit_solution(1898891659496581694)
XLA Ops:
  0.6 53.8 %shard_map.121 = (f32[6,32,2048]{2,1,0:T(8,128)}, f32[375,4,128]{2,1,0:T(4,128)}, f32[375,4,128]{2,1,0:T(4,128)}) custom-call(f32[6,32,2048]{2,1,0:T(8,128)} %refs_0_.1, f32[32,2048]{1,0:T(8,128)} %refs_1_.1, s32[32,2048]{1,0:T(8,128)} %refs_2_.1, s32[32,2048]{1,0:T(8,128)} %refs_3_.1, s32[32,2048]{1,0:T(8,128)} %refs_4_.1, f32[375,4,128]{2,1,0:T(4,128)} %bitcast.7, ...), custom_call_target="tpu_custom_call" | custom-call | tf_op jit(solution)/shard_map/pallas_call | solution.py:830
  54.5 95.3 %shard_map.122 = (f32[6,32,2048]{2,1,0:T(8,128)}, f32[375,4,128]{2,1,0:T(4,128)}, f32[375,4,128]{2,1,0:T(4,128)}) custom-call(f32[6,32,2048]{2,1,0:T(8,128)} %get-tuple-element.9.refs_0_, f32[375,4,128]{2,1,0:T(4,128)} %get-tuple-element.10.refs_1_, f32[375,4,128]{2,1,0:T(4,128)} %get-tuple-element.11.refs_2_), custom_call_target="tpu_custom_call" | custom-call | tf_op jit(solution)/shard_map/pallas_call | solution.py:844

commit v5 on v4

--- a/solution.py
+++ b/solution.py
@@ -44,7 +44,7 @@
 
 
 def surface(
-    drag_ref, wet_ref, elem_ref, node_ref, got, own_ref, beyond_ref, sides_ref,
+    drag_ref, wet_ref, elem_ref, node_ref, arrive, got, own_ref, beyond_ref, sides_ref,
     ext, drag, buoy, scale, tract, row_slot, col_slot, table_ref, store_fields,
 ):
     rows, cols = drag_ref.shape
@@ -55,61 +55,6 @@
 
     def wetness(x):
         return 1.0 - 0.6 * x
-
-    sub = lax.broadcasted_iota(jnp.int32, (8, 128), 0)
-    lane = lax.broadcasted_iota(jnp.int32, (8, 128), 1)
-    up_half = sub < 4
-    left_half = lane < 64
-
-    def zero_rows(tile):
-        tile = jnp.where(up_half & (at_x == last_x), 0.0, tile)
-        return jnp.where(jnp.logical_not(up_half) & (at_x == 0), 0.0, tile)
-
-    def zero_cols(tile):
-        tile = jnp.where(left_half & (at_y == last_y), 0.0, tile)
-        return jnp.where(jnp.logical_not(left_half) & (at_y == 0), 0.0, tile)
-
-    def received(k, n, *at):
-        if k < 6:
-            return got[0][n][(k, *at)]
-        tile = got[k - 5][n][at]
-        return tile if k == 6 else tile.astype(jnp.float32)
-
-    def place(k, r, c, tile):
-        if k < 6:
-            ext[0, k, r, c] = tile
-        elif k == 6:
-            drag[r, c] = tile
-        else:
-            buoy[r, c] = wetness(tile)
-
-    tail = pl.ds(cols, 128)
-    foot = pl.ds(rows, 8)
-    ones = jnp.full((8, 128), 0.2, jnp.float32)
-    row_scale = zero_rows(ones)
-    col_scale = zero_cols(ones)
-
-    def halo_rows(t, carry):
-        at = pl.ds(pl.multiple_of(t * 128, 128), 128)
-        for k in range(8):
-            place(k, foot, at, zero_rows(received(k, 0, slice(None), at)))
-        for r in range(0, rows, 8):
-            scale[r : r + 8, at] = ones
-        scale[foot, at] = row_scale
-        return carry
-
-    lax.fori_loop(0, cols // 128, halo_rows, 0)
-    for k in range(8):
-        for r in range(0, rows, 8):
-            at = (slice(r, r + 8), slice(None))
-            tile = jnp.where(left_half, received(k, 2, *at), received(k, 1, *at))
-            place(k, pl.ds(r, 8), tail, zero_cols(tile))
-        at = (slice(None), slice(None))
-        tile = jnp.where(left_half, received(k, 4, *at), received(k, 3, *at))
-        place(k, foot, tail, zero_cols(zero_rows(tile)))
-    for r in range(0, rows, 8):
-        scale[r : r + 8, tail] = col_scale
-    scale[foot, tail] = zero_cols(row_scale)
 
     def own_cells(t, carry):
         at = pl.ds(pl.multiple_of(t * 128, 128), 128)
@@ -136,6 +81,62 @@
         return carry
 
     lax.fori_loop(0, cols // 128, own_cells, 0)
+    arrive()
+
+    sub = lax.broadcasted_iota(jnp.int32, (8, 128), 0)
+    lane = lax.broadcasted_iota(jnp.int32, (8, 128), 1)
+    up_half = sub < 4
+    left_half = lane < 64
+
+    def zero_rows(tile):
+        tile = jnp.where(up_half & (at_x == last_x), 0.0, tile)
+        return jnp.where(jnp.logical_not(up_half) & (at_x == 0), 0.0, tile)
+
+    def zero_cols(tile):
+        tile = jnp.where(left_half & (at_y == last_y), 0.0, tile)
+        return jnp.where(jnp.logical_not(left_half) & (at_y == 0), 0.0, tile)
+
+    def received(k, n, *at):
+        if k < 6:
+            return got[0][n][(k, *at)]
+        tile = got[k - 5][n][at]
+        return tile if k == 6 else tile.astype(jnp.float32)
+
+    def place(k, r, c, tile):
+        if k < 6:
+            ext[0, k, r, c] = tile
+        elif k == 6:
+            drag[r, c] = tile
+        else:
+            buoy[r, c] = wetness(tile)
+
+    tail = pl.ds(cols, 128)
+    foot = pl.ds(rows, 8)
+    ones = jnp.full((8, 128), 0.2, jnp.float32)
+    row_scale = zero_rows(ones)
+    col_scale = zero_cols(ones)
+
+    def halo_rows(t, carry):
+        at = pl.ds(pl.multiple_of(t * 128, 128), 128)
+        for k in range(8):
+            place(k, foot, at, zero_rows(received(k, 0, slice(None), at)))
+        for r in range(0, rows, 8):
+            scale[r : r + 8, at] = ones
+        scale[foot, at] = row_scale
+        return carry
+
+    lax.fori_loop(0, cols // 128, halo_rows, 0)
+    for k in range(8):
+        for r in range(0, rows, 8):
+            at = (slice(r, r + 8), slice(None))
+            tile = jnp.where(left_half, received(k, 2, *at), received(k, 1, *at))
+            place(k, pl.ds(r, 8), tail, zero_cols(tile))
+        at = (slice(None), slice(None))
+        tile = jnp.where(left_half, received(k, 4, *at), received(k, 3, *at))
+        place(k, foot, tail, zero_cols(zero_rows(tile)))
+    for r in range(0, rows, 8):
+        scale[r : r + 8, tail] = col_scale
+    scale[foot, tail] = zero_cols(row_scale)
 
     lanes = lax.broadcasted_iota(jnp.int32, (tall, 128), 1)
     first_lane = lanes == 0
@@ -298,7 +299,7 @@
     return lane, row
 
 
-def internal_local(u_ref, lame_ref, shear_ref, stress, force):
+def internal_open(u_ref, lame_ref, shear_ref, stress, force):
     table = derivative_table()
 
     def slope_x(m, carry):
@@ -358,6 +359,74 @@
         return carry
 
     lax.fori_loop(0, 5, plane, 0)
+
+
+def internal_kick(kick, lame_ref, shear_ref, force):
+    table = derivative_table()
+    lame, shear = -lame_ref[...], -shear_ref[...]
+    five = range(5)
+
+    def grid(make):
+        return [[make(a, b) for b in five] for a in five]
+
+    def along_x(matrix, x):
+        lines = [line(matrix, [x[a][b] for a in five]) for b in five]
+        return grid(lambda a, b: lines[b][a])
+
+    def along_y(matrix, x):
+        lines = [line(matrix, x[a]) for a in five]
+        return grid(lambda a, b: lines[a][b])
+
+    def plus(x, y):
+        return grid(lambda a, b: x[a][b] + y[a][b])
+
+    def area(a, b):
+        return np.float32(gll_weights[a] * gll_weights[b])
+
+    d = [grid(lambda a, b: kick[i * 25 + a * 5 + b]) for i in range(3)]
+    d_x = [along_x(table, x) for x in d]
+    d_y = [along_y(table, x) for x in d]
+    lame_w = grid(lambda a, b: lame * area(a, b))
+    shear_w = grid(lambda a, b: shear * area(a, b))
+    t_side = grid(lambda a, b: lame_w[a][b] * d[2][a][b])
+    t_02 = grid(lambda a, b: shear_w[a][b] * d[0][a][b])
+    t_12 = grid(lambda a, b: shear_w[a][b] * d[1][a][b])
+    t_22 = grid(lambda a, b: t_side[a][b] + (shear_w[a][b] + shear_w[a][b]) * d[2][a][b])
+    first = np.float32(gll_weights[0])
+    l_0 = grid(lambda a, b: first * lame_w[a][b])
+    m_0 = grid(lambda a, b: first * shear_w[a][b])
+    e_22 = grid(lambda a, b: l_0[a][b] * (d_x[0][a][b] + d_y[1][a][b]))
+    e_00 = grid(lambda a, b: e_22[a][b] + (m_0[a][b] + m_0[a][b]) * d_x[0][a][b])
+    e_11 = grid(lambda a, b: e_22[a][b] + (m_0[a][b] + m_0[a][b]) * d_y[1][a][b])
+    e_01 = grid(lambda a, b: m_0[a][b] * (d_y[0][a][b] + d_x[1][a][b]))
+    e_02 = grid(lambda a, b: m_0[a][b] * d_x[2][a][b])
+    e_12 = grid(lambda a, b: m_0[a][b] * d_y[2][a][b])
+    turned = table.T
+    pulled = (
+        along_x(turned, t_side),
+        along_y(turned, t_side),
+        plus(along_x(turned, t_02), along_y(turned, t_12)),
+    )
+    flat = (
+        plus(along_x(turned, e_00), along_y(turned, e_01)),
+        plus(along_x(turned, e_01), along_y(turned, e_11)),
+        plus(along_x(turned, e_02), along_y(turned, e_12)),
+    )
+    share = [float(table[c, 0] * gll_weights[c]) for c in five]
+    upright = [float(sum(table[p, c] * share[p] for p in five)) for c in five]
+    for i, (t, e) in enumerate(((t_02, e_02), (t_12, e_12), (t_22, e_22))):
+        for a in five:
+            for b in five:
+                for c in five:
+                    value = share[c] * pulled[i][a][b] + upright[c] * t[a][b]
+                    value = value + float(table[0, c]) * e[a][b]
+                    if c == 0:
+                        value = value + flat[i][a][b]
+                    force[i * 125 + a * 25 + b * 5 + c] += value
+
+
+def internal_close(stress, force):
+    table = derivative_table()
     lane, row = lane_row()
     low_x = row % 2 == 0
     low_z = row < 2
@@ -398,12 +467,19 @@
     lane, row = lane_row()
     low_x = row % 2 == 0
 
+    def both(m, other):
+        for i in range(3):
+            near, far = force[i * 125 + m], force[i * 125 + 100 + m]
+            near_other, far_other = force[i * 125 + other], force[i * 125 + 100 + other]
+            face_x[0, i * 13 + m] = jnp.where(low_x, near, pltpu.roll(near_other, 1, 0))
+            face_x[1, i * 13 + m] = jnp.where(low_x, pltpu.roll(far, 3, 0), far_other)
+
     def pack_x(m, carry):
-        for i in range(3):
-            face_x[i * 25 + m] = jnp.where(low_x, force[i * 125 + m], force[i * 125 + 100 + m])
-        return carry
-
-    lax.fori_loop(0, 25, pack_x, 0)
+        both(m, m + 13)
+        return carry
+
+    lax.fori_loop(0, 12, pack_x, 0)
+    both(12, 12)
     ends = [jnp.zeros((4, 128), jnp.float32)] * 2
     for a in range(5):
         for i in range(3):
@@ -428,15 +504,23 @@
     lane, row = lane_row()
     low_x = row % 2 == 0
 
+    def one(m, other):
+        for i in range(3):
+            low, high = got_x[0][i * 13 + m], got_x[1][i * 13 + m]
+            force[i * 125 + m] += jnp.where(low_x & has_x[-1], low, 0.0)
+            force[i * 125 + 100 + m] += jnp.where(low_x | jnp.logical_not(has_x[1]), 0.0, pltpu.roll(high, 1, 0))
+            if other is not None:
+                low = jnp.where(low_x & has_x[-1], pltpu.roll(low, 3, 0), 0.0)
+                high = jnp.where(low_x | jnp.logical_not(has_x[1]), 0.0, high)
+                force[i * 125 + other] += low
+                force[i * 125 + 100 + other] += high
+
     def add_x(m, carry):
-        for i in range(3):
-            low = jnp.where(low_x & has_x[-1], pltpu.roll(got_x[0][i * 25 + m], 3, 0), 0.0)
-            high = jnp.where(low_x | jnp.logical_not(has_x[1]), 0.0, pltpu.roll(got_x[1][i * 25 + m], 1, 0))
-            force[i * 125 + m] += low
-            force[i * 125 + 100 + m] += high
-        return carry
-
-    lax.fori_loop(0, 25, add_x, 0)
+        one(m, m + 13)
+        return carry
+
+    lax.fori_loop(0, 12, add_x, 0)
+    one(12, None)
     first, final = lane < 15, (lane >= 60) & (lane < 75)
     columns = []
     for side, end in ((-1, 1), (1, 0)):
@@ -494,12 +578,26 @@
                 for c in range(5):
                     n = a * 25 + b * 5 + c
                     f = force[i * 125 + n]
-                    if c == 0:
+                    if c == 0 and load is not None:
                         f = f + load[i * 25 + a * 5 + b]
                     w = np.float32(1.0 / (gll_weights[a] * gll_weights[b] * gll_weights[c]))
                     step = (inverse[kind(a) * 9 + kind(b) * 3 + kind(c)] * w) * f
                     at = i * 125 + n
                     out_ref[at] = (now_ref[at] + now_ref[at] - before_ref[at]) + step
+        return carry
+
+    lax.fori_loop(0, 3, component, 0)
+
+
+def kick_solid(load, inverse, out_ref, kick):
+    def component(i, carry):
+        for a in range(5):
+            for b in range(5):
+                n = i * 25 + a * 5 + b
+                w = np.float32(1.0 / (gll_weights[a] * gll_weights[b] * gll_weights[0]))
+                step = (inverse[kind(a) * 9 + kind(b) * 3] * w) * load[n]
+                kick[n] = step
+                out_ref[i * 125 + a * 25 + b * 5] += step
         return carry
 
     lax.fori_loop(0, 3, component, 0)
@@ -675,8 +773,8 @@
     (u_zero, before, u_one, u_two, force, stress, load, inverse) = refs[40:48]
     (density, lame, shear, around) = refs[48:52]
     (face_x, face_y, got_face_x, got_face_y) = refs[52:56]
-    (own, beyond, sides, got_beyond, got_sides) = refs[56:61]
-    local_sem, sent, come = refs[61:]
+    (own, beyond, sides, got_beyond, got_sides, kick) = refs[56:62]
+    local_sem, sent, come = refs[62:]
     rows, cols = drag_own.shape
     at_x, at_y = lax.axis_index("gx"), lax.axis_index("gy")
     size_x, size_y = lax.axis_size("gx"), lax.axis_size("gy")
@@ -726,8 +824,8 @@
     first += [send(density_in, around.at[AROUND.index(opposite(move))], move) for move in AROUND]
 
     def send_faces(step):
-        copies = [send(face_x.at[step], got_face_x.at[step, 1], (-1, 0))]
-        copies += [send(face_x.at[step], got_face_x.at[step, 0], (1, 0))]
+        copies = [send(face_x.at[step, 0], got_face_x.at[step, 1], (-1, 0))]
+        copies += [send(face_x.at[step, 1], got_face_x.at[step, 0], (1, 0))]
         for move in ASIDE:
             copies.append(send(face_y.at[step], got_face_y.at[step, ASIDE.index(opposite(move))], move))
         return copies
@@ -740,14 +838,20 @@
 
     for copy in reads[:3]:
         copy.wait()
-    internal_local(u_zero, lame, shear, stress, force)
+    internal_open(u_zero, lame, shear, stress, force)
+    internal_close(stress, force)
     pack_faces(force, face_x.at[0], face_y.at[0])
     faces = send_faces(0)
-    for copy in reads[3:] + first:
+    for copy in reads[3:]:
         copy.wait()
-    inverse_masses(density, {move: around.at[n] for n, move in enumerate(AROUND)}, inverse)
+
+    def arrive():
+        for copy in first:
+            copy.wait()
+        inverse_masses(density, {move: around.at[n] for n, move in enumerate(AROUND)}, inverse)
+
     surface(
-        drag_own, wet_own, elem_own, node_own, (halos[0:5], halos[5:10], halos[10:15]),
+        drag_own, wet_own, elem_own, node_own, arrive, (halos[0:5], halos[5:10], halos[10:15]),
         own, beyond, sides, ext, drag, buoy, scale, tract, row_slot, col_slot, table, store_fields,
     )
     loads = [send(beyond, got_beyond.at[1], (-1, 0)), send(beyond, got_beyond.at[0], (1, 0))]
@@ -756,6 +860,8 @@
     for copy in faces:
         copy.wait()
     add_faces(force, *faces_of(0))
+    advance_solid(force, None, inverse, u_zero, before, u_one)
+    internal_open(u_one, lame, shear, stress, force)
     for copy in loads:
         copy.wait()
     load_total(
@@ -764,9 +870,10 @@
         {move: got_sides.at[n] for n, move in enumerate(ASIDE)},
         load,
     )
-    advance_solid(force, load, inverse, u_zero, before, u_one)
+    kick_solid(load, inverse, u_one, kick)
     store_last.start()
-    internal_local(u_one, lame, shear, stress, force)
+    internal_kick(kick, lame, shear, force)
+    internal_close(stress, force)
     pack_faces(force, face_x.at[1], face_y.at[1])
     faces = send_faces(1)
     for copy in faces:
@@ -780,11 +887,22 @@
 
 
 def store_body(*refs):
-    sems = refs[6]
-    copies = [pltpu.make_async_copy(refs[n], refs[3 + n], sems.at[n]) for n in range(3)]
-    for copy in copies:
+    taken, given = refs[9:]
+    reads, writes = [], []
+    for n in range(3):
+        source, target, held = refs[n], refs[3 + n], refs[6 + n]
+        step = source.shape[0] // 3
+        for m in range(3):
+            part = pl.ds(m * step, step)
+            at = 3 * n + m
+            reads.append(pltpu.make_async_copy(source.at[part], held.at[part], taken.at[at]))
+            writes.append(pltpu.make_async_copy(held.at[part], target.at[part], given.at[at]))
+    for copy in reads:
         copy.start()
-    for copy in copies:
+    for read, write in zip(reads, writes):
+        read.wait()
+        write.start()
+    for copy in writes:
         copy.wait()
 
 
@@ -822,8 +940,8 @@
         floats(rows, cols), integers(rows, cols), integers(rows, cols), integers(rows, cols),
         *[floats(*nodes)] * 6, floats(75, 4, 128), floats(27, 4, 128),
         floats(4, 128), floats(4, 128), floats(4, 128), floats(8, 4, 128),
-        floats(2, 75, 4, 128), floats(2, 2, 4, 128), floats(2, 2, 75, 4, 128), floats(2, 6, 2, 4, 128),
-        floats(3, 56, 128), floats(3, 56, 128), floats(8, 128), floats(2, 3, 56, 128), floats(6, 8, 128),
+        floats(2, 2, 39, 4, 128), floats(2, 2, 4, 128), floats(2, 2, 39, 4, 128), floats(2, 6, 2, 4, 128),
+        floats(3, 56, 128), floats(3, 56, 128), floats(8, 128), floats(2, 3, 56, 128), floats(6, 8, 128), floats(75, 4, 128),
         pltpu.SemaphoreType.DMA((13,)), pltpu.SemaphoreType.DMA((56,)), pltpu.SemaphoreType.DMA((56,)),
     ]
     anywhere = pl.BlockSpec(memory_space=pl.ANY)
@@ -846,7 +964,11 @@
         out_shape=tuple(shape(*x.shape) for x in results),
         in_specs=[anywhere] * 3,
         out_specs=(anywhere,) * 3,
-        scratch_shapes=[pltpu.SemaphoreType.DMA((3,))],
+        scratch_shapes=[
+            *[pltpu.VMEM(x.shape, jnp.float32) for x in results],
+            pltpu.SemaphoreType.DMA((9,)), pltpu.SemaphoreType.DMA((9,)),
+        ],
+        compiler_params=pltpu.CompilerParams(vmem_limit_bytes=60 * 2**20),
     )(*results)
     return (fields, u_two.reshape(grid), u_one.reshape(grid))
 

time: 150 us -> 55.1 us (0.37)
  Pallas kernels: 149 us -> 54.4 us
    pallas_call x1, Pallas kernels: 95.3 us -> 2.84 us  [per_device(): pl.pallas_call(store_body, out_shape=tuple((shape(*x.shape) for x in resu...]
    pallas_call x1, Pallas kernels: 53.8 us -> 51.5 us  [per_device(): pl.pallas_call(whole_body, out_shape=(shape(6, rows, cols), shape(*nodes)...]
where the time goes in v5:
time: 55.1 us; the launch traced here: 55 us
  Pallas kernels  54.4 us (99%)
  between operations  0.64 us (1%)
    pallas_call x1, Pallas kernels, per_device(): pl.pallas_call(whole_body, out_shape=(shape(6, rows, cols), shape(*nodes)...  51.5 us
    pallas_call x1, Pallas kernels, per_device(): pl.pallas_call(store_body, out_shape=tuple((shape(*x.shape) for x in resu...  2.84 us

profile of v5, /device:TPU:1, one launch (start us, length us, event | category | flops | bytes accessed | tf_op | source)
XLA Modules:
  0.0 55.0 jit_solution(5996937121548346831)
XLA Ops:
  0.6 51.5 %shard_map.121 = (f32[6,32,2048]{2,1,0:T(8,128)}, f32[375,4,128]{2,1,0:T(4,128)}, f32[375,4,128]{2,1,0:T(4,128)}) custom-call(f32[6,32,2048]{2,1,0:T(8,128)} %refs_0_.1, f32[32,2048]{1,0:T(8,128)} %refs_1_.1, s32[32,2048]{1,0:T(8,128)} %refs_2_.1, s32[32,2048]{1,0:T(8,128)} %refs_3_.1, s32[32,2048]{1,0:T(8,128)} %refs_4_.1, f32[375,4,128]{2,1,0:T(4,128)} %bitcast.7, ...), custom_call_target="tpu_custom_call" | custom-call | tf_op jit(solution)/shard_map/pallas_call | solution.py:948
  52.2 2.8 %shard_map.122 = (f32[6,32,2048]{2,1,0:T(8,128)}, f32[375,4,128]{2,1,0:T(4,128)}, f32[375,4,128]{2,1,0:T(4,128)}) custom-call(f32[6,32,2048]{2,1,0:T(8,128)} %get-tuple-element.9.refs_0_, f32[375,4,128]{2,1,0:T(4,128)} %get-tuple-element.10.refs_1_, f32[375,4,128]{2,1,0:T(4,128)} %get-tuple-element.11.refs_2_), custom_call_target="tpu_custom_call" | custom-call | tf_op jit(solution)/shard_map/pallas_call | solution.py:962

commit v6 on v5

--- a/solution.py
+++ b/solution.py
@@ -63,7 +63,7 @@
         e = elem_ref[:, at]
         n = node_ref[:, at]
         surface_cols = 128 * (last_y + 1)
-        er = e // surface_cols
+        er = lax.shift_right_logical(e, surface_cols.bit_length() - 1) if surface_cols & (surface_cols - 1) == 0 else e // surface_cols
         lx = er - 2 * at_x + 1
         ly = (e - er * surface_cols) - 128 * at_y + 1
         inside = (ly >= 1) & (ly <= 128)
@@ -499,28 +499,22 @@
     return has, has_y
 
 
-def add_faces(force, got_x, got_y):
+def add_faces(target, got_x, got_y, factor):
     has_x, has_y = open_edges()
     lane, row = lane_row()
     low_x = row % 2 == 0
-
-    def one(m, other):
+    from_low = low_x & has_x[-1]
+    from_high = jnp.logical_not(low_x) & has_x[1]
+    for m in range(13):
         for i in range(3):
             low, high = got_x[0][i * 13 + m], got_x[1][i * 13 + m]
-            force[i * 125 + m] += jnp.where(low_x & has_x[-1], low, 0.0)
-            force[i * 125 + 100 + m] += jnp.where(low_x | jnp.logical_not(has_x[1]), 0.0, pltpu.roll(high, 1, 0))
-            if other is not None:
-                low = jnp.where(low_x & has_x[-1], pltpu.roll(low, 3, 0), 0.0)
-                high = jnp.where(low_x | jnp.logical_not(has_x[1]), 0.0, high)
-                force[i * 125 + other] += low
-                force[i * 125 + 100 + other] += high
-
-    def add_x(m, carry):
-        one(m, m + 13)
-        return carry
-
-    lax.fori_loop(0, 12, add_x, 0)
-    one(12, None)
+            pairs = [(m, low, pltpu.roll(high, 1, 0))]
+            if m < 12:
+                pairs.append((m + 13, pltpu.roll(low, 3, 0), high))
+            for at, near, far in pairs:
+                b, c = at // 5, at % 5
+                target[i * 125 + at] += factor(0, b, c, jnp.where(from_low, near, 0.0))
+                target[i * 125 + 100 + at] += factor(4, b, c, jnp.where(from_high, far, 0.0))
     first, final = lane < 15, (lane >= 60) & (lane < 75)
     columns = []
     for side, end in ((-1, 1), (1, 0)):
@@ -535,8 +529,10 @@
             for c in range(5):
                 q = a * 15 + i * 5 + c
                 n = i * 125 + a * 25 + c
-                force[n] += jnp.where(lane == 0, pltpu.roll(columns[0], (128 - q) % 128, 1), 0.0)
-                force[n + 20] += jnp.where(lane == 127, pltpu.roll(columns[1], 127 - q, 1), 0.0)
+                near = jnp.where(lane == 0, pltpu.roll(columns[0], (128 - q) % 128, 1), 0.0)
+                far = jnp.where(lane == 127, pltpu.roll(columns[1], 127 - q, 1), 0.0)
+                target[n] += factor(a, 0, c, near)
+                target[n + 20] += factor(a, 4, c, far)
 
 
 def inverse_masses(density_ref, around, inverse):
@@ -571,6 +567,11 @@
     return 0 if node == 0 else 2 if node == 4 else 1
 
 
+def moved_by(inverse, a, b, c, f):
+    w = np.float32(1.0 / (gll_weights[a] * gll_weights[b] * gll_weights[c]))
+    return (inverse[kind(a) * 9 + kind(b) * 3 + kind(c)] * w) * f
+
+
 def advance_solid(force, load, inverse, now_ref, before_ref, out_ref):
     def component(i, carry):
         for a in range(5):
@@ -580,8 +581,7 @@
                     f = force[i * 125 + n]
                     if c == 0 and load is not None:
                         f = f + load[i * 25 + a * 5 + b]
-                    w = np.float32(1.0 / (gll_weights[a] * gll_weights[b] * gll_weights[c]))
-                    step = (inverse[kind(a) * 9 + kind(b) * 3 + kind(c)] * w) * f
+                    step = moved_by(inverse, a, b, c, f)
                     at = i * 125 + n
                     out_ref[at] = (now_ref[at] + now_ref[at] - before_ref[at]) + step
         return carry
@@ -594,8 +594,7 @@
         for a in range(5):
             for b in range(5):
                 n = i * 25 + a * 5 + b
-                w = np.float32(1.0 / (gll_weights[a] * gll_weights[b] * gll_weights[0]))
-                step = (inverse[kind(a) * 9 + kind(b) * 3] * w) * load[n]
+                step = moved_by(inverse, a, b, 0, load[n])
                 kick[n] = step
                 out_ref[i * 125 + a * 25 + b * 5] += step
         return carry
@@ -785,9 +784,17 @@
     def opposite(move):
         return -move[0], -move[1]
 
+    def there(move):
+        x, y = at_x + move[0], at_y + move[1]
+        return (x >= 0) & (x < size_x) & (y >= 0) & (y < size_y)
+
     barrier = pltpu.get_barrier_semaphore()
     for move in AROUND:
-        pl.semaphore_signal(barrier, inc=1, device_id=device(move), device_id_type=pl.DeviceIdType.MESH)
+
+        @pl.when(there(move))
+        def _(move=move):
+            pl.semaphore_signal(barrier, inc=1, device_id=device(move), device_id_type=pl.DeviceIdType.MESH)
+
     reads = [
         pltpu.make_async_copy(source, target, local_sem.at[n])
         for n, (source, target) in enumerate(
@@ -803,7 +810,9 @@
     store_fields = pltpu.make_async_copy(ext.at[0, :, 0:rows, 0:cols], fields_out, local_sem.at[10])
     store_last = pltpu.make_async_copy(u_one, last_out, local_sem.at[11])
     store_next = pltpu.make_async_copy(u_two, next_out, local_sem.at[12])
-    pl.semaphore_wait(barrier, len(AROUND))
+    beside_x = 3 - jnp.where(at_x == 0, 1, 0) - jnp.where(at_x == size_x - 1, 1, 0)
+    beside_y = 3 - jnp.where(at_y == 0, 1, 0) - jnp.where(at_y == size_y - 1, 1, 0)
+    pl.semaphore_wait(barrier, beside_x * beside_y - 1)
     number = [0]
 
     def send(source, target, move):
@@ -813,8 +822,23 @@
             src_ref=source, dst_ref=target, send_sem=sent.at[n], recv_sem=come.at[n],
             device_id=device(move), device_id_type=pl.DeviceIdType.MESH,
         )
-        copy.start()
-        return copy
+        pl.when(there(move))(copy.start)
+        return copy, move
+
+    def finish(messages):
+        for move in AROUND:
+            mine = [copy for copy, way in messages if way == move]
+            if mine:
+
+                @pl.when(there(opposite(move)))
+                def _(mine=mine):
+                    for copy in mine:
+                        copy.wait_recv()
+
+                @pl.when(there(move))
+                def _(mine=mine):
+                    for copy in mine:
+                        copy.wait_send()
 
     operands = (flow_in, drag_in, wet_in)
     first = [
@@ -846,8 +870,7 @@
         copy.wait()
 
     def arrive():
-        for copy in first:
-            copy.wait()
+        finish(first)
         inverse_masses(density, {move: around.at[n] for n, move in enumerate(AROUND)}, inverse)
 
     surface(
@@ -857,13 +880,11 @@
     loads = [send(beyond, got_beyond.at[1], (-1, 0)), send(beyond, got_beyond.at[0], (1, 0))]
     for move in ASIDE:
         loads.append(send(sides, got_sides.at[ASIDE.index(opposite(move))], move))
-    for copy in faces:
-        copy.wait()
-    add_faces(force, *faces_of(0))
+    finish(faces)
+    add_faces(force, *faces_of(0), lambda a, b, c, f: f)
     advance_solid(force, None, inverse, u_zero, before, u_one)
     internal_open(u_one, lame, shear, stress, force)
-    for copy in loads:
-        copy.wait()
+    finish(loads)
     load_total(
         own,
         [got_beyond.at[n] for n in range(2)],
@@ -876,10 +897,9 @@
     internal_close(stress, force)
     pack_faces(force, face_x.at[1], face_y.at[1])
     faces = send_faces(1)
-    for copy in faces:
-        copy.wait()
-    add_faces(force, *faces_of(1))
     advance_solid(force, load, inverse, u_one, u_zero, u_two)
+    finish(faces)
+    add_faces(u_two, *faces_of(1), lambda a, b, c, f: moved_by(inverse, a, b, c, f))
     store_next.start()
     store_fields.wait()
     store_last.wait()

time: 55.1 us -> 49.1 us (0.89)
  the two profiles are of different devices: /device:TPU:1 before, /device:TPU:25 now
where the time goes in v6:
time: 49.1 us; the launch traced here: 48.9 us
  Pallas kernels  48.3 us (98%)
  between operations  0.64 us (1%)
    pallas_call x1, Pallas kernels, per_device(): pl.pallas_call(whole_body, out_shape=(shape(6, rows, cols), shape(*nodes)...  45.4 us
    pallas_call x1, Pallas kernels, per_device(): pl.pallas_call(store_body, out_shape=tuple((shape(*x.shape) for x in resu...  2.84 us

profile of v6, /device:TPU:25, one launch (start us, length us, event | category | flops | bytes accessed | tf_op | source)
XLA Modules:
  0.0 48.9 jit_solution(8149621300523244911)
XLA Ops:
  0.6 45.4 %shard_map.121 = (f32[6,32,2048]{2,1,0:T(8,128)}, f32[375,4,128]{2,1,0:T(4,128)}, f32[375,4,128]{2,1,0:T(4,128)}) custom-call(f32[6,32,2048]{2,1,0:T(8,128)} %refs_0_.1, f32[32,2048]{1,0:T(8,128)} %refs_1_.1, s32[32,2048]{1,0:T(8,128)} %refs_2_.1, s32[32,2048]{1,0:T(8,128)} %refs_3_.1, s32[32,2048]{1,0:T(8,128)} %refs_4_.1, f32[375,4,128]{2,1,0:T(4,128)} %bitcast.7, ...), custom_call_target="tpu_custom_call" | custom-call | tf_op jit(solution)/shard_map/pallas_call | solution.py:968
  46.1 2.8 %shard_map.122 = (f32[6,32,2048]{2,1,0:T(8,128)}, f32[375,4,128]{2,1,0:T(4,128)}, f32[375,4,128]{2,1,0:T(4,128)}) custom-call(f32[6,32,2048]{2,1,0:T(8,128)} %get-tuple-element.9.refs_0_, f32[375,4,128]{2,1,0:T(4,128)} %get-tuple-element.10.refs_1_, f32[375,4,128]{2,1,0:T(4,128)} %get-tuple-element.11.refs_2_), custom_call_target="tpu_custom_call" | custom-call | tf_op jit(solution)/shard_map/pallas_call | solution.py:982

commit v7 on v6

--- a/solution.py
+++ b/solution.py
@@ -80,7 +80,7 @@
         col_slot[:, at] = b.astype(jnp.float32)
         return carry
 
-    lax.fori_loop(0, cols // 128, own_cells, 0)
+    lax.fori_loop(0, cols // 128, own_cells, 0, unroll=True)
     arrive()
 
     sub = lax.broadcasted_iota(jnp.int32, (8, 128), 0)
@@ -125,7 +125,7 @@
         scale[foot, at] = row_scale
         return carry
 
-    lax.fori_loop(0, cols // 128, halo_rows, 0)
+    lax.fori_loop(0, cols // 128, halo_rows, 0, unroll=True)
     for k in range(8):
         for r in range(0, rows, 8):
             at = (slice(r, r + 8), slice(None))
@@ -146,8 +146,10 @@
     def press(f0, f1, b):
         return b * (f0 + f1), upper_gravity * density_ratio * f0 + upper_gravity * f1
 
-    def step(now, carry):
+    def step(now, carry, final=False):
         later = 1 - now
+        height = rows if final else tall
+        cells = slice(0, height)
 
         def tile_step(t, carry):
             at = pl.ds(pl.multiple_of(t * 128, 128), 128)
@@ -166,8 +168,7 @@
             for ahead in (True, False):
                 by = tall - 1 if ahead else 1
                 def rolled(x):
-                    return pltpu.roll(x, by, 0)
-                sg = -1.0 if ahead else 1.0
+                    return pltpu.roll(x, by, 0)[cells]
                 def mix(x, y):
                     return x - y if ahead else x + y
                 add(0, rolled(mix(f[0], f[2])))
@@ -176,12 +177,14 @@
                 add(3, rolled(f[3]))
                 add(4, rolled(mix(f[4], two)))
                 add(5, rolled(f[5]))
+            f = [x[cells] for x in f]
+            b = b[cells]
             for ahead in (True, False):
                 by = 127 if ahead else 1
-                edge = first_lane if ahead else last_lane
+                edge = (first_lane if ahead else last_lane)[cells]
                 other = at_hi if ahead else at_lo
-                g = [jnp.where(edge, ext[now, k, :, other], f[k]) for k in range(6)]
-                gb = jnp.where(edge, buoy[:, other], b)
+                g = [jnp.where(edge, ext[now, k, cells, other], f[k]) for k in range(6)]
+                gb = jnp.where(edge, buoy[cells, other], b)
                 g_one, g_two = press(g[0], g[1], gb)
                 def rolled(x):
                     return pltpu.roll(x, by, 1)
@@ -194,31 +197,31 @@
                 add(4, rolled(g[4]))
                 add(5, rolled(mix(g[5], g_two)))
             speed = jnp.sqrt(f[2] * f[2] + f[3] * f[3] + speed_floor)
-            rub = 2.0 * drag[:, at] * speed
-            k = scale[:, at]
-            ext[later, 0, :, at] = k * (f[0] + sums[0])
-            ext[later, 1, :, at] = k * (f[1] + sums[1])
-            ext[later, 2, :, at] = k * (sums[2] + f[4] - rub * f[2])
-            ext[later, 3, :, at] = k * (sums[3] + f[5] - rub * f[3])
-            ext[later, 4, :, at] = k * (sums[4] + f[2])
-            ext[later, 5, :, at] = k * (sums[5] + f[3])
+            rub = 2.0 * drag[cells, at] * speed
+            k = scale[cells, at]
+            new = (
+                k * (f[0] + sums[0]),
+                k * (f[1] + sums[1]),
+                k * (sums[2] + f[4] - rub * f[2]),
+                k * (sums[3] + f[5] - rub * f[3]),
+                k * (sums[4] + f[2]),
+                k * (sums[5] + f[3]),
+            )
+            for n, value in enumerate(new):
+                ext[later, n, cells, at] = value
+            if final:
+                speed = jnp.sqrt(new[2] * new[2] + new[3] * new[3] + speed_floor)
+                rub = load_factor * drag[cells, at] * speed
+                tract[0, :, at] = rub * new[2]
+                tract[1, :, at] = rub * new[3]
+                tract[2, :, at] = -load_factor * (b * (new[0] + new[1]))
             return carry
 
-        return lax.fori_loop(0, tiles, tile_step, carry, unroll=True)
-
-    lax.fori_loop(0, FLOW_STEPS // 2, lambda _, carry: step(1, step(0, carry)), 0)
+        return lax.fori_loop(0, tiles - 1 if final else tiles, tile_step, carry, unroll=True)
+
+    lax.fori_loop(0, FLOW_STEPS // 2 - 1, lambda _, carry: step(1, step(0, carry)), 0)
+    step(1, step(0, 0), final=True)
     store_fields.start()
-
-    def pull(t, carry):
-        at = pl.ds(pl.multiple_of(t * 128, 128), 128)
-        f = [ext[0, k, 0:rows, at] for k in range(4)]
-        rub = load_factor * drag[0:rows, at] * jnp.sqrt(f[2] * f[2] + f[3] * f[3] + speed_floor)
-        tract[0, :, at] = rub * f[2]
-        tract[1, :, at] = rub * f[3]
-        tract[2, :, at] = -load_factor * (buoy[0:rows, at] * (f[0] + f[1]))
-        return carry
-
-    lax.fori_loop(0, cols // 128, pull, 0)
 
     table_ref[...] = jnp.zeros_like(table_ref)
     narrow = jnp.bfloat16
@@ -309,7 +312,7 @@
                 stress[i * 125 + a * 25 + m] = lines[a]
         return carry
 
-    lax.fori_loop(0, 25, slope_x, 0)
+    lax.fori_loop(0, 25, slope_x, 0, unroll=True)
 
     def plane(a, carry):
         weight = jnp.where(
@@ -441,7 +444,7 @@
                 force[i * 125 + a * 25 + m] = value
         return carry
 
-    lax.fori_loop(0, 25, close_x, 0)
+    lax.fori_loop(0, 25, close_x, 0, unroll=True)
 
     def close_yz(ia, carry):
         base = ia * 25
@@ -460,7 +463,7 @@
                     force[base + b * 5 + c] = f[b][c]
         return carry
 
-    lax.fori_loop(0, 15, close_yz, 0)
+    lax.fori_loop(0, 15, close_yz, 0, unroll=True)
 
 
 def pack_faces(force, face_x, face_y):
@@ -478,7 +481,7 @@
         both(m, m + 13)
         return carry
 
-    lax.fori_loop(0, 12, pack_x, 0)
+    lax.fori_loop(0, 12, pack_x, 0, unroll=True)
     both(12, 12)
     ends = [jnp.zeros((4, 128), jnp.float32)] * 2
     for a in range(5):
@@ -822,23 +825,26 @@
             src_ref=source, dst_ref=target, send_sem=sent.at[n], recv_sem=come.at[n],
             device_id=device(move), device_id_type=pl.DeviceIdType.MESH,
         )
-        pl.when(there(move))(copy.start)
         return copy, move
 
-    def finish(messages):
+    def each(messages, toward, act):
         for move in AROUND:
             mine = [copy for copy, way in messages if way == move]
             if mine:
 
-                @pl.when(there(opposite(move)))
+                @pl.when(there(move if toward else opposite(move)))
                 def _(mine=mine):
                     for copy in mine:
-                        copy.wait_recv()
-
-                @pl.when(there(move))
-                def _(mine=mine):
-                    for copy in mine:
-                        copy.wait_send()
+                        act(copy)
+
+    def launch(messages):
+        each(messages, True, lambda copy: copy.start())
+
+    def finish(messages):
+        each(messages, False, lambda copy: copy.wait_recv())
+
+    def drain(messages):
+        each(messages, True, lambda copy: copy.wait_send())
 
     operands = (flow_in, drag_in, wet_in)
     first = [
@@ -846,12 +852,14 @@
         for source, source_at, target, target_at, move in halo_plan(rows, cols)
     ]
     first += [send(density_in, around.at[AROUND.index(opposite(move))], move) for move in AROUND]
+    launch(first)
 
     def send_faces(step):
         copies = [send(face_x.at[step, 0], got_face_x.at[step, 1], (-1, 0))]
         copies += [send(face_x.at[step, 1], got_face_x.at[step, 0], (1, 0))]
         for move in ASIDE:
             copies.append(send(face_y.at[step], got_face_y.at[step, ASIDE.index(opposite(move))], move))
+        launch(copies)
         return copies
 
     def faces_of(step):
@@ -880,6 +888,7 @@
     loads = [send(beyond, got_beyond.at[1], (-1, 0)), send(beyond, got_beyond.at[0], (1, 0))]
     for move in ASIDE:
         loads.append(send(sides, got_sides.at[ASIDE.index(opposite(move))], move))
+    launch(loads)
     finish(faces)
     add_faces(force, *faces_of(0), lambda a, b, c, f: f)
     advance_solid(force, None, inverse, u_zero, before, u_one)
@@ -896,11 +905,12 @@
     internal_kick(kick, lame, shear, force)
     internal_close(stress, force)
     pack_faces(force, face_x.at[1], face_y.at[1])
-    faces = send_faces(1)
+    last_faces = send_faces(1)
     advance_solid(force, load, inverse, u_one, u_zero, u_two)
-    finish(faces)
+    finish(last_faces)
     add_faces(u_two, *faces_of(1), lambda a, b, c, f: moved_by(inverse, a, b, c, f))
     store_next.start()
+    drain(first + faces + loads + last_faces)
     store_fields.wait()
     store_last.wait()
     store_next.wait()

time: 49.1 us -> 47 us (0.957)
  the two profiles are of different devices: /device:TPU:25 before, /device:TPU:27 now
where the time goes in v7:
time: 47 us; the launch traced here: 46.9 us
  Pallas kernels  46.1 us (98%)
  between operations  0.8 us (2%)
    pallas_call x1, Pallas kernels, per_device(): pl.pallas_call(whole_body, out_shape=(shape(6, rows, cols), shape(*nodes)...  43.3 us
    pallas_call x1, Pallas kernels, per_device(): pl.pallas_call(store_body, out_shape=tuple((shape(*x.shape) for x in resu...  2.84 us

profile of v7, /device:TPU:27, one launch (start us, length us, event | category | flops | bytes accessed | tf_op | source)
XLA Modules:
  0.0 46.9 jit_solution(12248955060751935833)
XLA Ops:
  0.6 43.3 %shard_map.121 = (f32[6,32,2048]{2,1,0:T(8,128)}, f32[375,4,128]{2,1,0:T(4,128)}, f32[375,4,128]{2,1,0:T(4,128)}) custom-call(f32[6,32,2048]{2,1,0:T(8,128)} %refs_0_.1, f32[32,2048]{1,0:T(8,128)} %refs_1_.1, s32[32,2048]{1,0:T(8,128)} %refs_2_.1, s32[32,2048]{1,0:T(8,128)} %refs_3_.1, s32[32,2048]{1,0:T(8,128)} %refs_4_.1, f32[375,4,128]{2,1,0:T(4,128)} %bitcast.7, ...), custom_call_target="tpu_custom_call" | custom-call | tf_op jit(solution)/shard_map/pallas_call | solution.py:978
  43.9 2.8 %shard_map.122 = (f32[6,32,2048]{2,1,0:T(8,128)}, f32[375,4,128]{2,1,0:T(4,128)}, f32[375,4,128]{2,1,0:T(4,128)}) custom-call(f32[6,32,2048]{2,1,0:T(8,128)} %get-tuple-element.9.refs_0_, f32[375,4,128]{2,1,0:T(4,128)} %get-tuple-element.10.refs_1_, f32[375,4,128]{2,1,0:T(4,128)} %get-tuple-element.11.refs_2_), custom_call_target="tpu_custom_call" | custom-call | tf_op jit(solution)/shard_map/pallas_call | solution.py:992

commit v8 on v7

--- a/solution.py
+++ b/solution.py
@@ -466,23 +466,8 @@
     lax.fori_loop(0, 15, close_yz, 0, unroll=True)
 
 
-def pack_faces(force, face_x, face_y):
+def pack_faces_y(force, face_y):
     lane, row = lane_row()
-    low_x = row % 2 == 0
-
-    def both(m, other):
-        for i in range(3):
-            near, far = force[i * 125 + m], force[i * 125 + 100 + m]
-            near_other, far_other = force[i * 125 + other], force[i * 125 + 100 + other]
-            face_x[0, i * 13 + m] = jnp.where(low_x, near, pltpu.roll(near_other, 1, 0))
-            face_x[1, i * 13 + m] = jnp.where(low_x, pltpu.roll(far, 3, 0), far_other)
-
-    def pack_x(m, carry):
-        both(m, m + 13)
-        return carry
-
-    lax.fori_loop(0, 12, pack_x, 0, unroll=True)
-    both(12, 12)
     ends = [jnp.zeros((4, 128), jnp.float32)] * 2
     for a in range(5):
         for i in range(3):
@@ -495,6 +480,25 @@
     face_y[1] = ends[1]
 
 
+def pack_faces_x(force, face_x):
+    lane, row = lane_row()
+    low_x = row % 2 == 0
+
+    def both(m, other):
+        for i in range(3):
+            near, far = force[i * 125 + m], force[i * 125 + 100 + m]
+            near_other, far_other = force[i * 125 + other], force[i * 125 + 100 + other]
+            face_x[0, i * 13 + m] = jnp.where(low_x, near, pltpu.roll(near_other, 1, 0))
+            face_x[1, i * 13 + m] = jnp.where(low_x, pltpu.roll(far, 3, 0), far_other)
+
+    def pack_x(m, carry):
+        both(m, m + 13)
+        return carry
+
+    lax.fori_loop(0, 12, pack_x, 0, unroll=True)
+    both(12, 12)
+
+
 def open_edges():
     at_x, at_y = lax.axis_index("gx"), lax.axis_index("gy")
     has = {-1: at_x > 0, 1: at_x < lax.axis_size("gx") - 1}
@@ -502,12 +506,13 @@
     return has, has_y
 
 
-def add_faces(target, got_x, got_y, factor):
+def add_faces(target, got_x, got_y, factor, arrive):
     has_x, has_y = open_edges()
     lane, row = lane_row()
     low_x = row % 2 == 0
     from_low = low_x & has_x[-1]
     from_high = jnp.logical_not(low_x) & has_x[1]
+    arrive(AROUND[:2])
     for m in range(13):
         for i in range(3):
             low, high = got_x[0][i * 13 + m], got_x[1][i * 13 + m]
@@ -518,24 +523,31 @@
                 b, c = at // 5, at % 5
                 target[i * 125 + at] += factor(0, b, c, jnp.where(from_low, near, 0.0))
                 target[i * 125 + 100 + at] += factor(4, b, c, jnp.where(from_high, far, 0.0))
+
+    def add_columns(columns, ends):
+        for a in ends:
+            for i in range(3):
+                for c in range(5):
+                    q = a * 15 + i * 5 + c
+                    n = i * 125 + a * 25 + c
+                    near = jnp.where(lane == 0, pltpu.roll(columns[0], (128 - q) % 128, 1), 0.0)
+                    far = jnp.where(lane == 127, pltpu.roll(columns[1], 127 - q, 1), 0.0)
+                    target[n] += factor(a, 0, c, near)
+                    target[n + 20] += factor(a, 4, c, far)
+
+    sides = ((-1, 1), (1, 0))
+    arrive(AROUND[2:4])
+    add_columns([jnp.where(has_y[side], got_y[0, side][end], 0.0) for side, end in sides], range(5))
+    arrive(AROUND[4:])
     first, final = lane < 15, (lane >= 60) & (lane < 75)
     columns = []
-    for side, end in ((-1, 1), (1, 0)):
-        straight = got_y[0, side][end]
+    for side, end in sides:
         low = pltpu.roll(pltpu.roll(got_y[-1, side][end], 68, 1), 3, 0)
         high = pltpu.roll(pltpu.roll(got_y[1, side][end], 60, 1), 1, 0)
-        total = straight + jnp.where(first & low_x & has_x[-1], low, 0.0)
+        total = jnp.where(first & low_x & has_x[-1], low, 0.0)
         total = total + jnp.where(final & jnp.logical_not(low_x) & has_x[1], high, 0.0)
         columns.append(jnp.where(has_y[side], total, 0.0))
-    for a in range(5):
-        for i in range(3):
-            for c in range(5):
-                q = a * 15 + i * 5 + c
-                n = i * 125 + a * 25 + c
-                near = jnp.where(lane == 0, pltpu.roll(columns[0], (128 - q) % 128, 1), 0.0)
-                far = jnp.where(lane == 127, pltpu.roll(columns[1], 127 - q, 1), 0.0)
-                target[n] += factor(a, 0, c, near)
-                target[n + 20] += factor(a, 4, c, far)
+    add_columns(columns, (0, 4))
 
 
 def inverse_masses(density_ref, around, inverse):
@@ -840,8 +852,9 @@
     def launch(messages):
         each(messages, True, lambda copy: copy.start())
 
-    def finish(messages):
-        each(messages, False, lambda copy: copy.wait_recv())
+    def finish(messages, moves=AROUND):
+        some = [message for message in messages if message[1] in moves]
+        each(some, False, lambda copy: copy.wait_recv())
 
     def drain(messages):
         each(messages, True, lambda copy: copy.wait_send())
@@ -855,12 +868,19 @@
     launch(first)
 
     def send_faces(step):
-        copies = [send(face_x.at[step, 0], got_face_x.at[step, 1], (-1, 0))]
-        copies += [send(face_x.at[step, 1], got_face_x.at[step, 0], (1, 0))]
-        for move in ASIDE:
-            copies.append(send(face_y.at[step], got_face_y.at[step, ASIDE.index(opposite(move))], move))
+        pack_faces_y(force, face_y.at[step])
+        far = [
+            (face_y.at[step], got_face_y.at[step, ASIDE.index(opposite(move))], move) for move in ASIDE
+        ]
+        copies = [send(*message) for message in far]
         launch(copies)
-        return copies
+        pack_faces_x(force, face_x.at[step])
+        near = [
+            send(face_x.at[step, 0], got_face_x.at[step, 1], (-1, 0)),
+            send(face_x.at[step, 1], got_face_x.at[step, 0], (1, 0)),
+        ]
+        launch(near)
+        return near + copies
 
     def faces_of(step):
         return (
@@ -872,7 +892,6 @@
         copy.wait()
     internal_open(u_zero, lame, shear, stress, force)
     internal_close(stress, force)
-    pack_faces(force, face_x.at[0], face_y.at[0])
     faces = send_faces(0)
     for copy in reads[3:]:
         copy.wait()
@@ -889,8 +908,7 @@
     for move in ASIDE:
         loads.append(send(sides, got_sides.at[ASIDE.index(opposite(move))], move))
     launch(loads)
-    finish(faces)
-    add_faces(force, *faces_of(0), lambda a, b, c, f: f)
+    add_faces(force, *faces_of(0), lambda a, b, c, f: f, lambda moves: finish(faces, [opposite(move) for move in moves]))
     advance_solid(force, None, inverse, u_zero, before, u_one)
     internal_open(u_one, lame, shear, stress, force)
     finish(loads)
@@ -904,11 +922,12 @@
     store_last.start()
     internal_kick(kick, lame, shear, force)
     internal_close(stress, force)
-    pack_faces(force, face_x.at[1], face_y.at[1])
     last_faces = send_faces(1)
     advance_solid(force, load, inverse, u_one, u_zero, u_two)
-    finish(last_faces)
-    add_faces(u_two, *faces_of(1), lambda a, b, c, f: moved_by(inverse, a, b, c, f))
+    add_faces(
+        u_two, *faces_of(1), lambda a, b, c, f: moved_by(inverse, a, b, c, f),
+        lambda moves: finish(last_faces, [opposite(move) for move in moves]),
+    )
     store_next.start()
     drain(first + faces + loads + last_faces)
     store_fields.wait()

time: 47 us -> 47.1 us (level)
  the two profiles are of different devices: /device:TPU:27 before, /device:TPU:29 now
where the time goes in v8:
time: 47.1 us; the launch traced here: 46.9 us
  Pallas kernels  46.1 us (98%)
  between operations  0.8 us (2%)
    pallas_call x1, Pallas kernels, per_device(): pl.pallas_call(whole_body, out_shape=(shape(6, rows, cols), shape(*nodes)...  43.3 us
    pallas_call x1, Pallas kernels, per_device(): pl.pallas_call(store_body, out_shape=tuple((shape(*x.shape) for x in resu...  2.84 us

profile of v8, /device:TPU:29, one launch (start us, length us, event | category | flops | bytes accessed | tf_op | source)
XLA Modules:
  0.0 46.9 jit_solution(9620134463404414222)
XLA Ops:
  0.6 43.3 %shard_map.121 = (f32[6,32,2048]{2,1,0:T(8,128)}, f32[375,4,128]{2,1,0:T(4,128)}, f32[375,4,128]{2,1,0:T(4,128)}) custom-call(f32[6,32,2048]{2,1,0:T(8,128)} %refs_0_.1, f32[32,2048]{1,0:T(8,128)} %refs_1_.1, s32[32,2048]{1,0:T(8,128)} %refs_2_.1, s32[32,2048]{1,0:T(8,128)} %refs_3_.1, s32[32,2048]{1,0:T(8,128)} %refs_4_.1, f32[375,4,128]{2,1,0:T(4,128)} %bitcast.7, ...), custom_call_target="tpu_custom_call" | custom-call | tf_op jit(solution)/shard_map/pallas_call | solution.py:997
  43.9 2.8 %shard_map.122 = (f32[6,32,2048]{2,1,0:T(8,128)}, f32[375,4,128]{2,1,0:T(4,128)}, f32[375,4,128]{2,1,0:T(4,128)}) custom-call(f32[6,32,2048]{2,1,0:T(8,128)} %get-tuple-element.9.refs_0_, f32[375,4,128]{2,1,0:T(4,128)} %get-tuple-element.10.refs_1_, f32[375,4,128]{2,1,0:T(4,128)} %get-tuple-element.11.refs_2_), custom_call_target="tpu_custom_call" | custom-call | tf_op jit(solution)/shard_map/pallas_call | solution.py:1011
